TPU v7x, 32 devices: a whole 2x2x4 slice. The times are simulated.
32 devices in a mesh: groups: 2 (over x), blk: 16 (over z, y, core).
Axes of the slice: x: 2, y: 2, z: 4, core: 2. Of those that a mesh axis runs over, the one named last changes fastest.
Arguments:
- features: bfloat16 [8192, 512], P(('groups', 'blk')), parts along dimension 0, may hold values from -6 to 6
- tiles: bfloat16 [1536, 128, 128], P(('groups', 'blk')), parts along dimension 0, may hold values from -0.1875 to 0.1875
- block_rows: int32 [1536], P(('groups', 'blk')), parts along dimension 0, may hold values from 0 to 1, as said below
- block_cols: int32 [1536], P(('groups', 'blk')), parts along dimension 0, may hold values from 0 to 31
- block_count: int32 [32], P(('groups', 'blk')), parts along dimension 0, may hold values from 8 to 48, as said below
- ln_gain: float32 [512], replicated, may hold values from 0.1 to 1.9
- w_msg: bfloat16 [512, 512], replicated, may hold values from -0.25 to 0.25
- w_query: bfloat16 [512, 512], replicated, may hold values from -0.25 to 0.25
- w_key: bfloat16 [512, 512], replicated, may hold values from -0.25 to 0.25
- w_value: bfloat16 [512, 512], replicated, may hold values from -0.25 to 0.25
- w_gate: bfloat16 [512, 512], replicated, may hold values from -0.25 to 0.25
- w_out: bfloat16 [512, 512], replicated, may hold values from -0.25 to 0.25
- omega: float32 [64, 128], replicated, may hold values from -4 to 4
- ln2_gain: float32 [512], replicated, may hold values from 0.1 to 1.9
- w_up: bfloat16 [512, 1024], replicated, may hold values from -0.25 to 0.25
- w_down: bfloat16 [1024, 512], replicated, may hold values from -0.1875 to 0.1875
Outputs:
- updated: bfloat16 [8192, 512], P(('groups', 'blk')), parts along dimension 0
There are 2 independent parts, one for each index of `groups`. A program takes and returns all parts, laid end to end along the dimension named above; an argument that names none is the same for every part. Nothing has to cross between parts.
Inputs may be any that keep to these rules, and one draw needn't show every extreme that they name: `block_count`: in every draw exactly one device of each part uses all 48 slots; the others use 48 // 6 to 24. `block_rows`: no two slots of one device name the same row block and column block.
All inputs are finite; a program needn't handle non-finite values.
Results may differ from a plain program's by a relative error of at most 0.0055.
Values may be sent and summed in bfloat16 or wider, within the bound.
No kernel may reach another device: no remote copies, remote signals or barrier semaphores. Data moves between devices by JAX's collectives and lax.ppermute only.
A program may use at most 128 MiB of HBM per device.

v0:
```python
import jax
import jax.numpy as jnp
from jax import lax
from jax.sharding import PartitionSpec as P

HEADS = 8


def layer_norm(values, gain):
    mean = jnp.mean(values, axis=-1, keepdims=True)
    centered = values - mean
    var = jnp.mean(centered * centered, axis=-1, keepdims=True)
    return centered * lax.rsqrt(var + 1e-05) * gain


def on_device(
    features,
    tiles,
    block_rows,
    block_cols,
    block_count,
    ln_gain,
    w_msg,
    w_query,
    w_key,
    w_value,
    w_gate,
    w_out,
    omega,
    ln2_gain,
    w_up,
    w_down,
):
    hp = lax.Precision.HIGHEST
    node_rows, width = features.shape
    slots, tile_size = (tiles.shape[0], tiles.shape[1])
    row_blocks = node_rows // tile_size
    heads = HEADS
    head_size = width // heads
    base = features.astype(jnp.float32)
    normed = layer_norm(base, ln_gain).astype(jnp.bfloat16)
    message_src = jnp.dot(normed, w_msg, preferred_element_type=jnp.float32).astype(jnp.bfloat16)
    valid = (jnp.arange(slots, dtype=jnp.int32) < block_count[0]).astype(jnp.float32)
    row_onehot = (block_rows[:, None] == jnp.arange(row_blocks, dtype=jnp.int32)[None, :]).astype(
        jnp.float32
    ) * valid[:, None]
    gathered = lax.all_gather(message_src, "blk", axis=0, tiled=True)
    blocks = gathered.reshape(-1, tile_size, width)[block_cols]
    products = jnp.einsum("sij,sjd->sid", tiles, blocks, preferred_element_type=jnp.float32)
    local = jnp.einsum("sr,sid->rid", row_onehot, products, precision=hp).reshape(node_rows, width)
    scale = head_size ** (-0.25)
    query = (
        jnp.dot(normed, w_query, preferred_element_type=jnp.float32).reshape(
            node_rows, heads, head_size
        )
        * scale
    )
    keys = (
        jnp.dot(normed, w_key, preferred_element_type=jnp.float32).reshape(
            node_rows, heads, head_size
        )
        * scale
    )
    values = jnp.dot(normed, w_value, preferred_element_type=jnp.float32).reshape(
        node_rows, heads, head_size
    )
    qfeat = jnp.exp(jnp.einsum("nhe,em->nhm", query, omega, precision=hp))
    kfeat = jnp.exp(
        jnp.einsum("nhe,em->nhm", keys, omega, precision=hp)
        - 0.5 * jnp.sum(keys * keys, axis=-1, keepdims=True)
    )
    kv_part = jnp.einsum("nhm,nhe->hme", kfeat, values, precision=hp)
    ksum_part = jnp.sum(kfeat, axis=0)
    kvsum, ksum = lax.psum((kv_part, ksum_part), "blk")
    numer = jnp.einsum("nhm,hme->nhe", qfeat, kvsum, precision=hp)
    denom = jnp.einsum("nhm,hm->nh", qfeat, ksum, precision=hp)
    attn = (numer / denom[:, :, None]).reshape(node_rows, width)
    gate = jax.nn.sigmoid(jnp.dot(normed, w_gate, preferred_element_type=jnp.float32))
    gated = (attn * gate).astype(jnp.bfloat16)
    mixed = base + local + jnp.dot(gated, w_out, preferred_element_type=jnp.float32)
    second = layer_norm(mixed, ln2_gain).astype(jnp.bfloat16)
    inner = jax.nn.relu(jnp.dot(second, w_up, preferred_element_type=jnp.float32)).astype(
        jnp.bfloat16
    )
    return (mixed + jnp.dot(inner, w_down, preferred_element_type=jnp.float32)).astype(jnp.bfloat16)


def solution(mesh):
    return jax.shard_map(
        on_device,
        mesh=mesh,
        in_specs=(
            P(("groups", "blk"), None),
            P(("groups", "blk"), None, None),
            P(("groups", "blk")),
            P(("groups", "blk")),
            P(("groups", "blk")),
            P(),
            P(),
            P(),
            P(),
            P(),
            P(),
            P(),
            P(),
            P(),
            P(),
            P(),
        ),
        out_specs=P(("groups", "blk"), None),
        check_vma=False,
    )
```

profile of v0, /device:TPU:0, one launch (start us, length us, event | category | flops | bytes accessed | tf_op | source)
XLA Modules:
  0.0 211.6 jit_solution(14234806525752495728)
XLA Ops:
  6.5 0.0 copy-start
  6.5 0.0 all-reduce.2.cloned.1.call-start
  6.6 1.2 convert_reduce_fusion
  7.8 1.2 fusion.13
  9.0 1.5 convolution_multiply_fusion.1
  10.5 0.2 copy.20
  10.7 0.0 copy-start.6
  10.7 0.1 multiply_reduce_fusion.1
  10.8 1.6 fusion.38
  12.3 2.7 %fusion.42 = (f32[8,128]{1,0:T(8,128)S(1)}, f32[256,8,128]{2,0,1:T(8,128)S(1)}) fusion(f32[256,8]{0,1:T(8,128)S(1)} %broadcast_multiply_fusion, f32[256,8,64]{0,2,1:T(8,128)S(1)} %bitcast.53, f32[64,128]{1,0:T(8,128)} %param.28), kind=kOutput, calls=%fused_computation.59 | convolution fusion | flops 201849856 | bytes 1617920 | tf_op jit(solution)/shard_map/nhe,em->nhm/dot_general | solution.py:69
  15.1 1.5 fusion.47
  16.6 0.0 all-reduce.2.cloned.1.call-update
  16.6 0.0 all-gather.2.cloned.1.call-start
  16.7 2.1 convolution_convert_fusion
  18.8 0.0 all-gather.2.cloned.1.call-update
  18.8 1.4 convolution_multiply_fusion
  20.2 0.2 copy.22
  20.4 35.1 %psum.15 = f32[8,128]{1,0:T(8,128)S(1)} all-reduce(f32[8,128]{1,0:T(8,128)S(1)} %get-tuple-element.5), channel_id=1, replica_groups=mesh['groups'=2,'blk'=16] {'blk'}, use_global_device_ids=true, to_apply=%region_5.0 | all-reduce | flops 1024 | bytes 8192 | tf_op jit(solution)/shard_map/psum | solution.py:74
  55.6 1.8 convolution_exponential_fusion
  57.4 1.0 fusion.48
  59.0 0.0 copy-done.6
  59.1 49.1 %all-reduce.2.cloned.1.call-done = f32[8,128,64]{1,2,0:T(8,128)} async-done(((f32[8,128,64]{1,2,0:T(8,128)}), f32[8,128,64]{1,2,0:T(8,128)}) %all-reduce.2.cloned.1.call-update) | async-done | bytes 262160 | tf_op jit(solution)/shard_map/psum | solution.py:74
  108.2 2.2 %fusion.5 = f32[256,8,64]{0,2,1:T(8,128)S(1)} fusion(f32[8,128,64]{1,2,0:T(8,128)} %all-reduce.2.cloned.1.call-done, f32[256,8,128]{2,0,1:T(8,128)S(1)} %convolution_exponential_fusion, f32[256,8]{0,1:T(8,128)S(1)} %bitcast.58), kind=kOutput, calls=%fused_computation.12 | convolution fusion | flops 201457664 | bytes 1843200 | tf_op jit(solution)/shard_map/nhm,hme->nhe/dot_general | solution.py:75
  110.4 51.1 %all-gather.2.cloned.1.call-done = bf16[4096,512]{1,0:T(8,128)(2,1)} async-done(((bf16[256,512]{1,0:T(8,128)(2,1)}), bf16[4096,512]{1,0:T(8,128)(2,1)}) %all-gather.2.cloned.1.call-update) | async-done | bytes 4194320 | tf_op jit(solution)/shard_map/all_gather | solution.py:47
  161.5 7.1 %gather_fusion = bf16[48,128,512]{2,1,0:T(8,128)(2,1)} fusion(bf16[32,128,512]{2,1,0:T(8,128)(2,1)} %bitcast.52, s32[1024]{0:T(1024)S(1)} %pad_clamp_fusion), kind=kCustom, calls=%fused_computation | custom fusion | bytes 12583104 | tf_op jit(solution)/shard_map/gather | solution.py:48
  168.6 9.2 %fusion.46 = f32[48,512,128]{2,1,0:T(8,128)} fusion(bf16[48,128,512]{2,1,0:T(8,128)(2,1)} %gather_fusion, bf16[48,128,128]{2,1,0:T(8,128)(2,1)S(1)} %copy-done), kind=kOutput, calls=%fused_computation.61 | convolution fusion | flops 805306368 | bytes 20447232 | tf_op jit(solution)/shard_map/sij,sjd->sid/dot_general | solution.py:49
  177.8 12.8 %copy.23 = f32[48,512,128]{1,0,2:T(8,128)} copy(f32[48,512,128]{2,1,0:T(8,128)} %fusion.46) | data formatting | bytes 25165824 | tf_op jit(solution)/shard_map/sij,sjd->sid/dot_general | solution.py:49
  190.6 8.6 %fusion = f32[2,128,512]{2,0,1:T(2,128)S(1)} fusion(f32[48,512,128]{1,0,2:T(8,128)} %copy.23, f32[48]{0:T(128)S(1)} %compare_convert_fusion, s32[48]{0:T(128)S(1)} %copy-done.4), kind=kOutput, calls=%fused_computation.1 | convolution fusion | flops 75497664 | bytes 13107584 | tf_op jit(solution)/shard_map/sr,sid->rid/dot_general | solution.py:50
  199.2 0.1 copy.19
  199.3 2.2 %fusion.43 = (f32[256]{0:T(256)S(1)}, f32[256,512]{1,0:T(8,128)S(1)}) fusion(bf16[512,512]{1,0:T(8,128)(2,1)} %param.27, f32[256,512]{0,1:T(8,128)S(1)} %bitcast.56, bf16[512,512]{1,0:T(8,128)(2,1)} %param.26, bf16[256,512]{1,0:T(8,128)(2,1)S(1)} %copy-done.1, f32[512]{0:T(512)S(1)} %copy-done.3, f32[256]{0:T(256)S(1)} %add_rsqrt_fusion.1, ...), kind=kOutput, calls=%fused_computation.60 | convolution fusion | flops 270270208 | bytes 2888704 | tf_op jit(solution)/shard_map/dot_general | solution.py:80
  201.5 0.2 multiply_reduce_fusion
  201.8 3.0 %fusion.10 = bf16[256,512]{1,0:T(8,128)(2,1)} fusion(f32[256,512]{1,0:T(8,128)S(1)} %get-tuple-element.8, bf16[1024,512]{1,0:T(8,128)(2,1)} %param.31, bf16[512,1024]{1,0:T(8,128)(2,1)} %param.30, f32[512]{0:T(512)S(1)} %copy-done.5, f32[256]{0:T(256)S(1)} %add_rsqrt_fusion, f32[256]{0:T(256)S(1)} %broadcast_multiply_fusion.1), kind=kOutput, calls=%fused_computation.20 | convolution fusion | flops 538181632 | bytes 2887680 | tf_op jit(solution)/shard_map/dot_general | solution.py:85
  (20 shorter events, 0.1 us)
Async XLA Ops:
  6.5 162.0 %copy-start = (bf16[48,128,128]{2,1,0:T(8,128)(2,1)S(1)}, bf16[48,128,128]{2,1,0:T(8,128)(2,1)}, u32[]{:S(2)}) copy-start(bf16[48,128,128]{2,1,0:T(8,128)(2,1)} %param.17) | copy-start | bytes 4718596
  6.5 10.1 %copy-start.1 = (bf16[256,512]{1,0:T(8,128)(2,1)S(1)}, bf16[256,512]{1,0:T(8,128)(2,1)}, u32[]{:S(2)}) copy-start(bf16[256,512]{1,0:T(8,128)(2,1)} %param.16) | copy-start | bytes 786436
  6.5 10.1 %copy-start.3 = (f32[512]{0:T(512)S(1)}, f32[512]{0:T(512)}, u32[]{:S(2)}) copy-start(f32[512]{0:T(512)} %param.21) | copy-start | bytes 6148
  6.5 49.0 %copy-start.2 = (f32[64,128]{1,0:T(8,128)S(1)}, f32[64,128]{1,0:T(8,128)}, u32[]{:S(2)}) copy-start(f32[64,128]{1,0:T(8,128)} %param.28) | copy-start | bytes 98308
  6.5 101.7 %all-reduce.2.cloned.1.call-start = ((), (), s32[]{:S(2)}) async-start(), calls=%async_computation.1 | async-start | bytes 524288 | tf_op jit(solution)/shard_map/psum | solution.py:74
  10.7 48.4 %copy-start.6 = (s32[48]{0:T(128)S(1)}, s32[48]{0:T(128)}, u32[]{:S(2)}) copy-start(s32[48]{0:T(128)} %param.19) | copy-start | bytes 580
  16.6 144.8 %all-gather.2.cloned.1.call-start = ((), (), s32[]{:S(2)}) async-start(), calls=%async_computation | async-start | bytes 4456448 | tf_op jit(solution)/shard_map/all_gather | solution.py:47
  177.8 12.8 %copy-start.4 = (s32[48]{0:T(128)S(1)}, s32[48]{0:T(128)}, u32[]{:S(2)}) copy-start(s32[48]{0:T(128)} %param.18) | copy-start | bytes 580
  190.6 11.1 %copy-start.5 = (f32[512]{0:T(512)S(1)}, f32[512]{0:T(512)}, u32[]{:S(2)}) copy-start(f32[512]{0:T(512)} %param.29) | copy-start | bytes 6148
Sparse Core Ops, SparseCore 0:
  16.7 91.4 all-reduce.1
  110.4 51.0 all-gather.1
where the time goes:
time: 212 us
  waiting for transfers between devices  100 us (47%)
  matrix products  38.8 us (18%)
  blocking collectives  35.1 us (17%)
  local copies, waits for them, and re-layouts  20.5 us (10%)
  between operations  14.3 us (7%)
  other arithmetic  2.65 us (1%)
    all_gather x1, waiting for transfers between devices, on_device(): gathered = lax.all_gather(message_src, 'blk', axis=0, tiled=True)  51.1 us
    psum x1, waiting for transfers between devices, on_device(): kvsum, ksum = lax.psum((kv_part, ksum_part), 'blk')  49.1 us
    psum x1, blocking collectives, on_device(): kvsum, ksum = lax.psum((kv_part, ksum_part), 'blk')  35.1 us
    dot_general x1, local copies, waits for them, and re-layouts, on_device(): jnp.einsum('sij,sjd->sid', tiles, blocks, preferred_element_type=jnp.floa...  12.8 us
    dot_general x1, matrix products, on_device(): jnp.einsum('sij,sjd->sid', tiles, blocks, preferred_element_type=jnp.floa...  9.21 us
    dot_general x1, matrix products, on_device(): jnp.einsum('sr,sid->rid', row_onehot, products, precision=hp)  8.58 us
    gather x1, local copies, waits for them, and re-layouts, on_device(): blocks = gathered.reshape(-1, tile_size, width)[block_cols]  7.11 us
  transfers between devices with their start and end apart: 2, of which 2 were waited for; matrix products, arithmetic and copies ran while one was open for 4% of the time, Pallas kernels for 0%

commit v1 on v0

v1 whole, which is shorter than its diff:
```python
import jax
import jax.numpy as jnp
from jax import lax
from jax.experimental import pallas as pl
from jax.experimental.pallas import tpu as pltpu
from jax.sharding import PartitionSpec as P

HEADS = 8
EPS = 1e-05
F32 = jnp.float32
BF16 = jnp.bfloat16
VMEM = pl.BlockSpec(memory_space=pltpu.VMEM)
SMEM = pl.BlockSpec(memory_space=pltpu.SMEM)


def dot(a, b):
    return jnp.dot(a, b, preferred_element_type=F32)


def split(value):
    high = value.astype(BF16)
    return high, (value - high.astype(F32)).astype(BF16)


def layer_norm(values, gain):
    mean = jnp.mean(values, axis=-1, keepdims=True)
    centered = values - mean
    var = jnp.mean(centered * centered, axis=-1, keepdims=True)
    return (centered * lax.rsqrt(var + EPS) * gain).astype(BF16)


def call(body, outs, specs, args, flops, nbytes):
    return pl.pallas_call(
        body,
        out_shape=outs,
        in_specs=specs,
        out_specs=jax.tree.map(lambda _: VMEM, outs),
        compiler_params=pltpu.CompilerParams(vmem_limit_bytes=56 * 1024 * 1024),
        cost_estimate=pl.CostEstimate(flops=flops, bytes_accessed=nbytes, transcendentals=0),
    )(*args)


def sds(shape, dtype):
    return jax.ShapeDtypeStruct(shape, dtype)


def pair_ones(rows, lanes):
    top = lax.broadcasted_iota(jnp.int32, (rows, lanes), 0) < rows // 2
    left = lax.broadcasted_iota(jnp.int32, (rows, lanes), 1) < lanes // 2
    return jnp.where(top == left, 1.0, 0.0)


def pair_omega(omega):
    zero = jnp.zeros_like(omega)
    return jnp.concatenate(
        [jnp.concatenate([omega, zero], axis=1), jnp.concatenate([zero, omega], axis=1)], axis=0
    )


def message_kernel(x_ref, gain_ref, w_ref, normed_ref, msg_ref):
    normed = layer_norm(x_ref[...].astype(F32), gain_ref[...])
    normed_ref[...] = normed
    msg_ref[...] = dot(normed, w_ref[...]).astype(BF16)


def kv_kernel(core_ref, normed_ref, wk_ref, wv_ref, omega_ref, mine_ref, other_ref):
    normed = normed_ref[...]
    width = normed.shape[1]
    head = width // HEADS
    feat = omega_ref.shape[1]
    keys = dot(normed, wk_ref[...]) * (head ** (-0.25))
    values = dot(normed, wv_ref[...])
    high, low = split(pair_omega(omega_ref[...]))
    ones = (-0.5 * pair_ones(2 * head, 2 * feat)).astype(BF16)
    first = jnp.concatenate([high, high], axis=0)
    second = jnp.concatenate([low, ones, ones], axis=0)
    left = lax.broadcasted_iota(jnp.int32, (feat, 2 * head), 1) < head
    blocks, sums = [], []
    for pair in range(HEADS // 2):
        cols = slice(pair * 2 * head, (pair + 1) * 2 * head)
        k_pair = keys[:, cols]
        k_high, k_low = split(k_pair)
        s_high, s_low = split(k_pair * k_pair)
        logits = dot(jnp.concatenate([k_high, k_low], axis=1), first) + dot(
            jnp.concatenate([k_high, s_high, s_low], axis=1), second
        )
        kfeat = jnp.exp(logits)
        total = jnp.sum(kfeat, axis=0, keepdims=True)
        sums += [total[:, :feat], total[:, feat:]]
        f_high, f_low = split(kfeat)
        v_high, v_low = split(values[:, cols])
        dims = (((0,), (0,)), ((), ()))
        product = lax.dot_general(f_high, v_high, dims, preferred_element_type=F32)
        product += lax.dot_general(f_low, v_high, dims, preferred_element_type=F32)
        product += lax.dot_general(f_high, v_low, dims, preferred_element_type=F32)
        blocks.append(jnp.where(left, product[:feat], product[feat:]))
    half = HEADS // 4
    pad = jnp.zeros((16 - 2 * half, feat), F32)
    low_part = jnp.concatenate(blocks[:half] + sums[: 2 * half] + [pad], axis=0)
    high_part = jnp.concatenate(blocks[half:] + sums[2 * half :] + [pad], axis=0)
    first_core = core_ref[0] == 0
    mine_ref[...] = jnp.where(first_core, low_part, high_part)
    other_ref[...] = jnp.where(first_core, high_part, low_part).astype(BF16)


def query_kernel(normed_ref, wq_ref, wg_ref, omega_ref, qf_ref, gate_ref):
    normed = normed_ref[...]
    width = normed.shape[1]
    head = width // HEADS
    feat = omega_ref.shape[1]
    query = dot(normed, wq_ref[...]) * (head ** (-0.25))
    high, low = split(pair_omega(omega_ref[...]))
    first = jnp.concatenate([high, high], axis=0)
    for pair in range(HEADS // 2):
        q_high, q_low = split(query[:, pair * 2 * head : (pair + 1) * 2 * head])
        logits = dot(jnp.concatenate([q_high, q_low], axis=1), first) + dot(q_high, low)
        qf_ref[:, pair * 2 * feat : (pair + 1) * 2 * feat] = jnp.exp(logits).astype(BF16)
    gate_ref[...] = jax.nn.sigmoid(dot(normed, wg_ref[...]))


def place_kernel(rows_ref, cols_ref, count_ref, tiles_ref, dense_ref):
    dense_ref[...] = jnp.zeros_like(dense_ref)

    def body(slot, carry):
        dense_ref[cols_ref[slot], rows_ref[slot]] = tiles_ref[slot]
        return carry

    lax.fori_loop(0, count_ref[0], body, 0)


def attend_kernel(core_ref, x_ref, qf_ref, gate_ref, own_ref, swapped_ref, wo_ref, mixed_ref):
    feat = own_ref.shape[1]
    width = x_ref.shape[1]
    head = width // HEADS
    half = HEADS // 4
    own = own_ref[...]
    swapped = swapped_ref[...].astype(F32)
    first_core = core_ref[0] == 0
    parts = [jnp.where(first_core, own, swapped), jnp.where(first_core, swapped, own)]
    left = lax.broadcasted_iota(jnp.int32, (feat, 2 * head), 1) < head
    ones = pair_ones(2 * feat, 2 * head).astype(BF16)
    joined = []
    for pair in range(HEADS // 2):
        part = parts[pair // half]
        place = pair % half
        block = part[place * feat : (place + 1) * feat]
        block = jnp.concatenate([jnp.where(left, block, 0.0), jnp.where(left, 0.0, block)], axis=0)
        base = half * feat + 2 * place
        ksum = jnp.concatenate([part[base : base + 1], part[base + 1 : base + 2]], axis=1)
        q_pair = qf_ref[:, pair * 2 * feat : (pair + 1) * 2 * feat]
        numer = dot(q_pair, block.astype(BF16))
        d_high, d_low = split(q_pair.astype(F32) * ksum)
        denom = dot(d_high, ones) + dot(d_low, ones)
        joined.append(numer / denom)
    attn = jnp.concatenate(joined, axis=1)
    gated = (attn * gate_ref[...]).astype(BF16)
    mixed_ref[...] = x_ref[...].astype(F32) + dot(gated, wo_ref[...])


def add_messages(total, dense_ref, source_ref, start, chunks):
    for place, chunk in enumerate(chunks):
        device = source_ref[start + place]
        tile = dense_ref.shape[2]
        rows = dense_ref.shape[1]
        per = chunk.shape[0] // tile
        weights = jnp.concatenate(
            [
                jnp.concatenate([dense_ref[device * per + col, row] for col in range(per)], axis=1)
                for row in range(rows)
            ],
            axis=0,
        )
        total = total + dot(weights, chunk[...])
    return total


def early_kernel(source_ref, mixed_ref, dense_ref, *refs):
    refs[-1][...] = add_messages(mixed_ref[...], dense_ref, source_ref, 0, refs[:-1])


def solution(mesh):
    size = mesh.shape["blk"]
    chips = size // 2
    order = chip_order(mesh, size)

    def step(value, shift):
        pairs = [
            (order[p] * 2 + c, order[(p + shift) % chips] * 2 + c)
            for p in range(chips)
            for c in range(2)
        ]
        return lax.ppermute(value, "blk", pairs)

    def flip(value, bit):
        return lax.ppermute(value, "blk", [(i, i ^ bit) for i in range(size)])

    def on_device(
        features,
        tiles,
        block_rows,
        block_cols,
        block_count,
        ln_gain,
        w_msg,
        w_query,
        w_key,
        w_value,
        w_gate,
        w_out,
        omega,
        ln2_gain,
        w_up,
        w_down,
    ):
        nodes, width = features.shape
        tile = tiles.shape[1]
        feat = omega.shape[1]
        head = width // HEADS
        row_blocks = nodes // tile
        me = lax.axis_index("blk")
        core = (me % 2).reshape(1)
        normed, message = call(
            message_kernel,
            (sds((nodes, width), BF16), sds((nodes, width), BF16)),
            [VMEM] * 3,
            (features, ln_gain.reshape(1, width), w_msg),
            2 * nodes * width * width,
            2 * (width * width + 3 * nodes * width),
        )

        stages = [[message, flip(message, 1)]]
        sources = [[0, 0]]
        ahead = back = message
        full = (chips - 1) // 2
        for k in range(1, full + 1):
            ahead = step(ahead, 1)
            back = step(back, -1)
            stages.append([ahead, back, flip(ahead, 1), flip(back, 1)])
            sources.append([k, -k, k, -k])
        if chips % 2 == 0:
            half = nodes // 2
            upper = step(ahead[:half], 1)
            lower = step(back[half:], -1)
            last = jnp.concatenate([upper, lower], axis=0)
            stages.append([last, flip(last, 1)])
            sources.append([chips // 2] * 2)
        place = {chip: p for p, chip in enumerate(order)}
        table = []
        for device in range(size):
            entries = []
            for stage in sources:
                for i, shift in enumerate(stage):
                    chip = order[(place[device // 2] - shift) % chips]
                    same = i < len(stage) // 2
                    entries.append(chip * 2 + (device % 2 if same else 1 - device % 2))
            table.append(entries)
        source = jnp.asarray(table, jnp.int32)[me]

        rows = HEADS // 4 * feat + 16
        own, other = call(
            kv_kernel,
            (sds((rows, feat), F32), sds((rows, feat), BF16)),
            [SMEM] + [VMEM] * 4,
            (core, normed, w_key, w_value, omega),
            6 * nodes * width * width,
            4 * width * width,
        )
        own = own + flip(other, 1).astype(F32)
        if chips & (chips - 1) == 0:
            bit = 2
            while bit < size:
                own = own + flip(own.astype(BF16), bit).astype(F32)
                bit *= 2
        else:
            own = lax.psum(
                own, "blk", axis_index_groups=[list(range(c, size, 2)) for c in range(2)]
            )
        swapped = flip(own.astype(BF16), 1)

        qfeat, gate = call(
            query_kernel,
            (sds((nodes, HEADS * feat), BF16), sds((nodes, width), F32)),
            [VMEM] * 4,
            (normed, w_query, w_gate, omega),
            6 * nodes * width * width,
            4 * width * width,
        )
        dense = call(
            place_kernel,
            sds((size * row_blocks, row_blocks, tile, tile), BF16),
            [SMEM] * 3 + [VMEM],
            (block_rows, block_cols, block_count, tiles),
            0,
            4 * tiles.size,
        )
        mixed = call(
            attend_kernel,
            sds((nodes, width), F32),
            [SMEM] + [VMEM] * 6,
            (core, features, qfeat, gate, own, swapped, w_out),
            4 * nodes * width * width,
            4 * width * width,
        )
        early = [chunk for stage in stages[:-1] for chunk in stage]
        late = stages[-1]
        mixed = call(
            early_kernel,
            sds((nodes, width), F32),
            [SMEM] + [VMEM] * (2 + len(early)),
            (source, mixed, dense, *early),
            2 * nodes * nodes * width * len(early),
            2 * nodes * width * len(early),
        )
        start = len(early)

        def final_kernel(source_ref, mixed_ref, dense_ref, gain_ref, up_ref, down_ref, *refs):
            mixed = add_messages(mixed_ref[...], dense_ref, source_ref, start, refs[:-1])
            second = layer_norm(mixed, gain_ref[...])
            inner = jnp.maximum(dot(second, up_ref[...]), 0.0).astype(BF16)
            refs[-1][...] = (mixed + dot(inner, down_ref[...])).astype(BF16)

        return call(
            final_kernel,
            sds((nodes, width), BF16),
            [SMEM] + [VMEM] * (5 + len(late)),
            (source, mixed, dense, ln2_gain.reshape(1, width), w_up, w_down, *late),
            4 * nodes * width * w_up.shape[1],
            4 * width * w_up.shape[1],
        )

    split_rows = P(("groups", "blk"))
    return jax.shard_map(
        on_device,
        mesh=mesh,
        in_specs=(split_rows,) * 5 + (P(),) * 11,
        out_specs=P(("groups", "blk"), None),
        check_vma=False,
    )


def chip_order(mesh, size):
    devices = mesh.devices.reshape(-1, size)[0]
    coords = [getattr(d, "coords", None) for d in devices[::2]]
    if any(c is None for c in coords) or len({c[1] for c in map(tuple, coords)}) != 2:
        return list(range(size // 2))
    low = min(c[1] for c in coords)
    up = sorted((i for i, c in enumerate(coords) if c[1] == low), key=lambda i: coords[i][2])
    down = sorted((i for i, c in enumerate(coords) if c[1] != low), key=lambda i: -coords[i][2])
    return up + down
```

time: 212 us -> 62.5 us (0.29)
  waiting for transfers between devices: 100 us -> 11.8 us
  matrix products: 38.8 us -> 0 us
  blocking collectives: 35.1 us -> 0 us
  Pallas kernels: 0 us -> 24.1 us
  starting transfers between devices: 0.08 us -> 18.2 us
  local copies, waits for them, and re-layouts: 20.5 us -> 3.51 us
  between operations: 14.3 us -> 0.87 us
    all_gather x1 -> x0, waiting for transfers between devices: 51.1 us -> none  [on_device(): gathered = lax.all_gather(message_src, 'blk', axis=0, tiled=True)]
    psum x1 -> x0, waiting for transfers between devices: 49.1 us -> none  [on_device(): kvsum, ksum = lax.psum((kv_part, ksum_part), 'blk')]
    dot_general x13 -> x0, matrix products: 38.8 us -> none  [the longest x1 9.21 us: on_device(): jnp.einsum('sij,sjd->sid', tiles, blocks, preferred_element_type=jnp.floa...]
    psum x1 -> x0, blocking collectives: 35.1 us -> none  [on_device(): kvsum, ksum = lax.psum((kv_part, ksum_part), 'blk')]
    pallas_call x0 -> x7, Pallas kernels: none -> 24.1 us  [call(): pl.pallas_call(body, out_shape=outs, in_specs=specs, out_specs=jax.tree.m...]
    ppermute x0 -> x21, starting transfers between devices: none -> 18.2 us  [the longest x8 9.09 us: step(): return lax.ppermute(value, 'blk', pairs)]
    dot_general x3 -> x0, local copies, waits for them, and re-layouts: 12.9 us -> none  [the longest x1 12.8 us: on_device(): jnp.einsum('sij,sjd->sid', tiles, blocks, preferred_element_type=jnp.floa...]
    ppermute x0 -> x21, waiting for transfers between devices: none -> 11.8 us  [the longest x8 10.7 us: step(): return lax.ppermute(value, 'blk', pairs)]
  transfers between devices with their start and end apart: 2 -> 21, of which waited for: 2 -> 5; matrix products, arithmetic and copies ran while one was open for 4% -> 8% of each run, Pallas kernels for 0% -> 22%
where the time goes in v1:
time: 62.5 us; the launch traced here: 62 us
  Pallas kernels  24.1 us (39%)
  starting transfers between devices  18.2 us (29%)
  waiting for transfers between devices  11.8 us (19%)
  other arithmetic  3.52 us (6%)
  local copies, waits for them, and re-layouts  3.51 us (6%)
  between operations  0.87 us (1%)
    pallas_call x7, Pallas kernels, call(): pl.pallas_call(body, out_shape=outs, in_specs=specs, out_specs=jax.tree.m...  24.1 us
    ppermute x8, waiting for transfers between devices, step(): return lax.ppermute(value, 'blk', pairs)  10.7 us
    ppermute x8, starting transfers between devices, step(): return lax.ppermute(value, 'blk', pairs)  9.09 us
    ppermute x13, starting transfers between devices, flip(): return lax.ppermute(value, 'blk', [(i, i ^ bit) for i in range(size)])  9.07 us
    convert_element_type x3, other arithmetic, on_device(): own = own + flip(own.astype(BF16), bit).astype(F32)  2.81 us
    unnamed x37, local copies, waits for them, and re-layouts  2.25 us
  transfers between devices with their start and end apart: 21, of which 5 were waited for; matrix products, arithmetic and copies ran while one was open for 8% of the time, Pallas kernels for 22%

profile of v1, /device:TPU:0, one launch (start us, length us, event | category | flops | bytes accessed | tf_op | source)
XLA Modules:
  0.0 62.0 jit_solution(15529815191936551560)
XLA Ops:
  0.0 2.3 %shard_map.163 = (bf16[256,512]{1,0:T(8,128)(2,1)}, bf16[256,512]{1,0:T(8,128)(2,1)}) custom-call(bf16[256,512]{1,0:T(8,128)(2,1)} %x_ref.3, f32[1,512]{1,0:T(1,128)} %bitcast.5, bf16[512,512]{1,0:T(8,128)(2,1)} %w_ref.1), custom_call_target="tpu_custom_call" | custom-call | flops 134217728 | bytes 1310720 | tf_op jit(solution)/shard_map/pallas_call | solution.py:33
  2.3 3.6 %shard_map.165 = (f32[272,128]{1,0:T(8,128)}, bf16[272,128]{1,0:T(8,128)(2,1)}) custom-call(s32[1]{0:T(128)} %bitcast.1.core_ref, bf16[256,512]{1,0:T(8,128)(2,1)} %get-tuple-element.11.normed_ref, bf16[512,512]{1,0:T(8,128)(2,1)} %wk_ref.1, bf16[512,512]{1,0:T(8,128)(2,1)} %wv_ref.1, f32[64,128]{1,0:T(8,128)} %omega_ref.3), custom_call_target="tpu_custom_call" | custom-call | flops 402653184 | bytes 1048576 | tf_op jit(solution)/shard_map/pallas_call | solution.py:33
  6.0 0.5 collective-permute-start
  6.4 2.6 %collective-permute-start.6 = (bf16[256,512]{1,0:T(8,128)(2,1)}, bf16[256,512]{1,0:T(8,128)(2,1)S(1)}, u32[]{:S(2)}, u32[]{:S(2)}) collective-permute-start(bf16[256,512]{1,0:T(8,128)(2,1)} %get-tuple-element.16.refs_0_), channel_id=1, source_target_pairs={{0,4},{1,5},{4,8},{5,9},{8,12},{9,13},{12,14},{13,15},{14,10},{15,... | collective-permute-start | bytes 786440 | tf_op jit(solution)/shard_map/ppermute | solution.py:192
  9.0 0.9 %fusion = bf16[272,128]{1,0:T(8,128)(2,1)S(1)} fusion(f32[272,128]{1,0:T(8,128)} %get-tuple-element.14, bf16[272,128]{1,0:T(8,128)(2,1)S(1)} %collective-permute-done), kind=kLoop, calls=%fused_computation.4 | loop fusion | flops 104448 | bytes 278528 | tf_op jit(solution)/shard_map/convert_element_type | solution.py:272
  9.9 2.0 %collective-permute-start.1 = (bf16[272,128]{1,0:T(8,128)(2,1)S(1)}, bf16[272,128]{1,0:T(8,128)(2,1)S(1)}, u32[]{:S(2)}, u32[]{:S(2)}) collective-permute-start(bf16[272,128]{1,0:T(8,128)(2,1)S(1)} %fusion), channel_id=1, source_target_pairs={{0,2},{1,3},{2,0},{3,1},{4,6},{5,7},{6,4},{7,5},{8,10},{9,11},{10,... | collective-permute-start | bytes 208904 | tf_op jit(solution)/shard_map/ppermute | solution.py:195
  12.0 4.3 %collective-permute-done.6.refs_2_ = bf16[256,512]{1,0:T(8,128)(2,1)S(1)} collective-permute-done((bf16[256,512]{1,0:T(8,128)(2,1)}, bf16[256,512]{1,0:T(8,128)(2,1)S(1)}, u32[]{:S(2)}, u32[]{:S(2)}) %collective-permute-start.6) | collective-permute-done | bytes 262176 | tf_op jit(solution)/shard_map/ppermute | solution.py:192
  16.3 1.6 %collective-permute-start.10 = (bf16[256,512]{1,0:T(8,128)(2,1)S(1)}, bf16[256,512]{1,0:T(8,128)(2,1)S(1)}, u32[]{:S(2)}, u32[]{:S(2)}) collective-permute-start(bf16[256,512]{1,0:T(8,128)(2,1)S(1)} %collective-permute-done.6.refs_2_), channel_id=1, source_target_pairs={{0,4},{1,5},{4,8},{5,9},{8,12},{9,13},{12,14},{13,15},{14,10},{15,... | collective-permute-start | bytes 786440 | tf_op jit(solution)/shard_map/ppermute | solution.py:192
  18.4 0.9 %fusion.2 = bf16[272,128]{1,0:T(8,128)(2,1)S(1)} fusion(bf16[272,128]{1,0:T(8,128)(2,1)S(1)} %collective-permute-done.1, f32[272,128]{1,0:T(8,128)} %get-tuple-element.14, bf16[272,128]{1,0:T(8,128)(2,1)S(1)} %collective-permute-done), kind=kLoop, calls=%fused_computation.9 | loop fusion | flops 174080 | bytes 348160 | tf_op jit(solution)/shard_map/convert_element_type | solution.py:272
  19.3 1.7 %collective-permute-start.2 = (bf16[272,128]{1,0:T(8,128)(2,1)S(1)}, bf16[272,128]{1,0:T(8,128)(2,1)S(1)}, u32[]{:S(2)}, u32[]{:S(2)}) collective-permute-start(bf16[272,128]{1,0:T(8,128)(2,1)S(1)} %fusion.2), channel_id=1, source_target_pairs={{0,4},{1,5},{2,6},{3,7},{4,0},{5,1},{6,2},{7,3},{8,12},{9,13},{10,... | collective-permute-start | bytes 208904 | tf_op jit(solution)/shard_map/ppermute | solution.py:195
  21.0 3.3 %collective-permute-done.10.refs_6_ = bf16[256,512]{1,0:T(8,128)(2,1)S(1)} collective-permute-done((bf16[256,512]{1,0:T(8,128)(2,1)S(1)}, bf16[256,512]{1,0:T(8,128)(2,1)S(1)}, u32[]{:S(2)}, u32[]{:S(2)}) %collective-permute-start.10) | collective-permute-done | bytes 262176 | tf_op jit(solution)/shard_map/ppermute | solution.py:192
  24.3 2.3 %collective-permute-start.14 = (bf16[256,512]{1,0:T(8,128)(2,1)S(1)}, bf16[256,512]{1,0:T(8,128)(2,1)S(1)}, u32[]{:S(2)}, u32[]{:S(2)}) collective-permute-start(bf16[256,512]{1,0:T(8,128)(2,1)S(1)} %collective-permute-done.10.refs_6_), channel_id=1, source_target_pairs={{0,4},{1,5},{4,8},{5,9},{8,12},{9,13},{12,14},{13,15},{14,10},{15,... | collective-permute-start | bytes 786440 | tf_op jit(solution)/shard_map/ppermute | solution.py:192
  26.6 0.5 collective-permute-done.2
  27.1 0.9 %fusion.1 = bf16[272,128]{1,0:T(8,128)(2,1)S(1)} fusion(bf16[272,128]{1,0:T(8,128)(2,1)S(1)} %collective-permute-done.2, bf16[272,128]{1,0:T(8,128)(2,1)S(1)} %collective-permute-done.1, f32[272,128]{1,0:T(8,128)} %get-tuple-element.14, bf16[272,128]{1,0:T(8,128)(2,1)S(1)} %collective-permute-done), kind=kLoop, calls=%fused_computation.5 | loop fusion | flops 243712 | bytes 417792 | tf_op jit(solution)/shard_map/convert_element_type | solution.py:272
  28.0 2.7 %collective-permute-start.3 = (bf16[272,128]{1,0:T(8,128)(2,1)S(1)}, bf16[272,128]{1,0:T(8,128)(2,1)S(1)}, u32[]{:S(2)}, u32[]{:S(2)}) collective-permute-start(bf16[272,128]{1,0:T(8,128)(2,1)S(1)} %fusion.1), channel_id=1, source_target_pairs={{0,8},{1,9},{2,10},{3,11},{4,12},{5,13},{6,14},{7,15},{8,0},{9,1},... | collective-permute-start | bytes 208904 | tf_op jit(solution)/shard_map/ppermute | solution.py:195
  31.4 3.2 %shard_map.167.dense_ref = bf16[32,2,128,128]{3,2,1,0:T(8,128)(2,1)} custom-call(s32[48]{0:T(128)} %rows_ref.1, s32[48]{0:T(128)} %cols_ref.1, s32[1]{0:T(128)S(6)} %copy.19.count_ref, bf16[48,128,128]{2,1,0:T(8,128)(2,1)} %tiles_ref.1), custom_call_target="tpu_custom_call" | custom-call | bytes 3145728 | tf_op jit(solution)/shard_map/pallas_call | solution.py:33
  34.5 0.5 collective-permute-start.8
  35.2 1.6 %collective-permute-start.18 = (bf16[128,512]{1,0:T(8,128)(2,1)S(1)}, bf16[128,512]{1,0:T(8,128)(2,1)S(1)}, u32[]{:S(2)}, u32[]{:S(2)}) collective-permute-start(bf16[128,512]{1,0:T(8,128)(2,1)S(1)} %slice.8), channel_id=1, source_target_pairs={{0,4},{1,5},{4,8},{5,9},{8,12},{9,13},{12,14},{13,15},{14,10},{15,... | collective-permute-start | bytes 393224 | tf_op jit(solution)/shard_map/ppermute | solution.py:192
  36.8 0.5 collective-permute-start.19
  37.3 0.7 %fusion.3 = (bf16[272,128]{1,0:T(8,128)(2,1)S(1)}, f32[272,128]{1,0:T(8,128)}) fusion(bf16[272,128]{1,0:T(8,128)(2,1)S(1)} %collective-permute-done.3, bf16[272,128]{1,0:T(8,128)(2,1)S(1)} %collective-permute-done.2, bf16[272,128]{1,0:T(8,128)(2,1)S(1)} %collective-permute-done.1, f32[272,128]{1,0:T(8,128)S(1)} %copy-done, ...), kind=kLoop, calls=%fused_computation.10 | loop fusion | flops 313344 | bytes 626688 | tf_op jit(solution)/shard_map/convert_element_type | solution.py:278
  38.0 3.1 %collective-permute-done.18 = bf16[128,512]{1,0:T(8,128)(2,1)S(1)} collective-permute-done((bf16[128,512]{1,0:T(8,128)(2,1)S(1)}, bf16[128,512]{1,0:T(8,128)(2,1)S(1)}, u32[]{:S(2)}, u32[]{:S(2)}) %collective-permute-start.18) | collective-permute-done | bytes 131104 | tf_op jit(solution)/shard_map/ppermute | solution.py:192
  41.2 0.6 collective-permute-start.12
  41.7 0.6 %collective-permute-done.4.swapped_ref = bf16[272,128]{1,0:T(8,128)(2,1)S(1)} collective-permute-done((bf16[272,128]{1,0:T(8,128)(2,1)S(1)}, bf16[272,128]{1,0:T(8,128)(2,1)S(1)}, u32[]{:S(2)}, u32[]{:S(2)}) %collective-permute-start.4) | collective-permute-done | bytes 69664 | tf_op jit(solution)/shard_map/ppermute | solution.py:195
  43.1 0.4 collective-permute-start.20
  43.5 2.9 %shard_map.164 = (bf16[256,1024]{1,0:T(8,128)(2,1)}, f32[256,512]{1,0:T(8,128)}) custom-call(bf16[256,512]{1,0:T(8,128)(2,1)} %get-tuple-element.11.normed_ref, bf16[512,512]{1,0:T(8,128)(2,1)} %wq_ref.1, bf16[512,512]{1,0:T(8,128)(2,1)} %wg_ref.1, f32[64,128]{1,0:T(8,128)} %omega_ref.3), custom_call_target="tpu_custom_call" | custom-call | flops 402653184 | bytes 1048576 | tf_op jit(solution)/shard_map/pallas_call | solution.py:33
  46.5 1.2 %dynamic-slice_bitcast_fusion.source_ref = s32[16]{0:T(128)} fusion(s32[16,16]{1,0:T(8,128)} %constant.22.clone, s32[]{:T(128)S(6)} %select_n.10), kind=kLoop, calls=%fused_computation.8 | loop fusion | bytes 132 | tf_op jit(solution)/shard_map/squeeze | solution.py:257
  47.7 3.0 %shard_map.166.mixed_ref = f32[256,512]{1,0:T(8,128)} custom-call(s32[1]{0:T(128)} %bitcast.1.core_ref, bf16[256,512]{1,0:T(8,128)(2,1)} %x_ref.3, bf16[256,1024]{1,0:T(8,128)(2,1)} %get-tuple-element.12.qf_ref, f32[256,512]{1,0:T(8,128)} %get-tuple-element.13.gate_ref, f32[272,128]{1,0:T(8,128)} %get-tuple-element.18.own_ref, bf16[272,128]{1,0:T(8,128)(2,1)} %copy-done.17, ...), custom_call_target="tpu_custom_call" | custom-call | flops 268435456 | bytes 1048576 | tf_op jit(solution)/shard_map/pallas_call | solution.py:33
  50.8 0.6 %copy-done.12 = bf16[256,512]{1,0:T(8,128)(2,1)} copy-done((bf16[256,512]{1,0:T(8,128)(2,1)}, bf16[256,512]{1,0:T(8,128)(2,1)S(1)}, u32[]{:S(2)}) %copy-start.12) | copy-done | bytes 262168
  51.6 0.7 %copy-done.15 = bf16[256,512]{1,0:T(8,128)(2,1)} copy-done((bf16[256,512]{1,0:T(8,128)(2,1)}, bf16[256,512]{1,0:T(8,128)(2,1)S(1)}, u32[]{:S(2)}) %copy-start.15) | copy-done | bytes 262168
  52.3 4.7 %shard_map.168.mixed_ref = f32[256,512]{1,0:T(8,128)} custom-call(s32[16]{0:T(128)} %dynamic-slice_bitcast_fusion.source_ref, f32[256,512]{1,0:T(8,128)} %shard_map.166.mixed_ref, bf16[32,2,128,128]{3,2,1,0:T(8,128)(2,1)} %shard_map.167.dense_ref, bf16[256,512]{1,0:T(8,128)(2,1)} %get-tuple-element.16.refs_0_, bf16[256,512]{1,0:T(8,128)(2,1)} %copy-done.9, ...), custom_call_target="tpu_custom_call" | custom-call | flops 939524096 | bytes 3670016 | tf_op jit(solution)/shard_map/pallas_call | solution.py:33
  57.0 0.7 %copy-done.16 = bf16[256,512]{1,0:T(8,128)(2,1)} copy-done((bf16[256,512]{1,0:T(8,128)(2,1)}, bf16[256,512]{1,0:T(8,128)(2,1)S(1)}, u32[]{:S(2)}) %copy-start.16) | copy-done | bytes 262168
  57.7 4.3 %shard_map.169 = bf16[256,512]{1,0:T(8,128)(2,1)} custom-call(s32[16]{0:T(128)} %dynamic-slice_bitcast_fusion.source_ref, f32[256,512]{1,0:T(8,128)} %shard_map.168.mixed_ref, bf16[32,2,128,128]{3,2,1,0:T(8,128)(2,1)} %shard_map.167.dense_ref, f32[1,512]{1,0:T(1,128)} %bitcast.6, bf16[512,1024]{1,0:T(8,128)(2,1)} %up_ref.1, bf16[1024,512]{1,0:T(8,128)(2,1)} %down_ref.1, ...), custom_call_target="tpu_custom_call" | custom-call | flops 536870912 | bytes 2097152 | tf_op jit(solution)/shard_map/pallas_call | solution.py:33
  (62 shorter events, 1.5 us)
Async XLA Ops:
  2.3 28.4 %copy-start.4 = (bf16[256,512]{1,0:T(8,128)(2,1)S(1)}, bf16[256,512]{1,0:T(8,128)(2,1)}, u32[]{:S(2)}) copy-start(bf16[256,512]{1,0:T(8,128)(2,1)} %get-tuple-element.16.refs_0_) | copy-start | bytes 786436
  6.0 3.0 %collective-permute-start = (bf16[272,128]{1,0:T(8,128)(2,1)}, bf16[272,128]{1,0:T(8,128)(2,1)S(1)}, u32[]{:S(2)}, u32[]{:S(2)}) collective-permute-start(bf16[272,128]{1,0:T(8,128)(2,1)} %get-tuple-element.15), channel_id=1, source_target_pairs={{0,1},{1,0},{2,3},{3,2},{4,5},{5,4},{6,7},{7,6},{8,9},{9,8},{10,11... | collective-permute-start | bytes 208904 | tf_op jit(solution)/shard_map/ppermute | solution.py:195
  6.4 9.9 %collective-permute-start.6 = (bf16[256,512]{1,0:T(8,128)(2,1)}, bf16[256,512]{1,0:T(8,128)(2,1)S(1)}, u32[]{:S(2)}, u32[]{:S(2)}) collective-permute-start(bf16[256,512]{1,0:T(8,128)(2,1)} %get-tuple-element.16.refs_0_), channel_id=1, source_target_pairs={{0,4},{1,5},{4,8},{5,9},{8,12},{9,13},{12,14},{13,15},{14,10},{15,... | collective-permute-start | bytes 786440 | tf_op jit(solution)/shard_map/ppermute | solution.py:192
  9.0 8.9 %collective-permute-start.7 = (bf16[256,512]{1,0:T(8,128)(2,1)}, bf16[256,512]{1,0:T(8,128)(2,1)S(1)}, u32[]{:S(2)}, u32[]{:S(2)}) collective-permute-start(bf16[256,512]{1,0:T(8,128)(2,1)} %get-tuple-element.16.refs_0_), channel_id=1, source_target_pairs={{0,2},{1,3},{4,0},{5,1},{8,4},{9,5},{12,8},{13,9},{14,12},{15,13},... | collective-permute-start | bytes 786440 | tf_op jit(solution)/shard_map/ppermute | solution.py:192
  9.9 8.4 %collective-permute-start.1 = (bf16[272,128]{1,0:T(8,128)(2,1)S(1)}, bf16[272,128]{1,0:T(8,128)(2,1)S(1)}, u32[]{:S(2)}, u32[]{:S(2)}) collective-permute-start(bf16[272,128]{1,0:T(8,128)(2,1)S(1)} %fusion), channel_id=1, source_target_pairs={{0,2},{1,3},{2,0},{3,1},{4,6},{5,7},{6,4},{7,5},{8,10},{9,11},{10,... | collective-permute-start | bytes 208904 | tf_op jit(solution)/shard_map/ppermute | solution.py:195
  16.3 18.2 %copy-start.5 = (bf16[256,512]{1,0:T(8,128)(2,1)}, bf16[256,512]{1,0:T(8,128)(2,1)S(1)}, u32[]{:S(2)}) copy-start(bf16[256,512]{1,0:T(8,128)(2,1)S(1)} %collective-permute-done.6.refs_2_) | copy-start | bytes 786436
  16.3 8.0 %collective-permute-start.10 = (bf16[256,512]{1,0:T(8,128)(2,1)S(1)}, bf16[256,512]{1,0:T(8,128)(2,1)S(1)}, u32[]{:S(2)}, u32[]{:S(2)}) collective-permute-start(bf16[256,512]{1,0:T(8,128)(2,1)S(1)} %collective-permute-done.6.refs_2_), channel_id=1, source_target_pairs={{0,4},{1,5},{4,8},{5,9},{8,12},{9,13},{12,14},{13,15},{14,10},{15,... | collective-permute-start | bytes 786440 | tf_op jit(solution)/shard_map/ppermute | solution.py:192
  17.9 17.1 %copy-start.6 = (bf16[256,512]{1,0:T(8,128)(2,1)}, bf16[256,512]{1,0:T(8,128)(2,1)S(1)}, u32[]{:S(2)}) copy-start(bf16[256,512]{1,0:T(8,128)(2,1)S(1)} %collective-permute-done.7.refs_3_) | copy-start | bytes 786436
  17.9 8.7 %collective-permute-start.11 = (bf16[256,512]{1,0:T(8,128)(2,1)S(1)}, bf16[256,512]{1,0:T(8,128)(2,1)S(1)}, u32[]{:S(2)}, u32[]{:S(2)}) collective-permute-start(bf16[256,512]{1,0:T(8,128)(2,1)S(1)} %collective-permute-done.7.refs_3_), channel_id=1, source_target_pairs={{0,2},{1,3},{4,0},{5,1},{8,4},{9,5},{12,8},{13,9},{14,12},{15,13},... | collective-permute-start | bytes 786440 | tf_op jit(solution)/shard_map/ppermute | solution.py:192
  19.3 7.8 %collective-permute-start.2 = (bf16[272,128]{1,0:T(8,128)(2,1)S(1)}, bf16[272,128]{1,0:T(8,128)(2,1)S(1)}, u32[]{:S(2)}, u32[]{:S(2)}) collective-permute-start(bf16[272,128]{1,0:T(8,128)(2,1)S(1)} %fusion.2), channel_id=1, source_target_pairs={{0,4},{1,5},{2,6},{3,7},{4,0},{5,1},{6,2},{7,3},{8,12},{9,13},{10,... | collective-permute-start | bytes 208904 | tf_op jit(solution)/shard_map/ppermute | solution.py:195
  24.3 16.9 %copy-start.7 = (bf16[256,512]{1,0:T(8,128)(2,1)}, bf16[256,512]{1,0:T(8,128)(2,1)S(1)}, u32[]{:S(2)}) copy-start(bf16[256,512]{1,0:T(8,128)(2,1)S(1)} %collective-permute-done.10.refs_6_) | copy-start | bytes 786436
  24.3 10.8 %collective-permute-start.14 = (bf16[256,512]{1,0:T(8,128)(2,1)S(1)}, bf16[256,512]{1,0:T(8,128)(2,1)S(1)}, u32[]{:S(2)}, u32[]{:S(2)}) collective-permute-start(bf16[256,512]{1,0:T(8,128)(2,1)S(1)} %collective-permute-done.10.refs_6_), channel_id=1, source_target_pairs={{0,4},{1,5},{4,8},{5,9},{8,12},{9,13},{12,14},{13,15},{14,10},{15,... | collective-permute-start | bytes 786440 | tf_op jit(solution)/shard_map/ppermute | solution.py:192
  26.6 15.7 %copy-start.8 = (bf16[256,512]{1,0:T(8,128)(2,1)}, bf16[256,512]{1,0:T(8,128)(2,1)S(1)}, u32[]{:S(2)}) copy-start(bf16[256,512]{1,0:T(8,128)(2,1)S(1)} %collective-permute-done.11.refs_7_) | copy-start | bytes 786436
  26.6 8.5 %collective-permute-start.15 = (bf16[256,512]{1,0:T(8,128)(2,1)S(1)}, bf16[256,512]{1,0:T(8,128)(2,1)S(1)}, u32[]{:S(2)}, u32[]{:S(2)}) collective-permute-start(bf16[256,512]{1,0:T(8,128)(2,1)S(1)} %collective-permute-done.11.refs_7_), channel_id=1, source_target_pairs={{0,2},{1,3},{4,0},{5,1},{8,4},{9,5},{12,8},{13,9},{14,12},{15,13},... | collective-permute-start | bytes 786440 | tf_op jit(solution)/shard_map/ppermute | solution.py:192
  28.0 8.8 %collective-permute-start.3 = (bf16[272,128]{1,0:T(8,128)(2,1)S(1)}, bf16[272,128]{1,0:T(8,128)(2,1)S(1)}, u32[]{:S(2)}, u32[]{:S(2)}) collective-permute-start(bf16[272,128]{1,0:T(8,128)(2,1)S(1)} %fusion.1), channel_id=1, source_target_pairs={{0,8},{1,9},{2,10},{3,11},{4,12},{5,13},{6,14},{7,15},{8,0},{9,1},... | collective-permute-start | bytes 208904 | tf_op jit(solution)/shard_map/ppermute | solution.py:195
  30.7 10.4 %collective-permute-start.5 = (bf16[256,512]{1,0:T(8,128)(2,1)S(1)}, bf16[256,512]{1,0:T(8,128)(2,1)S(1)}, u32[]{:S(2)}, u32[]{:S(2)}) collective-permute-start(bf16[256,512]{1,0:T(8,128)(2,1)S(1)} %copy-done.4), channel_id=1, source_target_pairs={{0,1},{1,0},{2,3},{3,2},{4,5},{5,4},{6,7},{7,6},{8,9},{9,8},{10,11... | collective-permute-start | bytes 786440 | tf_op jit(solution)/shard_map/ppermute | solution.py:195
  34.5 8.0 %collective-permute-start.8 = (bf16[256,512]{1,0:T(8,128)(2,1)S(1)}, bf16[256,512]{1,0:T(8,128)(2,1)S(1)}, u32[]{:S(2)}, u32[]{:S(2)}) collective-permute-start(bf16[256,512]{1,0:T(8,128)(2,1)S(1)} %collective-permute-done.6.refs_2_), channel_id=1, source_target_pairs={{0,1},{1,0},{2,3},{3,2},{4,5},{5,4},{6,7},{7,6},{8,9},{9,8},{10,11... | collective-permute-start | bytes 786440 | tf_op jit(solution)/shard_map/ppermute | solution.py:195
  35.0 15.7 %copy-start.1 = (bf16[256,512]{1,0:T(8,128)(2,1)}, bf16[256,512]{1,0:T(8,128)(2,1)S(1)}, u32[]{:S(2)}) copy-start(bf16[256,512]{1,0:T(8,128)(2,1)S(1)} %collective-permute-done.14.refs_10_) | copy-start | bytes 786436
  35.1 8.0 %collective-permute-start.9 = (bf16[256,512]{1,0:T(8,128)(2,1)S(1)}, bf16[256,512]{1,0:T(8,128)(2,1)S(1)}, u32[]{:S(2)}, u32[]{:S(2)}) collective-permute-start(bf16[256,512]{1,0:T(8,128)(2,1)S(1)} %collective-permute-done.7.refs_3_), channel_id=1, source_target_pairs={{0,1},{1,0},{2,3},{3,2},{4,5},{5,4},{6,7},{7,6},{8,9},{9,8},{10,11... | collective-permute-start | bytes 786440 | tf_op jit(solution)/shard_map/ppermute | solution.py:195
  35.2 15.5 %copy-start.2 = (bf16[256,512]{1,0:T(8,128)(2,1)}, bf16[256,512]{1,0:T(8,128)(2,1)S(1)}, u32[]{:S(2)}) copy-start(bf16[256,512]{1,0:T(8,128)(2,1)S(1)} %collective-permute-done.15.refs_11_) | copy-start | bytes 786436
  35.2 5.9 %collective-permute-start.18 = (bf16[128,512]{1,0:T(8,128)(2,1)S(1)}, bf16[128,512]{1,0:T(8,128)(2,1)S(1)}, u32[]{:S(2)}, u32[]{:S(2)}) collective-permute-start(bf16[128,512]{1,0:T(8,128)(2,1)S(1)} %slice.8), channel_id=1, source_target_pairs={{0,4},{1,5},{4,8},{5,9},{8,12},{9,13},{12,14},{13,15},{14,10},{15,... | collective-permute-start | bytes 393224 | tf_op jit(solution)/shard_map/ppermute | solution.py:192
  36.8 6.1 %collective-permute-start.19 = (bf16[128,512]{1,0:T(8,128)(2,1)S(1)}, bf16[128,512]{1,0:T(8,128)(2,1)S(1)}, u32[]{:S(2)}, u32[]{:S(2)}) collective-permute-start(bf16[128,512]{1,0:T(8,128)(2,1)S(1)} %slice.9), channel_id=1, source_target_pairs={{0,2},{1,3},{4,0},{5,1},{8,4},{9,5},{12,8},{13,9},{14,12},{15,13},... | collective-permute-start | bytes 393224 | tf_op jit(solution)/shard_map/ppermute | solution.py:192
  41.1 1.3 %collective-permute-start.4 = (bf16[272,128]{1,0:T(8,128)(2,1)S(1)}, bf16[272,128]{1,0:T(8,128)(2,1)S(1)}, u32[]{:S(2)}, u32[]{:S(2)}) collective-permute-start(bf16[272,128]{1,0:T(8,128)(2,1)S(1)} %get-tuple-element.17), channel_id=1, source_target_pairs={{0,1},{1,0},{2,3},{3,2},{4,5},{5,4},{6,7},{7,6},{8,9},{9,8},{10,11... | collective-permute-start | bytes 208904 | tf_op jit(solution)/shard_map/ppermute | solution.py:195
  41.1 9.6 %copy-start.9 = (bf16[256,512]{1,0:T(8,128)(2,1)}, bf16[256,512]{1,0:T(8,128)(2,1)S(1)}, u32[]{:S(2)}) copy-start(bf16[256,512]{1,0:T(8,128)(2,1)S(1)} %collective-permute-done.5.refs_1_) | copy-start | bytes 786436
  41.2 9.6 %collective-permute-start.12 = (bf16[256,512]{1,0:T(8,128)(2,1)S(1)}, bf16[256,512]{1,0:T(8,128)(2,1)S(1)}, u32[]{:S(2)}, u32[]{:S(2)}) collective-permute-start(bf16[256,512]{1,0:T(8,128)(2,1)S(1)} %collective-permute-done.10.refs_6_), channel_id=1, source_target_pairs={{0,1},{1,0},{2,3},{3,2},{4,5},{5,4},{6,7},{7,6},{8,9},{9,8},{10,11... | collective-permute-start | bytes 786440 | tf_op jit(solution)/shard_map/ppermute | solution.py:195
  42.4 8.4 %collective-permute-start.13 = (bf16[256,512]{1,0:T(8,128)(2,1)S(1)}, bf16[256,512]{1,0:T(8,128)(2,1)S(1)}, u32[]{:S(2)}, u32[]{:S(2)}) collective-permute-start(bf16[256,512]{1,0:T(8,128)(2,1)S(1)} %collective-permute-done.11.refs_7_), channel_id=1, source_target_pairs={{0,1},{1,0},{2,3},{3,2},{4,5},{5,4},{6,7},{7,6},{8,9},{9,8},{10,11... | collective-permute-start | bytes 786440 | tf_op jit(solution)/shard_map/ppermute | solution.py:195
  42.5 8.2 %copy-start.10 = (bf16[256,512]{1,0:T(8,128)(2,1)}, bf16[256,512]{1,0:T(8,128)(2,1)S(1)}, u32[]{:S(2)}) copy-start(bf16[256,512]{1,0:T(8,128)(2,1)S(1)} %collective-permute-done.8.refs_4_) | copy-start | bytes 786436
  42.5 8.2 %collective-permute-start.16 = (bf16[256,512]{1,0:T(8,128)(2,1)S(1)}, bf16[256,512]{1,0:T(8,128)(2,1)S(1)}, u32[]{:S(2)}, u32[]{:S(2)}) collective-permute-start(bf16[256,512]{1,0:T(8,128)(2,1)S(1)} %collective-permute-done.14.refs_10_), channel_id=1, source_target_pairs={{0,1},{1,0},{2,3},{3,2},{4,5},{5,4},{6,7},{7,6},{8,9},{9,8},{10,11... | collective-permute-start | bytes 786440 | tf_op jit(solution)/shard_map/ppermute | solution.py:195
  42.9 7.9 %collective-permute-start.17 = (bf16[256,512]{1,0:T(8,128)(2,1)S(1)}, bf16[256,512]{1,0:T(8,128)(2,1)S(1)}, u32[]{:S(2)}, u32[]{:S(2)}) collective-permute-start(bf16[256,512]{1,0:T(8,128)(2,1)S(1)} %collective-permute-done.15.refs_11_), channel_id=1, source_target_pairs={{0,1},{1,0},{2,3},{3,2},{4,5},{5,4},{6,7},{7,6},{8,9},{9,8},{10,11... | collective-permute-start | bytes 786440 | tf_op jit(solution)/shard_map/ppermute | solution.py:195
  43.1 13.9 %copy-start.3 = (bf16[256,512]{1,0:T(8,128)(2,1)}, bf16[256,512]{1,0:T(8,128)(2,1)S(1)}, u32[]{:S(2)}) copy-start(bf16[256,512]{1,0:T(8,128)(2,1)S(1)} %constant_dynamic-update-slice_fusion.refs_0_) | copy-start | bytes 786436
  43.1 7.7 %copy-start.11 = (bf16[256,512]{1,0:T(8,128)(2,1)}, bf16[256,512]{1,0:T(8,128)(2,1)S(1)}, u32[]{:S(2)}) copy-start(bf16[256,512]{1,0:T(8,128)(2,1)S(1)} %collective-permute-done.9.refs_5_) | copy-start | bytes 786436
  43.1 13.9 %collective-permute-start.20 = (bf16[256,512]{1,0:T(8,128)(2,1)S(1)}, bf16[256,512]{1,0:T(8,128)(2,1)S(1)}, u32[]{:S(2)}, u32[]{:S(2)}) collective-permute-start(bf16[256,512]{1,0:T(8,128)(2,1)S(1)} %constant_dynamic-update-slice_fusion.refs_0_), channel_id=1, source_target_pairs={{0,1},{1,0},{2,3},{3,2},{4,5},{5,4},{6,7},{7,6},{8,9},{9,8},{10,11... | collective-permute-start | bytes 786440 | tf_op jit(solution)/shard_map/ppermute | solution.py:195
  (7 other events, 15.0 us)

commit v2 on v1

v2 whole, which is shorter than its diff:
```python
import jax
import jax.numpy as jnp
from jax import lax
from jax.experimental import pallas as pl
from jax.experimental.pallas import tpu as pltpu
from jax.sharding import PartitionSpec as P

HEADS = 8
EPS = 1e-05
F32 = jnp.float32
BF16 = jnp.bfloat16
VMEM = pl.BlockSpec(memory_space=pltpu.VMEM)
SMEM = pl.BlockSpec(memory_space=pltpu.SMEM)
HBM = pl.BlockSpec(memory_space=pltpu.HBM)


def dot(a, b):
    return jnp.dot(a, b, preferred_element_type=F32)


def split(value):
    high = value.astype(BF16)
    return high, (value - high.astype(F32)).astype(BF16)


def layer_norm(values, gain):
    mean = jnp.mean(values, axis=-1, keepdims=True)
    centered = values - mean
    var = jnp.mean(centered * centered, axis=-1, keepdims=True)
    return (centered * lax.rsqrt(var + EPS) * gain).astype(BF16)


def call(body, outs, specs, args, scratch=(), limit=None):
    held = sum(a.size * a.dtype.itemsize for a in (*args, *jax.tree.leaves(outs)))
    limit = limit or held // 2**20 + 7
    return pl.pallas_call(
        body,
        out_shape=outs,
        in_specs=specs,
        out_specs=jax.tree.map(lambda _: VMEM, outs),
        scratch_shapes=scratch,
        compiler_params=pltpu.CompilerParams(vmem_limit_bytes=limit * 2**20),
        cost_estimate=pl.CostEstimate(flops=1, bytes_accessed=1, transcendentals=0),
    )(*args)


def after(values, *others):
    any_space = pl.BlockSpec(memory_space=pl.ANY)
    return pl.pallas_call(
        lambda *refs: None,
        out_shape=[sds(v.shape, v.dtype) for v in values],
        in_specs=[any_space] * (len(values) + len(others)),
        out_specs=[any_space] * len(values),
        input_output_aliases={i: i for i in range(len(values))},
        compiler_params=pltpu.CompilerParams(vmem_limit_bytes=2**20),
        cost_estimate=pl.CostEstimate(flops=1, bytes_accessed=1, transcendentals=0),
    )(*values, *others)


def sds(shape, dtype):
    return jax.ShapeDtypeStruct(shape, dtype)


def pair_ones(rows, lanes):
    top = lax.broadcasted_iota(jnp.int32, (rows, lanes), 0) < rows // 2
    left = lax.broadcasted_iota(jnp.int32, (rows, lanes), 1) < lanes // 2
    return jnp.where(top == left, 1.0, 0.0)


def pair_omega(omega):
    zero = jnp.zeros_like(omega)
    return jnp.concatenate(
        [jnp.concatenate([omega, zero], axis=1), jnp.concatenate([zero, omega], axis=1)], axis=0
    )


class Fetch:
    def __init__(self, source, target, sems, pieces):
        rows = source.shape[0] // pieces
        self.copies = [
            pltpu.make_async_copy(
                source.at[pl.ds(i * rows, rows)], target.at[pl.ds(i * rows, rows)], sems.at[i]
            )
            for i in range(pieces)
        ]
        for copy in self.copies:
            copy.start()

    def wait(self):
        for copy in self.copies:
            copy.wait()


def buffers(*fetches):
    return [pltpu.VMEM(a.shape, a.dtype) for a, _ in fetches] + [
        pltpu.SemaphoreType.DMA((pieces,)) for _, pieces in fetches
    ]


PIECES = 4
EXTRA = 56


def message_kernel(
    core_ref,
    x_hbm,
    sibling_hbm,
    gain_hbm,
    w_hbm,
    normed_ref,
    msg_ref,
    x_ref,
    sibling_ref,
    gain_ref,
    w_ref,
    x_sem,
    sibling_sem,
    gain_sem,
    w_sem,
):
    nodes, width = x_hbm.shape
    core = core_ref[0]
    half = pl.ds(pl.multiple_of(core * (width // 2), width // 2), width // 2)
    x_copy = Fetch(x_hbm, x_ref, x_sem, PIECES)
    sibling_copy = Fetch(sibling_hbm, sibling_ref, sibling_sem, PIECES)
    gain_copy = Fetch(gain_hbm, gain_ref, gain_sem, 1)
    w_copy = Fetch(w_hbm.at[:, half], w_ref, w_sem, PIECES)
    gain_copy.wait()
    gain = gain_ref[...]
    mine = pl.ds(pl.multiple_of(core * nodes, nodes), nodes)
    theirs = pl.ds(pl.multiple_of((1 - core) * nodes, nodes), nodes)
    x_copy.wait()
    normed = layer_norm(x_ref[...].astype(F32), gain)
    normed_ref[mine, :] = normed
    w_copy.wait()
    msg_ref[mine, :] = dot(normed, w_ref[...]).astype(BF16)
    sibling_copy.wait()
    normed = layer_norm(sibling_ref[...].astype(F32), gain)
    normed_ref[theirs, :] = normed
    msg_ref[theirs, :] = dot(normed, w_ref[...]).astype(BF16)


def kv_kernel(core_ref, normed_ref, wk_ref, wv_ref, omega_ref, sums_ref):
    width = normed_ref.shape[1]
    head = width // HEADS
    feat = omega_ref.shape[1]
    half = HEADS // 4
    cols = pl.ds(pl.multiple_of(core_ref[0] * (width // 2), width // 2), width // 2)
    normed = normed_ref[...]
    keys = dot(normed, wk_ref[:, cols]) * (head ** (-0.25))
    values = dot(normed, wv_ref[:, cols])
    high, low = split(pair_omega(omega_ref[...]))
    ones = (-0.5 * pair_ones(2 * head, 2 * feat)).astype(BF16)
    first = jnp.concatenate([high, high], axis=0)
    second = jnp.concatenate([low, ones, ones], axis=0)
    left = lax.broadcasted_iota(jnp.int32, (feat, 2 * head), 1) < head
    for pair in range(half):
        k_pair = keys[:, pair * 2 * head : (pair + 1) * 2 * head]
        k_high, k_low = split(k_pair)
        s_high, s_low = split(k_pair * k_pair)
        logits = dot(jnp.concatenate([k_high, k_low], axis=1), first) + dot(
            jnp.concatenate([k_high, s_high, s_low], axis=1), second
        )
        kfeat = jnp.exp(logits)
        total = jnp.sum(kfeat, axis=0, keepdims=True)
        base = half * feat + 2 * pair
        sums_ref[base : base + 1, :] = total[:, :feat]
        sums_ref[base + 1 : base + 2, :] = total[:, feat:]
        f_high, f_low = split(kfeat)
        v_high, v_low = split(values[:, pair * 2 * head : (pair + 1) * 2 * head])
        dims = (((0,), (0,)), ((), ()))
        product = lax.dot_general(f_high, v_high, dims, preferred_element_type=F32)
        product += lax.dot_general(f_low, v_high, dims, preferred_element_type=F32)
        product += lax.dot_general(f_high, v_low, dims, preferred_element_type=F32)
        sums_ref[pair * feat : (pair + 1) * feat, :] = jnp.where(
            left, product[:feat], product[feat:]
        )
    used = half * feat + 2 * half
    sums_ref[used:, :] = jnp.zeros((sums_ref.shape[0] - used, feat), F32)


def query_kernel(core_ref, normed_ref, wq_ref, wg_ref, omega_ref, qf_ref, gate_ref):
    nodes = qf_ref.shape[0]
    normed = normed_ref[pl.ds(pl.multiple_of(core_ref[0] * nodes, nodes), nodes), :]
    width = normed.shape[1]
    head = width // HEADS
    feat = omega_ref.shape[1]
    query = dot(normed, wq_ref[...]) * (head ** (-0.25))
    high, low = split(pair_omega(omega_ref[...]))
    first = jnp.concatenate([high, high], axis=0)
    for pair in range(HEADS // 2):
        q_high, q_low = split(query[:, pair * 2 * head : (pair + 1) * 2 * head])
        logits = dot(jnp.concatenate([q_high, q_low], axis=1), first) + dot(q_high, low)
        qf_ref[:, pair * 2 * feat : (pair + 1) * 2 * feat] = jnp.exp(logits).astype(BF16)
    gate_ref[...] = jax.nn.sigmoid(dot(normed, wg_ref[...]))


def place_kernel(rows_ref, cols_ref, count_ref, tiles_ref, before_ref, dense_ref):
    del before_ref
    dense_ref[...] = jnp.zeros_like(dense_ref)

    def body(slot, carry):
        dense_ref[cols_ref[slot], rows_ref[slot]] = tiles_ref[slot]
        return carry

    lax.fori_loop(0, count_ref[0], body, 0)


def attend_kernel(core_ref, x_ref, qf_ref, gate_ref, own_ref, swapped_ref, wo_ref, mixed_ref):
    feat = own_ref.shape[1]
    width = x_ref.shape[1]
    head = width // HEADS
    half = HEADS // 4
    own = own_ref[...]
    swapped = swapped_ref[...].astype(F32)
    first_core = core_ref[0] == 0
    parts = [jnp.where(first_core, own, swapped), jnp.where(first_core, swapped, own)]
    left = lax.broadcasted_iota(jnp.int32, (feat, 2 * head), 1) < head
    ones = pair_ones(2 * feat, 2 * head).astype(BF16)
    joined = []
    for pair in range(HEADS // 2):
        part = parts[pair // half]
        place = pair % half
        block = part[place * feat : (place + 1) * feat]
        block = jnp.concatenate([jnp.where(left, block, 0.0), jnp.where(left, 0.0, block)], axis=0)
        base = half * feat + 2 * place
        ksum = jnp.concatenate([part[base : base + 1], part[base + 1 : base + 2]], axis=1)
        q_pair = qf_ref[:, pair * 2 * feat : (pair + 1) * 2 * feat]
        numer = dot(q_pair, block.astype(BF16))
        d_high, d_low = split(q_pair.astype(F32) * ksum)
        denom = dot(d_high, ones) + dot(d_low, ones)
        joined.append(numer / denom)
    attn = jnp.concatenate(joined, axis=1)
    gated = (attn * gate_ref[...]).astype(BF16)
    mixed_ref[...] = x_ref[...].astype(F32) + dot(gated, wo_ref[...])


def product(dense_ref, column, chunk):
    rows, tile = dense_ref.shape[1:3]
    weights = [
        jnp.concatenate(
            [dense_ref[column + col, row] for col in range(chunk.shape[0] // tile)], axis=1
        )
        for row in range(rows)
    ]
    return dot(jnp.concatenate(weights, axis=0), chunk)


def solution(mesh):
    size = mesh.shape["blk"]
    chips = size // 2
    order = chip_order(mesh, size)

    def step(value, shift):
        pairs = [
            (order[p] * 2 + c, order[(p + shift) % chips] * 2 + c)
            for p in range(chips)
            for c in range(2)
        ]
        return lax.ppermute(value, "blk", pairs)

    def flip(value, bit):
        return lax.ppermute(value, "blk", [(i, i ^ bit) for i in range(size)])

    def on_device(
        features,
        tiles,
        block_rows,
        block_cols,
        block_count,
        ln_gain,
        w_msg,
        w_query,
        w_key,
        w_value,
        w_gate,
        w_out,
        omega,
        ln2_gain,
        w_up,
        w_down,
    ):
        nodes, width = features.shape
        tile = tiles.shape[1]
        feat = omega.shape[1]
        head = width // HEADS
        row_blocks = nodes // tile
        me = lax.axis_index("blk")
        core = (me % 2).reshape(1)
        half = width // 2
        normed, message = call(
            message_kernel,
            (sds((2 * nodes, width), BF16), sds((2 * nodes, half), BF16)),
            [SMEM] + [HBM] * 4,
            (core, features, flip(features, 1), ln_gain.reshape(1, width), w_msg),
            buffers(
                (features, PIECES),
                (features, PIECES),
                (sds((1, width), F32), 1),
                (sds((width, half), BF16), PIECES),
            ),
            EXTRA,
        )

        first_ahead, first_back = step(message, 1), step(message, -1)

        rows = HEADS // 4 * feat + 16
        own = call(
            kv_kernel,
            sds((rows, feat), F32),
            [SMEM] + [VMEM] * 4,
            (core, normed, w_key, w_value, omega),
        )
        first_ahead, first_back = after([first_ahead, first_back], own)
        if chips & (chips - 1) == 0:
            bit = size // 2
            while bit > 1:
                own = own + flip(own.astype(BF16), bit).astype(F32)
                bit //= 2
        else:
            own = lax.psum(
                own, "blk", axis_index_groups=[list(range(c, size, 2)) for c in range(2)]
            )
        swapped = flip(own.astype(BF16), 1)

        qfeat, gate = call(
            query_kernel,
            (sds((nodes, HEADS * feat), BF16), sds((nodes, width), F32)),
            [SMEM] + [VMEM] * 4,
            (core, normed, w_query, w_gate, omega),
        )
        dense = call(
            place_kernel,
            sds((size * row_blocks, row_blocks, tile, tile), BF16),
            [SMEM] * 3 + [VMEM, pl.BlockSpec(memory_space=pl.ANY)],
            (block_rows, block_cols, block_count, tiles, first_ahead),
        )
        sibling = flip(dense, 1)
        mixed = call(
            attend_kernel,
            sds((nodes, width), F32),
            [SMEM] + [VMEM] * 6,
            (core, features, qfeat, gate, own, swapped, w_out),
        )

        full = (chips - 1) // 2
        shifts = [0] + [sign * k for k in range(1, full + 1) for sign in (1, -1)]
        if chips % 2 == 0:
            shifts += [chips // 2]
        home = {chip: p for p, chip in enumerate(order)}
        table = jnp.asarray(
            [order[(home[chip] - shift) % chips] for chip in range(chips) for shift in shifts],
            jnp.int32,
        )

        def accumulate(totals, first, chunks):
            totals = list(totals)

            def body(me_ref, table_ref, mine_ref, sibling_ref, *refs):
                outs = refs[-2:]
                chunk_refs = refs[len(totals) : -2]
                for dense_ref, total, out in zip((mine_ref, sibling_ref), refs, outs):
                    value = total[...] if totals else None
                    place, rows_seen = first, 0
                    for chunk_ref in chunk_refs:
                        chip = table_ref[(me_ref[0] // 2) * chips + place]
                        column = chip * (2 * nodes // tile) + rows_seen // tile
                        part = product(dense_ref, column, chunk_ref[...])
                        value = part if value is None else value + part
                        rows_seen += chunk_ref.shape[0]
                        if rows_seen == 2 * nodes:
                            place, rows_seen = place + 1, 0
                    out[...] = value

            return call(
                body,
                (sds((nodes, half), F32), sds((nodes, half), F32)),
                [SMEM] * 2 + [VMEM] * (2 + len(totals) + len(chunks)),
                (me.reshape(1), table, dense, sibling, *totals, *chunks),
            )

        ahead, back = first_ahead, first_back
        chunks = [message, ahead, back]
        totals, used = (), 0
        for k in range(2, full + 1):
            if k == 3:
                ahead, back = after([ahead, back], qfeat, dense)
                chunks[-2:] = [ahead, back]
            if k > 3:
                ready = 1 + 2 * (k - 2)
                totals = accumulate(totals, used, chunks[used:ready])
                used = ready
            ahead, back = step(ahead, 1), step(back, -1)
            chunks += [ahead, back]
        ready = 1 + 2 * (full - 1)
        totals = accumulate(totals, used, chunks[used:ready])
        used = ready
        ahead, back = after([ahead, back], totals[0])
        chunks[-2:] = [ahead, back]
        late = []
        if chips % 2 == 0:
            late = [step(ahead[:nodes], 1), step(back[nodes:], -1)]
            totals = accumulate(totals, used, chunks[used:])
            used = len(chunks)
        totals = accumulate(totals, used, late or chunks[used:])
        theirs = flip(totals[1], 1)

        def final_kernel(core_ref, mixed_ref, mine_ref, theirs_ref, gain_ref, up_ref, down_ref, out_ref):
            first_core = core_ref[0] == 0
            mine, theirs = mine_ref[...], theirs_ref[...]
            local = jnp.concatenate(
                [jnp.where(first_core, mine, theirs), jnp.where(first_core, theirs, mine)], axis=1
            )
            mixed = mixed_ref[...] + local
            second = layer_norm(mixed, gain_ref[...])
            inner = jnp.maximum(dot(second, up_ref[...]), 0.0).astype(BF16)
            out_ref[...] = (mixed + dot(inner, down_ref[...])).astype(BF16)

        return call(
            final_kernel,
            sds((nodes, width), BF16),
            [SMEM] + [VMEM] * 6,
            (core, mixed, totals[0], theirs, ln2_gain.reshape(1, width), w_up, w_down),
        )

    split_rows = P(("groups", "blk"))
    return jax.shard_map(
        on_device,
        mesh=mesh,
        in_specs=(split_rows,) * 5 + (P(),) * 11,
        out_specs=P(("groups", "blk"), None),
        check_vma=False,
    )


def chip_order(mesh, size):
    devices = mesh.devices.reshape(-1, size)[0]
    coords = [getattr(d, "coords", None) for d in devices[::2]]
    if any(c is None for c in coords) or len({c[1] for c in map(tuple, coords)}) != 2:
        return list(range(size // 2))
    low = min(c[1] for c in coords)
    up = sorted((i for i, c in enumerate(coords) if c[1] == low), key=lambda i: coords[i][2])
    down = sorted((i for i, c in enumerate(coords) if c[1] != low), key=lambda i: -coords[i][2])
    return up + down
```

time: 62.5 us -> 47.9 us (0.77)
  Pallas kernels: 24.1 us -> 12 us
  other arithmetic: 3.52 us -> 0.11 us
  starting transfers between devices: 18.2 us -> 15.9 us
  waiting for transfers between devices: 11.8 us -> 14 us
  local copies, waits for them, and re-layouts: 3.51 us -> 4.66 us
    pallas_call x7 -> x9, Pallas kernels: 24.1 us -> 12 us  [call(): pl.pallas_call(body, out_shape=outs, in_specs=specs, out_specs=jax.tree.m...]
    ppermute x13 -> x7, starting transfers between devices: 9.07 us -> 5.6 us  [flip(): return lax.ppermute(value, 'blk', [(i, i ^ bit) for i in range(size)])]
    convert_element_type x3, other arithmetic: 2.81 us -> 0.07 us  [on_device(): own = own + flip(own.astype(BF16), bit).astype(F32)]
    unnamed x37 -> x38, local copies, waits for them, and re-layouts: 2.25 us -> 4.64 us
    ppermute x13 -> x7, waiting for transfers between devices: 1.13 us -> 2.86 us  [flip(): return lax.ppermute(value, 'blk', [(i, i ^ bit) for i in range(size)])]
    squeeze x1 -> x0, local copies, waits for them, and re-layouts: 1.23 us -> none  [on_device(): source = jnp.asarray(table, jnp.int32)[me]]
    ppermute x8, starting transfers between devices: 9.09 us -> 10.3 us  [step(): return lax.ppermute(value, 'blk', pairs)]
    convert_element_type x1, other arithmetic: 0.71 us -> 0.04 us  [on_device(): swapped = flip(own.astype(BF16), 1)]
  transfers between devices with their start and end apart: 21 -> 15, of which waited for: 5 -> 9; matrix products, arithmetic and copies ran while one was open for 8% -> 0% of each run, Pallas kernels for 22% -> 14%
where the time goes in v2:
time: 47.9 us; the launch traced here: 47.7 us
  starting transfers between devices  15.9 us (33%)
  waiting for transfers between devices  14 us (29%)
  Pallas kernels  12 us (25%)
  local copies, waits for them, and re-layouts  4.66 us (10%)
  between operations  0.93 us (2%)
    pallas_call x9, Pallas kernels, call(): pl.pallas_call(body, out_shape=outs, in_specs=specs, out_specs=jax.tree.m...  12 us
    ppermute x8, waiting for transfers between devices, step(): return lax.ppermute(value, 'blk', pairs)  11.2 us
    ppermute x8, starting transfers between devices, step(): return lax.ppermute(value, 'blk', pairs)  10.3 us
    ppermute x7, starting transfers between devices, flip(): return lax.ppermute(value, 'blk', [(i, i ^ bit) for i in range(size)])  5.6 us
    unnamed x38, local copies, waits for them, and re-layouts  4.64 us
    ppermute x7, waiting for transfers between devices, flip(): return lax.ppermute(value, 'blk', [(i, i ^ bit) for i in range(size)])  2.86 us
  transfers between devices with their start and end apart: 15, of which 9 were waited for; matrix products, arithmetic and copies ran while one was open for 0% of the time, Pallas kernels for 14%

profile of v2, /device:TPU:0, one launch (start us, length us, event | category | flops | bytes accessed | tf_op | source)
XLA Modules:
  0.0 47.7 jit_solution(15686294600165320999)
XLA Ops:
  0.0 0.5 collective-permute-start
  0.5 1.4 %collective-permute-done.sibling_hbm = bf16[256,512]{1,0:T(8,128)(2,1)S(1)} collective-permute-done((bf16[256,512]{1,0:T(8,128)(2,1)}, bf16[256,512]{1,0:T(8,128)(2,1)S(1)}, u32[]{:S(2)}, u32[]{:S(2)}) %collective-permute-start) | collective-permute-done | bytes 262176 | tf_op jit(solution)/shard_map/ppermute | solution.py:263
  1.8 0.7 %copy-done.18 = bf16[256,512]{1,0:T(8,128)(2,1)} copy-done((bf16[256,512]{1,0:T(8,128)(2,1)}, bf16[256,512]{1,0:T(8,128)(2,1)S(1)}, u32[]{:S(2)}) %copy-start.18) | copy-done | bytes 262168
  2.5 3.0 %shard_map.163 = (bf16[512,512]{1,0:T(8,128)(2,1)}, bf16[512,256]{1,0:T(8,128)(2,1)}) custom-call(s32[1]{0:T(128)} %bitcast.core_ref, bf16[256,512]{1,0:T(8,128)(2,1)} %x_ref.1, bf16[256,512]{1,0:T(8,128)(2,1)} %copy-done.18, f32[1,512]{1,0:T(1,128)} %bitcast.5, bf16[512,512]{1,0:T(8,128)(2,1)} %w_hbm.1), custom_call_target="tpu_custom_call" | custom-call | flops 1 | bytes 1 | tf_op jit(solution)/shard_map/pallas_call | solution.py:36
  5.5 2.9 %collective-permute-start.6 = (bf16[512,256]{1,0:T(8,128)(2,1)}, bf16[512,256]{1,0:T(8,128)(2,1)S(1)}, u32[]{:S(2)}, u32[]{:S(2)}) collective-permute-start(bf16[512,256]{1,0:T(8,128)(2,1)} %get-tuple-element.24.refs_0_), channel_id=1, source_target_pairs={{0,2},{1,3},{4,0},{5,1},{8,4},{9,5},{12,8},{13,9},{14,12},{15,13},... | collective-permute-start | bytes 786440 | tf_op jit(solution)/shard_map/ppermute | solution.py:260
  9.2 1.0 %copy-done = bf16[512,512]{1,0:T(8,128)(2,1)S(1)} copy-done((bf16[512,512]{1,0:T(8,128)(2,1)S(1)}, bf16[512,512]{1,0:T(8,128)(2,1)}, u32[]{:S(2)}) %copy-start) | copy-done | bytes 524312
  10.3 1.0 %copy-done.6 = bf16[512,512]{1,0:T(8,128)(2,1)S(1)} copy-done((bf16[512,512]{1,0:T(8,128)(2,1)S(1)}, bf16[512,512]{1,0:T(8,128)(2,1)}, u32[]{:S(2)}) %copy-start.6) | copy-done | bytes 524312
  11.3 1.0 %copy-done.7 = bf16[512,512]{1,0:T(8,128)(2,1)S(1)} copy-done((bf16[512,512]{1,0:T(8,128)(2,1)S(1)}, bf16[512,512]{1,0:T(8,128)(2,1)}, u32[]{:S(2)}) %copy-start.7) | copy-done | bytes 524312
  12.3 0.8 %copy-done.12 = f32[64,128]{1,0:T(8,128)S(1)} copy-done((f32[64,128]{1,0:T(8,128)S(1)}, f32[64,128]{1,0:T(8,128)}, u32[]{:S(2)}) %copy-start.12) | copy-done | bytes 32792
  13.1 1.8 %shard_map.165.refs_2_ = f32[272,128]{1,0:T(8,128)S(1)} custom-call(s32[1]{0:T(128)} %bitcast.core_ref, bf16[512,512]{1,0:T(8,128)(2,1)S(1)} %copy-done, bf16[512,512]{1,0:T(8,128)(2,1)S(1)} %copy-done.6, bf16[512,512]{1,0:T(8,128)(2,1)S(1)} %copy-done.7, f32[64,128]{1,0:T(8,128)S(1)} %copy-done.12), custom_call_target="tpu_custom_call" | custom-call | flops 1 | bytes 1 | tf_op jit(solution)/shard_map/pallas_call | solution.py:36
  14.9 0.5 collective-permute-done.6.refs_1_
  15.3 1.4 %collective-permute-done.5.refs_0_ = bf16[512,256]{1,0:T(8,128)(2,1)S(1)} collective-permute-done((bf16[512,256]{1,0:T(8,128)(2,1)}, bf16[512,256]{1,0:T(8,128)(2,1)S(1)}, u32[]{:S(2)}, u32[]{:S(2)}) %collective-permute-start.5) | collective-permute-done | bytes 262176 | tf_op jit(solution)/shard_map/ppermute | solution.py:260
  16.8 1.0 %shard_map.168.refs_3_.mine_ref = bf16[32,2,128,128]{3,2,1,0:T(8,128)(2,1)S(1)} custom-call(s32[48]{0:T(128)S(1)} %copy-done.16, s32[48]{0:T(128)S(1)} %copy-done.17, s32[1]{0:T(128)S(6)} %copy.30.count_ref, bf16[48,128,128]{2,1,0:T(8,128)(2,1)S(1)} %copy-done.2, bf16[512,256]{1,0:T(8,128)(2,1)S(1)} %get-tuple-element.25.before_ref.refs_1_), custom_call_target="tpu_custom_call" | custom-call | flops 1 | bytes 1 | tf_op jit(solution)/shard_map/pallas_call | solution.py:36
  17.8 1.7 %collective-permute-start.9 = (bf16[512,256]{1,0:T(8,128)(2,1)S(1)}, bf16[512,256]{1,0:T(8,128)(2,1)S(1)}, u32[]{:S(2)}, u32[]{:S(2)}) collective-permute-start(bf16[512,256]{1,0:T(8,128)(2,1)S(1)} %get-tuple-element.26.refs_2_), channel_id=1, source_target_pairs={{0,2},{1,3},{4,0},{5,1},{8,4},{9,5},{12,8},{13,9},{14,12},{15,13},... | collective-permute-start | bytes 786440 | tf_op jit(solution)/shard_map/ppermute | solution.py:260
  19.5 0.4 collective-permute-start.8
  19.9 1.5 %collective-permute-start.1 = (bf16[272,128]{1,0:T(8,128)(2,1)S(1)}, bf16[272,128]{1,0:T(8,128)(2,1)S(1)}, u32[]{:S(2)}, u32[]{:S(2)}) collective-permute-start(bf16[272,128]{1,0:T(8,128)(2,1)S(1)} %convert_element_type.21), channel_id=1, source_target_pairs={{0,8},{1,9},{2,10},{3,11},{4,12},{5,13},{6,14},{7,15},{8,0},{9,1},... | collective-permute-start | bytes 208904 | tf_op jit(solution)/shard_map/ppermute | solution.py:263
  21.5 0.8 %shard_map.164 = (bf16[256,1024]{1,0:T(8,128)(2,1)S(1)}, f32[256,512]{1,0:T(8,128)S(1)}) custom-call(s32[1]{0:T(128)} %bitcast.core_ref, bf16[512,512]{1,0:T(8,128)(2,1)S(1)} %copy-done.1, bf16[512,512]{1,0:T(8,128)(2,1)S(1)} %copy-done.8, bf16[512,512]{1,0:T(8,128)(2,1)S(1)} %copy-done.9, f32[64,128]{1,0:T(8,128)S(1)} %copy-done.13), custom_call_target="tpu_custom_call" | custom-call | flops 1 | bytes 1 | tf_op jit(solution)/shard_map/pallas_call | solution.py:36
  22.3 5.0 %collective-permute-done.9.refs_1_ = bf16[512,256]{1,0:T(8,128)(2,1)S(1)} collective-permute-done((bf16[512,256]{1,0:T(8,128)(2,1)S(1)}, bf16[512,256]{1,0:T(8,128)(2,1)S(1)}, u32[]{:S(2)}, u32[]{:S(2)}) %collective-permute-start.9) | collective-permute-done | bytes 262176 | tf_op jit(solution)/shard_map/ppermute | solution.py:260
  27.3 0.5 %collective-permute-done.8.refs_0_ = bf16[512,256]{1,0:T(8,128)(2,1)S(1)} collective-permute-done((bf16[512,256]{1,0:T(8,128)(2,1)S(1)}, bf16[512,256]{1,0:T(8,128)(2,1)S(1)}, u32[]{:S(2)}, u32[]{:S(2)}) %collective-permute-start.8) | collective-permute-done | bytes 262176 | tf_op jit(solution)/shard_map/ppermute | solution.py:260
  27.9 1.2 %collective-permute-start.10 = (bf16[512,256]{1,0:T(8,128)(2,1)S(1)}, bf16[512,256]{1,0:T(8,128)(2,1)S(1)}, u32[]{:S(2)}, u32[]{:S(2)}) collective-permute-start(bf16[512,256]{1,0:T(8,128)(2,1)S(1)} %get-tuple-element.27.refs_3_), channel_id=1, source_target_pairs={{0,4},{1,5},{4,8},{5,9},{8,12},{9,13},{12,14},{13,15},{14,10},{15,... | collective-permute-start | bytes 786440 | tf_op jit(solution)/shard_map/ppermute | solution.py:260
  29.0 0.9 %collective-permute-start.11 = (bf16[512,256]{1,0:T(8,128)(2,1)S(1)}, bf16[512,256]{1,0:T(8,128)(2,1)S(1)}, u32[]{:S(2)}, u32[]{:S(2)}) collective-permute-start(bf16[512,256]{1,0:T(8,128)(2,1)S(1)} %get-tuple-element.28.refs_4_), channel_id=1, source_target_pairs={{0,2},{1,3},{4,0},{5,1},{8,4},{9,5},{12,8},{13,9},{14,12},{15,13},... | collective-permute-start | bytes 786440 | tf_op jit(solution)/shard_map/ppermute | solution.py:260
  29.9 1.2 %collective-permute-start.2 = (bf16[272,128]{1,0:T(8,128)(2,1)S(1)}, bf16[272,128]{1,0:T(8,128)(2,1)S(1)}, u32[]{:S(2)}, u32[]{:S(2)}) collective-permute-start(bf16[272,128]{1,0:T(8,128)(2,1)S(1)} %fusion), channel_id=1, source_target_pairs={{0,4},{1,5},{2,6},{3,7},{4,0},{5,1},{6,2},{7,3},{8,12},{9,13},{10,... | collective-permute-start | bytes 208904 | tf_op jit(solution)/shard_map/ppermute | solution.py:263
  31.2 1.4 %shard_map.170 = (f32[256,256]{1,0:T(8,128)S(1)}, f32[256,256]{1,0:T(8,128)S(1)}) custom-call(s32[1]{0:T(128)} %bitcast.2.me_ref, s32[64]{0:T(128)S(1)} %copy-done.14, bf16[32,2,128,128]{3,2,1,0:T(8,128)(2,1)S(1)} %shard_map.168.refs_3_.mine_ref, bf16[32,2,128,128]{3,2,1,0:T(8,128)(2,1)S(1)} %collective-permute-done.7.sibling_ref, ...), custom_call_target="tpu_custom_call" | custom-call | flops 1 | bytes 1 | tf_op jit(solution)/shard_map/pallas_call | solution.py:36
  32.5 2.9 %collective-permute-done.10.refs_0_ = bf16[512,256]{1,0:T(8,128)(2,1)S(1)} collective-permute-done((bf16[512,256]{1,0:T(8,128)(2,1)S(1)}, bf16[512,256]{1,0:T(8,128)(2,1)S(1)}, u32[]{:S(2)}, u32[]{:S(2)}) %collective-permute-start.10) | collective-permute-done | bytes 262176 | tf_op jit(solution)/shard_map/ppermute | solution.py:260
  35.4 0.9 %collective-permute-done.11.refs_1_ = bf16[512,256]{1,0:T(8,128)(2,1)S(1)} collective-permute-done((bf16[512,256]{1,0:T(8,128)(2,1)S(1)}, bf16[512,256]{1,0:T(8,128)(2,1)S(1)}, u32[]{:S(2)}, u32[]{:S(2)}) %collective-permute-start.11) | collective-permute-done | bytes 262176 | tf_op jit(solution)/shard_map/ppermute | solution.py:260
  36.7 2.8 %collective-permute-start.13 = (bf16[256,256]{1,0:T(8,128)(2,1)S(1)}, bf16[256,256]{1,0:T(8,128)(2,1)S(1)}, u32[]{:S(2)}, u32[]{:S(2)}) collective-permute-start(bf16[256,256]{1,0:T(8,128)(2,1)S(1)} %slice.7), channel_id=1, source_target_pairs={{0,2},{1,3},{4,0},{5,1},{8,4},{9,5},{12,8},{13,9},{14,12},{15,13},... | collective-permute-start | bytes 393224 | tf_op jit(solution)/shard_map/ppermute | solution.py:260
  39.5 2.0 %collective-permute-start.3 = (bf16[272,128]{1,0:T(8,128)(2,1)S(1)}, bf16[272,128]{1,0:T(8,128)(2,1)S(1)}, u32[]{:S(2)}, u32[]{:S(2)}) collective-permute-start(bf16[272,128]{1,0:T(8,128)(2,1)S(1)} %fusion.1), channel_id=1, source_target_pairs={{0,2},{1,3},{2,0},{3,1},{4,6},{5,7},{6,4},{7,5},{8,10},{9,11},{10,... | collective-permute-start | bytes 208904 | tf_op jit(solution)/shard_map/ppermute | solution.py:263
  41.5 1.0 %shard_map.172 = (f32[256,256]{1,0:T(8,128)S(1)}, f32[256,256]{1,0:T(8,128)S(1)}) custom-call(s32[1]{0:T(128)} %bitcast.2.me_ref, s32[64]{0:T(128)S(1)} %copy-done.14, bf16[32,2,128,128]{3,2,1,0:T(8,128)(2,1)S(1)} %shard_map.168.refs_3_.mine_ref, bf16[32,2,128,128]{3,2,1,0:T(8,128)(2,1)S(1)} %collective-permute-done.7.sibling_ref, ...), custom_call_target="tpu_custom_call" | custom-call | flops 1 | bytes 1 | tf_op jit(solution)/shard_map/pallas_call | solution.py:36
  42.6 0.8 %shard_map.173 = (f32[256,256]{1,0:T(8,128)S(1)}, f32[256,256]{1,0:T(8,128)S(1)}) custom-call(s32[1]{0:T(128)} %bitcast.2.me_ref, s32[64]{0:T(128)S(1)} %copy-done.14, bf16[32,2,128,128]{3,2,1,0:T(8,128)(2,1)S(1)} %shard_map.168.refs_3_.mine_ref, bf16[32,2,128,128]{3,2,1,0:T(8,128)(2,1)S(1)} %collective-permute-done.7.sibling_ref, ...), custom_call_target="tpu_custom_call" | custom-call | flops 1 | bytes 1 | tf_op jit(solution)/shard_map/pallas_call | solution.py:36
  44.1 1.1 %collective-permute-done.4.swapped_ref = bf16[272,128]{1,0:T(8,128)(2,1)S(1)} collective-permute-done((bf16[272,128]{1,0:T(8,128)(2,1)S(1)}, bf16[272,128]{1,0:T(8,128)(2,1)S(1)}, u32[]{:S(2)}, u32[]{:S(2)}) %collective-permute-start.4) | collective-permute-done | bytes 69664 | tf_op jit(solution)/shard_map/ppermute | solution.py:263
  45.3 0.7 %shard_map.166.mixed_ref = f32[256,512]{1,0:T(8,128)S(1)} custom-call(s32[1]{0:T(128)} %bitcast.core_ref, bf16[256,512]{1,0:T(8,128)(2,1)S(1)} %copy-done.5, bf16[256,1024]{1,0:T(8,128)(2,1)S(1)} %get-tuple-element.22.qf_ref.refs_2_, f32[256,512]{1,0:T(8,128)S(1)} %get-tuple-element.23.gate_ref, f32[272,128]{1,0:T(8,128)S(1)} %get-tuple-element.38.own_ref, ...), custom_call_target="tpu_custom_call" | custom-call | flops 1 | bytes 1 | tf_op jit(solution)/shard_map/pallas_call | solution.py:36
  46.0 1.6 %shard_map.174 = bf16[256,512]{1,0:T(8,128)(2,1)} custom-call(s32[1]{0:T(128)} %bitcast.core_ref, f32[256,512]{1,0:T(8,128)S(1)} %shard_map.166.mixed_ref, f32[256,256]{1,0:T(8,128)S(1)} %get-tuple-element.35.mine_ref, f32[256,256]{1,0:T(8,128)S(1)} %collective-permute-done.14.theirs_ref, f32[1,512]{1,0:T(1,128)S(1)} %bitcast.4, ...), custom_call_target="tpu_custom_call" | custom-call | flops 1 | bytes 1 | tf_op jit(solution)/shard_map/pallas_call | solution.py:36
  (54 shorter events, 1.4 us)
Async XLA Ops:
  0.0 16.7 %copy-start.17 = (s32[48]{0:T(128)S(1)}, s32[48]{0:T(128)}, u32[]{:S(2)}) copy-start(s32[48]{0:T(128)} %cols_ref.1) | copy-start | bytes 580
  0.0 16.7 %copy-start.16 = (s32[48]{0:T(128)S(1)}, s32[48]{0:T(128)}, u32[]{:S(2)}) copy-start(s32[48]{0:T(128)} %rows_ref.1) | copy-start | bytes 580
  0.0 1.8 %collective-permute-start = (bf16[256,512]{1,0:T(8,128)(2,1)}, bf16[256,512]{1,0:T(8,128)(2,1)S(1)}, u32[]{:S(2)}, u32[]{:S(2)}) collective-permute-start(bf16[256,512]{1,0:T(8,128)(2,1)} %x_ref.1), channel_id=1, source_target_pairs={{0,1},{1,0},{2,3},{3,2},{4,5},{5,4},{6,7},{7,6},{8,9},{9,8},{10,11... | collective-permute-start | bytes 786440 | tf_op jit(solution)/shard_map/ppermute | solution.py:263
  5.5 9.8 %collective-permute-start.6 = (bf16[512,256]{1,0:T(8,128)(2,1)}, bf16[512,256]{1,0:T(8,128)(2,1)S(1)}, u32[]{:S(2)}, u32[]{:S(2)}) collective-permute-start(bf16[512,256]{1,0:T(8,128)(2,1)} %get-tuple-element.24.refs_0_), channel_id=1, source_target_pairs={{0,2},{1,3},{4,0},{5,1},{8,4},{9,5},{12,8},{13,9},{14,12},{15,13},... | collective-permute-start | bytes 786440 | tf_op jit(solution)/shard_map/ppermute | solution.py:260
  8.4 8.3 %collective-permute-start.5 = (bf16[512,256]{1,0:T(8,128)(2,1)}, bf16[512,256]{1,0:T(8,128)(2,1)S(1)}, u32[]{:S(2)}, u32[]{:S(2)}) collective-permute-start(bf16[512,256]{1,0:T(8,128)(2,1)} %get-tuple-element.24.refs_0_), channel_id=1, source_target_pairs={{0,4},{1,5},{4,8},{5,9},{8,12},{9,13},{12,14},{13,15},{14,10},{15,... | collective-permute-start | bytes 786440 | tf_op jit(solution)/shard_map/ppermute | solution.py:260
  9.2 1.0 %copy-start = (bf16[512,512]{1,0:T(8,128)(2,1)S(1)}, bf16[512,512]{1,0:T(8,128)(2,1)}, u32[]{:S(2)}) copy-start(bf16[512,512]{1,0:T(8,128)(2,1)} %get-tuple-element.21.normed_ref) | copy-start | bytes 1572868
  10.3 1.0 %copy-start.6 = (bf16[512,512]{1,0:T(8,128)(2,1)S(1)}, bf16[512,512]{1,0:T(8,128)(2,1)}, u32[]{:S(2)}) copy-start(bf16[512,512]{1,0:T(8,128)(2,1)} %wk_ref.1) | copy-start | bytes 1572868
  11.3 1.0 %copy-start.7 = (bf16[512,512]{1,0:T(8,128)(2,1)S(1)}, bf16[512,512]{1,0:T(8,128)(2,1)}, u32[]{:S(2)}) copy-start(bf16[512,512]{1,0:T(8,128)(2,1)} %wv_ref.1) | copy-start | bytes 1572868
  13.1 3.7 %copy-start.2 = (bf16[48,128,128]{2,1,0:T(8,128)(2,1)S(1)}, bf16[48,128,128]{2,1,0:T(8,128)(2,1)}, u32[]{:S(2)}) copy-start(bf16[48,128,128]{2,1,0:T(8,128)(2,1)} %tiles_ref.1) | copy-start | bytes 4718596
  16.7 4.7 %copy-start.1 = (bf16[512,512]{1,0:T(8,128)(2,1)S(1)}, bf16[512,512]{1,0:T(8,128)(2,1)}, u32[]{:S(2)}) copy-start(bf16[512,512]{1,0:T(8,128)(2,1)} %get-tuple-element.21.normed_ref) | copy-start | bytes 1572868
  16.7 4.7 %copy-start.8 = (bf16[512,512]{1,0:T(8,128)(2,1)S(1)}, bf16[512,512]{1,0:T(8,128)(2,1)}, u32[]{:S(2)}) copy-start(bf16[512,512]{1,0:T(8,128)(2,1)} %wq_ref.1) | copy-start | bytes 1572868
  16.7 4.7 %copy-start.9 = (bf16[512,512]{1,0:T(8,128)(2,1)S(1)}, bf16[512,512]{1,0:T(8,128)(2,1)}, u32[]{:S(2)}) copy-start(bf16[512,512]{1,0:T(8,128)(2,1)} %wg_ref.1) | copy-start | bytes 1572868
  16.7 4.7 %copy-start.13 = (f32[64,128]{1,0:T(8,128)S(1)}, f32[64,128]{1,0:T(8,128)}, u32[]{:S(2)}) copy-start(f32[64,128]{1,0:T(8,128)} %omega_ref.3) | copy-start | bytes 98308
  17.8 13.4 %collective-permute-start.7 = (bf16[32,2,128,128]{3,2,1,0:T(8,128)(2,1)S(1)}, bf16[32,2,128,128]{3,2,1,0:T(8,128)(2,1)S(1)}, u32[]{:S(2)}, u32[]{:S(2)}) collective-permute-start(bf16[32,2,128,128]{3,2,1,0:T(8,128)(2,1)S(1)} %shard_map.168.refs_3_.mine_ref), channel_id=1, source_target_pairs={{0,1},{1,0},{2,3},{3,2},{4,5},{5,4},{6,7},{7,6},{8,9},{9,8},{10,11... | collective-permute-start | bytes 6291464 | tf_op jit(solution)/shard_map/ppermute | solution.py:263
  17.8 9.5 %collective-permute-start.9 = (bf16[512,256]{1,0:T(8,128)(2,1)S(1)}, bf16[512,256]{1,0:T(8,128)(2,1)S(1)}, u32[]{:S(2)}, u32[]{:S(2)}) collective-permute-start(bf16[512,256]{1,0:T(8,128)(2,1)S(1)} %get-tuple-element.26.refs_2_), channel_id=1, source_target_pairs={{0,2},{1,3},{4,0},{5,1},{8,4},{9,5},{12,8},{13,9},{14,12},{15,13},... | collective-permute-start | bytes 786440 | tf_op jit(solution)/shard_map/ppermute | solution.py:260
  19.5 8.4 %collective-permute-start.8 = (bf16[512,256]{1,0:T(8,128)(2,1)S(1)}, bf16[512,256]{1,0:T(8,128)(2,1)S(1)}, u32[]{:S(2)}, u32[]{:S(2)}) collective-permute-start(bf16[512,256]{1,0:T(8,128)(2,1)S(1)} %get-tuple-element.25.before_ref.refs_1_), channel_id=1, source_target_pairs={{0,4},{1,5},{4,8},{5,9},{8,12},{9,13},{12,14},{13,15},{14,10},{15,... | collective-permute-start | bytes 786440 | tf_op jit(solution)/shard_map/ppermute | solution.py:260
  19.9 10.0 %collective-permute-start.1 = (bf16[272,128]{1,0:T(8,128)(2,1)S(1)}, bf16[272,128]{1,0:T(8,128)(2,1)S(1)}, u32[]{:S(2)}, u32[]{:S(2)}) collective-permute-start(bf16[272,128]{1,0:T(8,128)(2,1)S(1)} %convert_element_type.21), channel_id=1, source_target_pairs={{0,8},{1,9},{2,10},{3,11},{4,12},{5,13},{6,14},{7,15},{8,0},{9,1},... | collective-permute-start | bytes 208904 | tf_op jit(solution)/shard_map/ppermute | solution.py:263
  22.3 8.9 %copy-start.11 = (bf16[512,256]{1,0:T(8,128)(2,1)S(1)}, bf16[512,256]{1,0:T(8,128)(2,1)}, u32[]{:S(2)}) copy-start(bf16[512,256]{1,0:T(8,128)(2,1)} %get-tuple-element.24.refs_0_) | copy-start | bytes 786436
  22.3 8.9 %copy-start.14 = (s32[64]{0:T(128)S(1)}, s32[64]{0:T(128)}, u32[]{:S(2)}) copy-start(s32[64]{0:T(128)} %constant.19.clone.table_ref) | copy-start | bytes 772
  27.9 7.6 %collective-permute-start.10 = (bf16[512,256]{1,0:T(8,128)(2,1)S(1)}, bf16[512,256]{1,0:T(8,128)(2,1)S(1)}, u32[]{:S(2)}, u32[]{:S(2)}) collective-permute-start(bf16[512,256]{1,0:T(8,128)(2,1)S(1)} %get-tuple-element.27.refs_3_), channel_id=1, source_target_pairs={{0,4},{1,5},{4,8},{5,9},{8,12},{9,13},{12,14},{13,15},{14,10},{15,... | collective-permute-start | bytes 786440 | tf_op jit(solution)/shard_map/ppermute | solution.py:260
  29.0 7.3 %collective-permute-start.11 = (bf16[512,256]{1,0:T(8,128)(2,1)S(1)}, bf16[512,256]{1,0:T(8,128)(2,1)S(1)}, u32[]{:S(2)}, u32[]{:S(2)}) collective-permute-start(bf16[512,256]{1,0:T(8,128)(2,1)S(1)} %get-tuple-element.28.refs_4_), channel_id=1, source_target_pairs={{0,2},{1,3},{4,0},{5,1},{8,4},{9,5},{12,8},{13,9},{14,12},{15,13},... | collective-permute-start | bytes 786440 | tf_op jit(solution)/shard_map/ppermute | solution.py:260
  29.9 9.6 %collective-permute-start.2 = (bf16[272,128]{1,0:T(8,128)(2,1)S(1)}, bf16[272,128]{1,0:T(8,128)(2,1)S(1)}, u32[]{:S(2)}, u32[]{:S(2)}) collective-permute-start(bf16[272,128]{1,0:T(8,128)(2,1)S(1)} %fusion), channel_id=1, source_target_pairs={{0,4},{1,5},{2,6},{3,7},{4,0},{5,1},{6,2},{7,3},{8,12},{9,13},{10,... | collective-permute-start | bytes 208904 | tf_op jit(solution)/shard_map/ppermute | solution.py:263
  36.3 6.2 %collective-permute-start.12 = (bf16[256,256]{1,0:T(8,128)(2,1)S(1)}, bf16[256,256]{1,0:T(8,128)(2,1)S(1)}, u32[]{:S(2)}, u32[]{:S(2)}) collective-permute-start(bf16[256,256]{1,0:T(8,128)(2,1)S(1)} %slice.6), channel_id=1, source_target_pairs={{0,4},{1,5},{4,8},{5,9},{8,12},{9,13},{12,14},{13,15},{14,10},{15,... | collective-permute-start | bytes 393224 | tf_op jit(solution)/shard_map/ppermute | solution.py:260
  36.7 5.9 %collective-permute-start.13 = (bf16[256,256]{1,0:T(8,128)(2,1)S(1)}, bf16[256,256]{1,0:T(8,128)(2,1)S(1)}, u32[]{:S(2)}, u32[]{:S(2)}) collective-permute-start(bf16[256,256]{1,0:T(8,128)(2,1)S(1)} %slice.7), channel_id=1, source_target_pairs={{0,2},{1,3},{4,0},{5,1},{8,4},{9,5},{12,8},{13,9},{14,12},{15,13},... | collective-permute-start | bytes 393224 | tf_op jit(solution)/shard_map/ppermute | solution.py:260
  39.5 4.4 %collective-permute-start.3 = (bf16[272,128]{1,0:T(8,128)(2,1)S(1)}, bf16[272,128]{1,0:T(8,128)(2,1)S(1)}, u32[]{:S(2)}, u32[]{:S(2)}) collective-permute-start(bf16[272,128]{1,0:T(8,128)(2,1)S(1)} %fusion.1), channel_id=1, source_target_pairs={{0,2},{1,3},{2,0},{3,1},{4,6},{5,7},{6,4},{7,5},{8,10},{9,11},{10,... | collective-permute-start | bytes 208904 | tf_op jit(solution)/shard_map/ppermute | solution.py:263
  42.5 2.7 %copy-start.5 = (bf16[256,512]{1,0:T(8,128)(2,1)S(1)}, bf16[256,512]{1,0:T(8,128)(2,1)}, u32[]{:S(2)}) copy-start(bf16[256,512]{1,0:T(8,128)(2,1)} %x_ref.1) | copy-start | bytes 786436
  42.6 2.7 %copy-start.10 = (bf16[512,512]{1,0:T(8,128)(2,1)S(1)}, bf16[512,512]{1,0:T(8,128)(2,1)}, u32[]{:S(2)}) copy-start(bf16[512,512]{1,0:T(8,128)(2,1)} %wo_ref.1) | copy-start | bytes 1572868
  43.4 2.6 %copy-start.3 = (bf16[512,1024]{1,0:T(8,128)(2,1)S(1)}, bf16[512,1024]{1,0:T(8,128)(2,1)}, u32[]{:S(2)}) copy-start(bf16[512,1024]{1,0:T(8,128)(2,1)} %up_ref.1) | copy-start | bytes 3145732
  43.4 2.6 %copy-start.4 = (bf16[1024,512]{1,0:T(8,128)(2,1)S(1)}, bf16[1024,512]{1,0:T(8,128)(2,1)}, u32[]{:S(2)}) copy-start(bf16[1024,512]{1,0:T(8,128)(2,1)} %down_ref.1) | copy-start | bytes 3145732
  43.4 2.6 %copy-start.15 = (f32[512]{0:T(512)S(1)}, f32[512]{0:T(512)}, u32[]{:S(2)}) copy-start(f32[512]{0:T(512)} %param.30) | copy-start | bytes 6148
  43.5 2.5 %collective-permute-start.14 = (f32[256,256]{1,0:T(8,128)S(1)}, f32[256,256]{1,0:T(8,128)S(1)}, u32[]{:S(2)}, u32[]{:S(2)}) collective-permute-start(f32[256,256]{1,0:T(8,128)S(1)} %get-tuple-element.36), channel_id=1, source_target_pairs={{0,1},{1,0},{2,3},{3,2},{4,5},{5,4},{6,7},{7,6},{8,9},{9,8},{10,11... | collective-permute-start | bytes 786440 | tf_op jit(solution)/shard_map/ppermute | solution.py:263
  43.9 1.3 %collective-permute-start.4 = (bf16[272,128]{1,0:T(8,128)(2,1)S(1)}, bf16[272,128]{1,0:T(8,128)(2,1)S(1)}, u32[]{:S(2)}, u32[]{:S(2)}) collective-permute-start(bf16[272,128]{1,0:T(8,128)(2,1)S(1)} %get-tuple-element.37), channel_id=1, source_target_pairs={{0,1},{1,0},{2,3},{3,2},{4,5},{5,4},{6,7},{7,6},{8,9},{9,8},{10,11... | collective-permute-start | bytes 208904 | tf_op jit(solution)/shard_map/ppermute | solution.py:263
  (2 other events, 1.5 us)

commit v3 on v2

v3 whole, which is shorter than its diff:
```python
import jax
import jax.numpy as jnp
from jax import lax
from jax.experimental import pallas as pl
from jax.experimental.pallas import tpu as pltpu
from jax.sharding import PartitionSpec as P

HEADS = 8
EPS = 1e-05
F32 = jnp.float32
BF16 = jnp.bfloat16
VMEM = pl.BlockSpec(memory_space=pltpu.VMEM)
SMEM = pl.BlockSpec(memory_space=pltpu.SMEM)
HBM = pl.BlockSpec(memory_space=pltpu.HBM)


def dot(a, b):
    return jnp.dot(a, b, preferred_element_type=F32)


def split(value):
    high = value.astype(BF16)
    return high, (value - high.astype(F32)).astype(BF16)


def layer_norm(values, gain):
    mean = jnp.mean(values, axis=-1, keepdims=True)
    centered = values - mean
    var = jnp.mean(centered * centered, axis=-1, keepdims=True)
    return (centered * lax.rsqrt(var + EPS) * gain).astype(BF16)


def call(body, outs, specs, args, scratch=(), limit=None):
    held = sum(a.size * a.dtype.itemsize for a in (*args, *jax.tree.leaves(outs)))
    limit = limit or held // 2**20 + 7
    return pl.pallas_call(
        body,
        out_shape=outs,
        in_specs=specs,
        out_specs=jax.tree.map(lambda _: VMEM, outs),
        scratch_shapes=scratch,
        compiler_params=pltpu.CompilerParams(vmem_limit_bytes=int(limit * 2**20)),
        cost_estimate=pl.CostEstimate(flops=1, bytes_accessed=1, transcendentals=0),
    )(*args)


def after(values, *others):
    any_space = pl.BlockSpec(memory_space=pl.ANY)
    return pl.pallas_call(
        lambda *refs: None,
        out_shape=[sds(v.shape, v.dtype) for v in values],
        in_specs=[any_space] * (len(values) + len(others)),
        out_specs=[any_space] * len(values),
        input_output_aliases={i: i for i in range(len(values))},
        compiler_params=pltpu.CompilerParams(vmem_limit_bytes=2**20),
        cost_estimate=pl.CostEstimate(flops=1, bytes_accessed=1, transcendentals=0),
    )(*values, *others)


def sds(shape, dtype):
    return jax.ShapeDtypeStruct(shape, dtype)


def pair_ones(rows, lanes):
    top = lax.broadcasted_iota(jnp.int32, (rows, lanes), 0) < rows // 2
    left = lax.broadcasted_iota(jnp.int32, (rows, lanes), 1) < lanes // 2
    return jnp.where(top == left, 1.0, 0.0)


def pair_omega(omega):
    zero = jnp.zeros_like(omega)
    return jnp.concatenate(
        [jnp.concatenate([omega, zero], axis=1), jnp.concatenate([zero, omega], axis=1)], axis=0
    )


class Fetch:
    def __init__(self, source, target, sems, pieces):
        rows = source.shape[0] // pieces
        self.copies = [
            pltpu.make_async_copy(
                source.at[pl.ds(i * rows, rows)], target.at[pl.ds(i * rows, rows)], sems.at[i]
            )
            for i in range(pieces)
        ]
        for copy in self.copies:
            copy.start()

    def wait(self):
        for copy in self.copies:
            copy.wait()


def buffers(*fetches):
    return [pltpu.VMEM(a.shape, a.dtype) for a, _ in fetches] + [
        pltpu.SemaphoreType.DMA((pieces,)) for _, pieces in fetches
    ]


PIECES = 4
EXTRA = 56


def message_kernel(
    x_hbm, gain_hbm, w_hbm, normed_ref, msg_ref, x_ref, gain_ref, w_ref, x_sem, gain_sem, w_sem
):
    x_copy = Fetch(x_hbm, x_ref, x_sem, PIECES)
    gain_copy = Fetch(gain_hbm, gain_ref, gain_sem, 1)
    w_copy = Fetch(w_hbm, w_ref, w_sem, PIECES)
    gain_copy.wait()
    x_copy.wait()
    normed = layer_norm(x_ref[...].astype(F32), gain_ref[...])
    normed_ref[...] = normed
    w_copy.wait()
    msg_ref[...] = dot(normed, w_ref[...]).astype(BF16)


def kv_kernel(
    me_ref, normed_hbm, wk_hbm, wv_hbm, omega_hbm, own_ref, near_ref, core_ref, both_ref, sums_ref,
    normed_ref, wk_ref, wv_ref, omega_ref, normed_sem, wk_sem, wv_sem, omega_sem
):
    normed_copy = Fetch(normed_hbm, normed_ref, normed_sem, PIECES)
    wk_copy = Fetch(wk_hbm, wk_ref, wk_sem, PIECES)
    omega_copy = Fetch(omega_hbm, omega_ref, omega_sem, 1)
    wv_copy = Fetch(wv_hbm, wv_ref, wv_sem, PIECES)
    width = normed_ref.shape[1]
    head = width // HEADS
    feat = omega_ref.shape[1]
    normed_copy.wait()
    normed = normed_ref[...]
    wk_copy.wait()
    keys = dot(normed, wk_ref[...]) * (head ** (-0.25))
    omega_copy.wait()
    wv_copy.wait()
    values = dot(normed, wv_ref[...])
    high, low = split(pair_omega(omega_ref[...]))
    ones = (-0.5 * pair_ones(2 * head, 2 * feat)).astype(BF16)
    first = jnp.concatenate([high, high], axis=0)
    second = jnp.concatenate([low, ones, ones], axis=0)
    left = lax.broadcasted_iota(jnp.int32, (feat, 2 * head), 1) < head
    pad = jnp.zeros((own_ref.shape[0] - feat - 2, feat), F32)
    for pair in range(HEADS // 2):
        k_pair = keys[:, pair * 2 * head : (pair + 1) * 2 * head]
        k_high, k_low = split(k_pair)
        s_high, s_low = split(k_pair * k_pair)
        logits = dot(jnp.concatenate([k_high, k_low], axis=1), first) + dot(
            jnp.concatenate([k_high, s_high, s_low], axis=1), second
        )
        kfeat = jnp.exp(logits)
        total = jnp.sum(kfeat, axis=0, keepdims=True)
        f_high, f_low = split(kfeat)
        v_high, v_low = split(values[:, pair * 2 * head : (pair + 1) * 2 * head])
        dims = (((0,), (0,)), ((), ()))
        both = lax.dot_general(f_high, v_high, dims, preferred_element_type=F32)
        both += lax.dot_general(f_low, v_high, dims, preferred_element_type=F32)
        both += lax.dot_general(f_high, v_low, dims, preferred_element_type=F32)
        block = jnp.where(left, both[:feat], both[feat:])
        sums_ref[pair] = jnp.concatenate([block, total[:, :feat], total[:, feat:], pad], axis=0)
    mine = (me_ref[0] % 2) * 2 + (me_ref[0] // 2) % 2
    own_ref[...] = sums_ref[mine]
    near_ref[...] = sums_ref[mine ^ 1].astype(BF16)
    core_ref[...] = sums_ref[mine ^ 2].astype(BF16)
    both_ref[...] = sums_ref[mine ^ 3].astype(BF16)


def query_kernel(normed_ref, wq_ref, wg_ref, omega_ref, qf_ref, gate_ref):
    normed = normed_ref[...]
    width = normed.shape[1]
    head = width // HEADS
    feat = omega_ref.shape[1]
    query = dot(normed, wq_ref[...]) * (head ** (-0.25))
    high, low = split(pair_omega(omega_ref[...]))
    first = jnp.concatenate([high, high], axis=0)
    for pair in range(HEADS // 2):
        q_high, q_low = split(query[:, pair * 2 * head : (pair + 1) * 2 * head])
        logits = dot(jnp.concatenate([q_high, q_low], axis=1), first) + dot(q_high, low)
        qf_ref[:, pair * 2 * feat : (pair + 1) * 2 * feat] = jnp.exp(logits).astype(BF16)
    gate_ref[...] = jax.nn.sigmoid(dot(normed, wg_ref[...]))


def place_kernel(core_ref, rows_ref, cols_ref, count_ref, tiles_ref, before_ref, mine_ref, theirs_ref):
    del before_ref
    per = mine_ref.shape[1]
    mine_ref[...] = jnp.zeros_like(mine_ref)
    theirs_ref[...] = jnp.zeros_like(theirs_ref)

    def body(slot, carry):
        col, row = cols_ref[slot], rows_ref[slot]
        place = (col // (2 * per)) * per + col % per
        own = (col // per) % 2 == core_ref[0]

        @pl.when(own)
        def _():
            mine_ref[place, row] = tiles_ref[slot]

        @pl.when(jnp.logical_not(own))
        def _():
            theirs_ref[place, row] = tiles_ref[slot]

        return carry

    lax.fori_loop(0, count_ref[0], body, 0)


def attend_kernel(
    me_ref, x_ref, qf_ref, gate_ref, own_ref, pair_ref, core_ref, both_ref, wo_ref, total_ref, mixed_ref
):
    width = x_ref.shape[1]
    head = width // HEADS
    feat = own_ref.shape[1]
    mine = (me_ref[0] % 2) * 2 + (me_ref[0] // 2) % 2
    left = lax.broadcasted_iota(jnp.int32, (feat, 2 * head), 1) < head
    ones = pair_ones(2 * feat, 2 * head).astype(BF16)
    joined = []
    for pair in range(HEADS // 2):
        offset = mine ^ pair
        part = own_ref[...].astype(F32)
        for other, ref in ((1, pair_ref), (2, core_ref), (3, both_ref)):
            part = jnp.where(offset == other, ref[...].astype(F32), part)
        block = part[:feat]
        block = jnp.concatenate([jnp.where(left, block, 0.0), jnp.where(left, 0.0, block)], axis=0)
        ksum = jnp.concatenate([part[feat : feat + 1], part[feat + 1 : feat + 2]], axis=1)
        q_pair = qf_ref[:, pair * 2 * feat : (pair + 1) * 2 * feat]
        numer = dot(q_pair, block.astype(BF16))
        d_high, d_low = split(q_pair.astype(F32) * ksum)
        denom = dot(d_high, ones) + dot(d_low, ones)
        joined.append(numer / denom)
    attn = jnp.concatenate(joined, axis=1)
    gated = (attn * gate_ref[...]).astype(BF16)
    mixed_ref[...] = x_ref[...].astype(F32) + total_ref[...] + dot(gated, wo_ref[...])


def product(dense_ref, column, chunk):
    rows, tile = dense_ref.shape[1:3]
    weights = [
        jnp.concatenate(
            [dense_ref[column + col, row] for col in range(chunk.shape[0] // tile)], axis=1
        )
        for row in range(rows)
    ]
    return dot(jnp.concatenate(weights, axis=0), chunk)


def solution(mesh):
    size = mesh.shape["blk"]
    chips = size // 2
    order = chip_order(mesh, size)

    def step(value, shift):
        pairs = [
            (order[p] * 2 + c, order[(p + shift) % chips] * 2 + c)
            for p in range(chips)
            for c in range(2)
        ]
        return lax.ppermute(value, "blk", pairs)

    def flip(value, bit):
        return lax.ppermute(value, "blk", [(i, i ^ bit) for i in range(size)])

    def on_device(
        features,
        tiles,
        block_rows,
        block_cols,
        block_count,
        ln_gain,
        w_msg,
        w_query,
        w_key,
        w_value,
        w_gate,
        w_out,
        omega,
        ln2_gain,
        w_up,
        w_down,
    ):
        nodes, width = features.shape
        tile = tiles.shape[1]
        feat = omega.shape[1]
        head = width // HEADS
        row_blocks = nodes // tile
        me = lax.axis_index("blk")
        core = (me % 2).reshape(1)
        me = me.reshape(1)
        normed, message = call(
            message_kernel,
            (sds((nodes, width), BF16), sds((nodes, width), BF16)),
            [HBM] * 3,
            (features, ln_gain.reshape(1, width), w_msg),
            buffers((features, PIECES), (sds((1, width), F32), 1), (w_msg, PIECES)),
            EXTRA,
        )

        full = (chips - 1) // 2
        ahead, back = step(message, 1), step(message, -1)

        rows = feat + 16
        given = sds((rows, feat), BF16)
        own, near, across, both = call(
            kv_kernel,
            (sds((rows, feat), F32), given, given, given),
            [SMEM] + [HBM] * 4,
            (me, normed, w_key, w_value, omega),
            [pltpu.VMEM((HEADS // 2, rows, feat), F32)]
            + buffers((normed, PIECES), (w_key, PIECES), (w_value, PIECES), (omega, 1)),
            56,
        )
        ahead, back = after([ahead, back], near)
        sums = [sum((flip(v, b).astype(F32) for v, b in ((near, 2), (across, 1), (both, 3))), own)]
        bit = 4
        while bit < size:
            hops = [bit, 2 * bit, 3 * bit] if 2 * bit < size else [bit]
            sent = sums[-1].astype(BF16)
            sums.append(sum((flip(sent, hop).astype(F32) for hop in hops), sums[-1]))
            bit *= 4
        quarter = sums[-1].astype(BF16)

        qfeat, gate = call(
            query_kernel,
            (sds((nodes, HEADS * feat), BF16), sds((nodes, width), F32)),
            [VMEM] * 4,
            (normed, w_query, w_gate, omega),
        )
        blocks = sds((chips * row_blocks, row_blocks, tile, tile), BF16)
        dense, others = call(
            place_kernel,
            (blocks, blocks),
            [SMEM] * 4 + [VMEM, pl.BlockSpec(memory_space=pl.ANY)],
            (core, block_rows, block_cols, block_count, tiles, sums[0]),
        )
        shifts = [0] + [sign * k for k in range(1, full + 1) for sign in (1, -1)]
        if chips % 2 == 0:
            shifts += [chips // 2]
        home = {chip: p for p, chip in enumerate(order)}
        table = jnp.asarray(
            [order[(home[chip] - shift) % chips] for chip in range(chips) for shift in shifts],
            jnp.int32,
        )

        def accumulate(matrices, totals, first, chunks, dtype=F32):
            totals, count = list(totals), len(matrices)

            def body(me_ref, table_ref, *refs):
                for dense_ref, out, total in zip(refs, refs[-count:], totals or [None] * count):
                    value = None
                    if totals:
                        value = refs[count + [t is total for t in totals].index(True)][...]
                    place, seen = first, 0
                    for chunk_ref in refs[count + len(totals) : -count]:
                        chip = table_ref[(me_ref[0] // 2) * chips + place]
                        column = chip * row_blocks + seen // tile
                        part = product(dense_ref, column, chunk_ref[...])
                        value = part if value is None else value + part
                        seen += chunk_ref.shape[0]
                        if seen == nodes:
                            place, seen = place + 1, 0
                    out[...] = value.astype(out.dtype)

            return call(
                body,
                [sds((nodes, width), dtype)] * count,
                [SMEM] * 2 + [VMEM] * (count + len(totals) + len(chunks)),
                (me, table, *matrices, *totals, *chunks),
            )

        chunks = [message, ahead, back]
        totals, used = (), 0
        sibling = None
        for k in range(2, full + 1):
            if k == 3:
                ahead, back, others = after([ahead, back, others], dense)
                chunks[-2:] = [ahead, back]
                sibling = flip(others, 1)
            if k > 3:
                ready = 1 + 2 * (k - 2)
                totals = accumulate((dense, sibling), totals, used, chunks[used:ready])
                used = ready
                ahead, back = after([ahead, back], totals[0])
                chunks[-2:] = [ahead, back]
            ahead, back = step(ahead, 1), step(back, -1)
            chunks += [ahead, back]
        ready = 1 + 2 * (full - 1)
        totals = accumulate((dense, sibling), totals, used, chunks[used:ready])
        ahead, back = after([ahead, back], totals[0], qfeat)
        chunks[-2:] = [ahead, back]
        late = [step(ahead[: nodes // 2], 1), step(back[nodes // 2 :], -1)]
        totals = accumulate((dense, sibling), totals, ready, chunks[ready:])
        mixed = call(
            attend_kernel,
            sds((nodes, width), F32),
            [SMEM] + [VMEM] * 9,
            (me, features, qfeat, gate, quarter, flip(quarter, 2), flip(quarter, 1), flip(quarter, 3), w_out, totals[0]),
        )
        late = after(late, *totals, mixed)
        start = len(chunks)
        (given,) = accumulate((sibling,), totals[1:], start, late, BF16)
        (mine,) = accumulate((dense,), [mixed], start, late)
        theirs = flip(given, 1)

        def final_kernel(mine_ref, theirs_ref, gain_ref, up_ref, down_ref, out_ref):
            mixed = mine_ref[...] + theirs_ref[...].astype(F32)
            second = layer_norm(mixed, gain_ref[...])
            inner = jnp.maximum(dot(second, up_ref[...]), 0.0).astype(BF16)
            out_ref[...] = (mixed + dot(inner, down_ref[...])).astype(BF16)

        return call(
            final_kernel,
            sds((nodes, width), BF16),
            [VMEM] * 5,
            (mine, theirs, ln2_gain.reshape(1, width), w_up, w_down),
        )

    split_rows = P(("groups", "blk"))
    return jax.shard_map(
        on_device,
        mesh=mesh,
        in_specs=(split_rows,) * 5 + (P(),) * 11,
        out_specs=P(("groups", "blk"), None),
        check_vma=False,
    )


def chip_order(mesh, size):
    devices = mesh.devices.reshape(-1, size)[0]
    coords = [getattr(d, "coords", None) for d in devices[::2]]
    if any(c is None for c in coords) or len({c[1] for c in map(tuple, coords)}) != 2:
        return list(range(size // 2))
    low = min(c[1] for c in coords)
    up = sorted((i for i, c in enumerate(coords) if c[1] == low), key=lambda i: coords[i][2])
    down = sorted((i for i, c in enumerate(coords) if c[1] != low), key=lambda i: -coords[i][2])
    return up + down
```

time: 47.9 us -> 46.4 us (0.969)
  waiting for transfers between devices: 14 us -> 10.1 us
  local copies, waits for them, and re-layouts: 4.66 us -> 0.86 us
  Pallas kernels: 12 us -> 14.9 us
  starting transfers between devices: 15.9 us -> 18.4 us
  other arithmetic: 0.11 us -> 0.94 us
    ppermute x8, waiting for transfers between devices: 11.2 us -> 6.79 us  [step(): return lax.ppermute(value, 'blk', pairs)]
    unnamed x38 -> x30, local copies, waits for them, and re-layouts: 4.64 us -> 0.84 us
    ppermute x7 -> x11, starting transfers between devices: 5.6 us -> 9.05 us  [flip(): return lax.ppermute(value, 'blk', [(i, i ^ bit) for i in range(size)])]
    pallas_call x9 -> x10, Pallas kernels: 12 us -> 14.9 us  [call(): pl.pallas_call(body, out_shape=outs, in_specs=specs, out_specs=jax.tree.m...]
    ppermute x8, starting transfers between devices: 10.3 us -> 9.39 us  [step(): return lax.ppermute(value, 'blk', pairs)]
    convert_element_type x4 -> x2, other arithmetic: 0.11 us -> 0.94 us  [the longest x1 0.91 us: on_device(): sent = sums[-1].astype(BF16)]
    ppermute x7 -> x11, waiting for transfers between devices: 2.86 us -> 3.32 us  [flip(): return lax.ppermute(value, 'blk', [(i, i ^ bit) for i in range(size)])]
  transfers between devices with their start and end apart: 15 -> 19, of which waited for: 9 -> 8; matrix products, arithmetic and copies ran while one was open for 0% -> 2% of each run, Pallas kernels for 14% -> 21%
where the time goes in v3:
time: 46.4 us; the launch traced here: 46.1 us
  starting transfers between devices  18.4 us (40%)
  Pallas kernels  14.9 us (32%)
  waiting for transfers between devices  10.1 us (22%)
  other arithmetic  0.94 us (2%)
  between operations  0.94 us (2%)
  local copies, waits for them, and re-layouts  0.86 us (2%)
    pallas_call x10, Pallas kernels, call(): pl.pallas_call(body, out_shape=outs, in_specs=specs, out_specs=jax.tree.m...  14.9 us
    ppermute x8, starting transfers between devices, step(): return lax.ppermute(value, 'blk', pairs)  9.39 us
    ppermute x11, starting transfers between devices, flip(): return lax.ppermute(value, 'blk', [(i, i ^ bit) for i in range(size)])  9.05 us
    ppermute x8, waiting for transfers between devices, step(): return lax.ppermute(value, 'blk', pairs)  6.79 us
    ppermute x11, waiting for transfers between devices, flip(): return lax.ppermute(value, 'blk', [(i, i ^ bit) for i in range(size)])  3.32 us
  transfers between devices with their start and end apart: 19, of which 8 were waited for; matrix products, arithmetic and copies ran while one was open for 2% of the time, Pallas kernels for 21%

profile of v3, /device:TPU:0, one launch (start us, length us, event | category | flops | bytes accessed | tf_op | source)
XLA Modules:
  0.0 46.1 jit_solution(2674195788653688844)
XLA Ops:
  0.0 2.6 %shard_map.163 = (bf16[256,512]{1,0:T(8,128)(2,1)}, bf16[256,512]{1,0:T(8,128)(2,1)}) custom-call(bf16[256,512]{1,0:T(8,128)(2,1)} %x_ref.1, f32[1,512]{1,0:T(1,128)} %bitcast.5, bf16[512,512]{1,0:T(8,128)(2,1)} %w_hbm.1), custom_call_target="tpu_custom_call" | custom-call | flops 1 | bytes 1 | tf_op jit(solution)/shard_map/pallas_call | solution.py:36
  2.6 3.0 %collective-permute-start.10 = (bf16[256,512]{1,0:T(8,128)(2,1)}, bf16[256,512]{1,0:T(8,128)(2,1)S(1)}, u32[]{:S(2)}, u32[]{:S(2)}) collective-permute-start(bf16[256,512]{1,0:T(8,128)(2,1)} %get-tuple-element.36.refs_2_), channel_id=1, source_target_pairs={{0,2},{1,3},{4,0},{5,1},{8,4},{9,5},{12,8},{13,9},{14,12},{15,13},... | collective-permute-start | bytes 786440 | tf_op jit(solution)/shard_map/ppermute | solution.py:255
  5.7 3.9 %shard_map.164 = (f32[144,128]{1,0:T(8,128)}, bf16[144,128]{1,0:T(8,128)(2,1)}, bf16[144,128]{1,0:T(8,128)(2,1)}, bf16[144,128]{1,0:T(8,128)(2,1)}) custom-call(s32[1]{0:T(128)} %bitcast.me_ref, bf16[256,512]{1,0:T(8,128)(2,1)} %get-tuple-element.28.normed_hbm.normed_ref, bf16[512,512]{1,0:T(8,128)(2,1)} %wk_hbm.1, bf16[512,512]{1,0:T(8,128)(2,1)} %wv_hbm.1, ...), custom_call_target="tpu_custom_call" | custom-call | flops 1 | bytes 1 | tf_op jit(solution)/shard_map/pallas_call | solution.py:36
  9.6 2.0 %collective-permute-start = (bf16[144,128]{1,0:T(8,128)(2,1)}, bf16[144,128]{1,0:T(8,128)(2,1)S(1)}, u32[]{:S(2)}, u32[]{:S(2)}) collective-permute-start(bf16[144,128]{1,0:T(8,128)(2,1)} %get-tuple-element.30.refs_2_), channel_id=1, source_target_pairs={{0,2},{1,3},{2,0},{3,1},{4,6},{5,7},{6,4},{7,5},{8,10},{9,11},{10,... | collective-permute-start | bytes 110600 | tf_op jit(solution)/shard_map/ppermute | solution.py:258
  11.8 0.3 collective-permute-done.10.refs_1_
  12.2 1.8 %collective-permute-done.9.refs_0_ = bf16[256,512]{1,0:T(8,128)(2,1)S(1)} collective-permute-done((bf16[256,512]{1,0:T(8,128)(2,1)}, bf16[256,512]{1,0:T(8,128)(2,1)S(1)}, u32[]{:S(2)}, u32[]{:S(2)}) %collective-permute-start.9) | collective-permute-done | bytes 262176 | tf_op jit(solution)/shard_map/ppermute | solution.py:255
  14.0 0.8 %copy-done.10 = bf16[144,128]{1,0:T(8,128)(2,1)S(1)} copy-done((bf16[144,128]{1,0:T(8,128)(2,1)S(1)}, bf16[144,128]{1,0:T(8,128)(2,1)}, u32[]{:S(2)}) %copy-start.10) | copy-done | bytes 36888
  14.8 2.0 %collective-permute-start.12 = (bf16[256,512]{1,0:T(8,128)(2,1)S(1)}, bf16[256,512]{1,0:T(8,128)(2,1)S(1)}, u32[]{:S(2)}, u32[]{:S(2)}) collective-permute-start(bf16[256,512]{1,0:T(8,128)(2,1)S(1)} %get-tuple-element.38.refs_4_), channel_id=1, source_target_pairs={{0,2},{1,3},{4,0},{5,1},{8,4},{9,5},{12,8},{13,9},{14,12},{15,13},... | collective-permute-start | bytes 786440 | tf_op jit(solution)/shard_map/ppermute | solution.py:255
  17.5 0.9 %fusion = (bf16[144,128]{1,0:T(8,128)(2,1)S(1)}, f32[144,128]{1,0:T(8,128)S(1)}) fusion(bf16[144,128]{1,0:T(8,128)(2,1)S(1)} %collective-permute-done.2, bf16[144,128]{1,0:T(8,128)(2,1)S(1)} %collective-permute-done.1, f32[144,128]{1,0:T(8,128)} %get-tuple-element.29, bf16[144,128]{1,0:T(8,128)(2,1)S(1)} %collective-permute-done), kind=kLoop, calls=%fused_computation.2 | loop fusion | flops 129024 | bytes 294912 | tf_op jit(solution)/shard_map/convert_element_type | solution.py:314
  18.4 1.2 %shard_map.165 = (bf16[16,2,128,128]{3,2,1,0:T(8,128)(2,1)S(1)}, bf16[16,2,128,128]{3,2,1,0:T(8,128)(2,1)S(1)}) custom-call(s32[1]{0:T(128)} %bitcast.1.core_ref, s32[48]{0:T(128)S(1)} %copy-done.13, s32[48]{0:T(128)S(1)} %copy-done.14, s32[1]{0:T(128)S(6)} %copy.36.count_ref, bf16[48,128,128]{2,1,0:T(8,128)(2,1)S(1)} %copy-done, ...), custom_call_target="tpu_custom_call" | custom-call | flops 1 | bytes 1 | tf_op jit(solution)/shard_map/pallas_call | solution.py:36
  19.7 1.8 %collective-permute-done.11.refs_0_ = bf16[256,512]{1,0:T(8,128)(2,1)S(1)} collective-permute-done((bf16[256,512]{1,0:T(8,128)(2,1)S(1)}, bf16[256,512]{1,0:T(8,128)(2,1)S(1)}, u32[]{:S(2)}, u32[]{:S(2)}) %collective-permute-start.11) | collective-permute-done | bytes 262176 | tf_op jit(solution)/shard_map/ppermute | solution.py:255
  21.5 1.0 %collective-permute-done.12.refs_1_ = bf16[256,512]{1,0:T(8,128)(2,1)S(1)} collective-permute-done((bf16[256,512]{1,0:T(8,128)(2,1)S(1)}, bf16[256,512]{1,0:T(8,128)(2,1)S(1)}, u32[]{:S(2)}, u32[]{:S(2)}) %collective-permute-start.12) | collective-permute-done | bytes 262176 | tf_op jit(solution)/shard_map/ppermute | solution.py:255
  22.5 1.6 %collective-permute-start.14 = (bf16[256,512]{1,0:T(8,128)(2,1)S(1)}, bf16[256,512]{1,0:T(8,128)(2,1)S(1)}, u32[]{:S(2)}, u32[]{:S(2)}) collective-permute-start(bf16[256,512]{1,0:T(8,128)(2,1)S(1)} %get-tuple-element.41.refs_5_), channel_id=1, source_target_pairs={{0,4},{1,5},{4,8},{5,9},{8,12},{9,13},{12,14},{13,15},{14,10},{15,... | collective-permute-start | bytes 786440 | tf_op jit(solution)/shard_map/ppermute | solution.py:255
  24.2 0.4 collective-permute-start.15
  24.6 1.6 %collective-permute-start.3 = (bf16[144,128]{1,0:T(8,128)(2,1)S(1)}, bf16[144,128]{1,0:T(8,128)(2,1)S(1)}, u32[]{:S(2)}, u32[]{:S(2)}) collective-permute-start(bf16[144,128]{1,0:T(8,128)(2,1)S(1)} %get-tuple-element.51), channel_id=1, source_target_pairs={{0,4},{1,5},{2,6},{3,7},{4,0},{5,1},{6,2},{7,3},{8,12},{9,13},{10,... | collective-permute-start | bytes 110600 | tf_op jit(solution)/shard_map/ppermute | solution.py:258
  26.2 2.5 %collective-permute-start.4 = (bf16[144,128]{1,0:T(8,128)(2,1)S(1)}, bf16[144,128]{1,0:T(8,128)(2,1)S(1)}, u32[]{:S(2)}, u32[]{:S(2)}) collective-permute-start(bf16[144,128]{1,0:T(8,128)(2,1)S(1)} %get-tuple-element.51), channel_id=1, source_target_pairs={{0,8},{1,9},{2,10},{3,11},{4,12},{5,13},{6,14},{7,15},{8,0},{9,1},... | collective-permute-start | bytes 110600 | tf_op jit(solution)/shard_map/ppermute | solution.py:258
  28.7 0.3 collective-permute-start.5
  29.0 0.8 %shard_map.166 = (bf16[256,1024]{1,0:T(8,128)(2,1)S(1)}, f32[256,512]{1,0:T(8,128)S(1)}) custom-call(bf16[256,512]{1,0:T(8,128)(2,1)S(1)} %copy-done.2, bf16[512,512]{1,0:T(8,128)(2,1)S(1)} %copy-done.6, bf16[512,512]{1,0:T(8,128)(2,1)S(1)} %copy-done.7, f32[64,128]{1,0:T(8,128)S(1)} %copy-done.9), custom_call_target="tpu_custom_call" | custom-call | flops 1 | bytes 1 | tf_op jit(solution)/shard_map/pallas_call | solution.py:36
  29.8 1.4 %shard_map.169 = (f32[256,512]{1,0:T(8,128)S(1)}, f32[256,512]{1,0:T(8,128)S(1)}) custom-call(s32[1]{0:T(128)} %bitcast.me_ref, s32[64]{0:T(128)S(1)} %copy-done.11, bf16[16,2,128,128]{3,2,1,0:T(8,128)(2,1)S(1)} %get-tuple-element.33.refs_3_.refs_0_, bf16[16,2,128,128]{3,2,1,0:T(8,128)(2,1)S(1)} %collective-permute-done.13.refs_1_.refs_0_, ...), custom_call_target="tpu_custom_call" | custom-call | flops 1 | bytes 1 | tf_op jit(solution)/shard_map/pallas_call | solution.py:36
  31.2 1.8 %collective-permute-done.15.refs_1_ = bf16[256,512]{1,0:T(8,128)(2,1)S(1)} collective-permute-done((bf16[256,512]{1,0:T(8,128)(2,1)S(1)}, bf16[256,512]{1,0:T(8,128)(2,1)S(1)}, u32[]{:S(2)}, u32[]{:S(2)}) %collective-permute-start.15) | collective-permute-done | bytes 262176 | tf_op jit(solution)/shard_map/ppermute | solution.py:255
  33.1 1.9 %collective-permute-start.16 = (bf16[128,512]{1,0:T(8,128)(2,1)S(1)}, bf16[128,512]{1,0:T(8,128)(2,1)S(1)}, u32[]{:S(2)}, u32[]{:S(2)}) collective-permute-start(bf16[128,512]{1,0:T(8,128)(2,1)S(1)} %slice.6), channel_id=1, source_target_pairs={{0,4},{1,5},{4,8},{5,9},{8,12},{9,13},{12,14},{13,15},{14,10},{15,... | collective-permute-start | bytes 393224 | tf_op jit(solution)/shard_map/ppermute | solution.py:255
  35.0 0.3 collective-permute-start.17
  35.3 1.7 %collective-permute-done.5 = bf16[144,128]{1,0:T(8,128)(2,1)S(1)} collective-permute-done((bf16[144,128]{1,0:T(8,128)(2,1)S(1)}, bf16[144,128]{1,0:T(8,128)(2,1)S(1)}, u32[]{:S(2)}, u32[]{:S(2)}) %collective-permute-start.5) | collective-permute-done | bytes 36896 | tf_op jit(solution)/shard_map/ppermute | solution.py:258
  37.2 2.0 %collective-permute-start.8 = (bf16[144,128]{1,0:T(8,128)(2,1)S(1)}, bf16[144,128]{1,0:T(8,128)(2,1)S(1)}, u32[]{:S(2)}, u32[]{:S(2)}) collective-permute-start(bf16[144,128]{1,0:T(8,128)(2,1)S(1)} %add_convert_fusion.own_ref), channel_id=1, source_target_pairs={{0,3},{1,2},{2,1},{3,0},{4,7},{5,6},{6,5},{7,4},{8,11},{9,10},{10,... | collective-permute-start | bytes 110600 | tf_op jit(solution)/shard_map/ppermute | solution.py:258
  39.2 1.0 %shard_map.171 = (f32[256,512]{1,0:T(8,128)S(1)}, f32[256,512]{1,0:T(8,128)S(1)}) custom-call(s32[1]{0:T(128)} %bitcast.me_ref, s32[64]{0:T(128)S(1)} %copy-done.11, bf16[16,2,128,128]{3,2,1,0:T(8,128)(2,1)S(1)} %get-tuple-element.33.refs_3_.refs_0_, bf16[16,2,128,128]{3,2,1,0:T(8,128)(2,1)S(1)} %collective-permute-done.13.refs_1_.refs_0_, ...), custom_call_target="tpu_custom_call" | custom-call | flops 1 | bytes 1 | tf_op jit(solution)/shard_map/pallas_call | solution.py:36
  40.2 1.0 %collective-permute-done.6.pair_ref = bf16[144,128]{1,0:T(8,128)(2,1)S(1)} collective-permute-done((bf16[144,128]{1,0:T(8,128)(2,1)S(1)}, bf16[144,128]{1,0:T(8,128)(2,1)S(1)}, u32[]{:S(2)}, u32[]{:S(2)}) %collective-permute-start.6) | collective-permute-done | bytes 36896 | tf_op jit(solution)/shard_map/ppermute | solution.py:258
  41.3 0.7 %shard_map.172.refs_4_.refs_1_ = f32[256,512]{1,0:T(8,128)S(1)} custom-call(s32[1]{0:T(128)} %bitcast.me_ref, bf16[256,512]{1,0:T(8,128)(2,1)S(1)} %copy-done.1, bf16[256,1024]{1,0:T(8,128)(2,1)S(1)} %get-tuple-element.34.refs_3_.qf_ref, f32[256,512]{1,0:T(8,128)S(1)} %get-tuple-element.35.gate_ref, bf16[144,128]{1,0:T(8,128)(2,1)S(1)} %add_convert_fusion.own_ref, ...), custom_call_target="tpu_custom_call" | custom-call | flops 1 | bytes 1 | tf_op jit(solution)/shard_map/pallas_call | solution.py:36
  42.1 0.8 %shard_map.175 = bf16[256,512]{1,0:T(8,128)(2,1)S(1)} custom-call(s32[1]{0:T(128)} %bitcast.me_ref, s32[64]{0:T(128)S(1)} %copy-done.11, bf16[16,2,128,128]{3,2,1,0:T(8,128)(2,1)S(1)} %collective-permute-done.13.refs_1_.refs_0_, f32[256,512]{1,0:T(8,128)S(1)} %get-tuple-element.48.refs_3_.refs_1_, bf16[128,512]{1,0:T(8,128)(2,1)S(1)} %get-tuple-element.49.refs_2_, ...), custom_call_target="tpu_custom_call" | custom-call | flops 1 | bytes 1 | tf_op jit(solution)/shard_map/pallas_call | solution.py:36
  42.9 0.3 collective-permute-start.18
  43.2 0.8 %shard_map.174.mine_ref = f32[256,512]{1,0:T(8,128)S(1)} custom-call(s32[1]{0:T(128)} %bitcast.me_ref, s32[64]{0:T(128)S(1)} %copy-done.11, bf16[16,2,128,128]{3,2,1,0:T(8,128)(2,1)S(1)} %get-tuple-element.33.refs_3_.refs_0_, f32[256,512]{1,0:T(8,128)S(1)} %shard_map.172.refs_4_.refs_1_, bf16[128,512]{1,0:T(8,128)(2,1)S(1)} %get-tuple-element.49.refs_2_, ...), custom_call_target="tpu_custom_call" | custom-call | flops 1 | bytes 1 | tf_op jit(solution)/shard_map/pallas_call | solution.py:36
  44.0 0.5 %collective-permute-done.18.theirs_ref = bf16[256,512]{1,0:T(8,128)(2,1)S(1)} collective-permute-done((bf16[256,512]{1,0:T(8,128)(2,1)S(1)}, bf16[256,512]{1,0:T(8,128)(2,1)S(1)}, u32[]{:S(2)}, u32[]{:S(2)}) %collective-permute-start.18) | collective-permute-done | bytes 262176 | tf_op jit(solution)/shard_map/ppermute | solution.py:258
  44.5 1.6 %shard_map.176 = bf16[256,512]{1,0:T(8,128)(2,1)} custom-call(f32[256,512]{1,0:T(8,128)S(1)} %shard_map.174.mine_ref, bf16[256,512]{1,0:T(8,128)(2,1)S(1)} %collective-permute-done.18.theirs_ref, f32[1,512]{1,0:T(1,128)S(1)} %bitcast.4, bf16[512,1024]{1,0:T(8,128)(2,1)S(1)} %copy-done.3, bf16[1024,512]{1,0:T(8,128)(2,1)S(1)} %copy-done.4), custom_call_target="tpu_custom_call" | custom-call | flops 1 | bytes 1 | tf_op jit(solution)/shard_map/pallas_call | solution.py:36
  (54 shorter events, 0.7 us)
Async XLA Ops:
  0.0 18.4 %copy-start = (bf16[48,128,128]{2,1,0:T(8,128)(2,1)S(1)}, bf16[48,128,128]{2,1,0:T(8,128)(2,1)}, u32[]{:S(2)}) copy-start(bf16[48,128,128]{2,1,0:T(8,128)(2,1)} %tiles_ref.1) | copy-start | bytes 4718596
  0.0 18.4 %copy-start.13 = (s32[48]{0:T(128)S(1)}, s32[48]{0:T(128)}, u32[]{:S(2)}) copy-start(s32[48]{0:T(128)} %rows_ref.1) | copy-start | bytes 580
  0.0 18.4 %copy-start.14 = (s32[48]{0:T(128)S(1)}, s32[48]{0:T(128)}, u32[]{:S(2)}) copy-start(s32[48]{0:T(128)} %cols_ref.1) | copy-start | bytes 580
  2.6 9.6 %collective-permute-start.10 = (bf16[256,512]{1,0:T(8,128)(2,1)}, bf16[256,512]{1,0:T(8,128)(2,1)S(1)}, u32[]{:S(2)}, u32[]{:S(2)}) collective-permute-start(bf16[256,512]{1,0:T(8,128)(2,1)} %get-tuple-element.36.refs_2_), channel_id=1, source_target_pairs={{0,2},{1,3},{4,0},{5,1},{8,4},{9,5},{12,8},{13,9},{14,12},{15,13},... | collective-permute-start | bytes 786440 | tf_op jit(solution)/shard_map/ppermute | solution.py:255
  5.6 8.4 %collective-permute-start.9 = (bf16[256,512]{1,0:T(8,128)(2,1)}, bf16[256,512]{1,0:T(8,128)(2,1)S(1)}, u32[]{:S(2)}, u32[]{:S(2)}) collective-permute-start(bf16[256,512]{1,0:T(8,128)(2,1)} %get-tuple-element.36.refs_2_), channel_id=1, source_target_pairs={{0,4},{1,5},{4,8},{5,9},{8,12},{9,13},{12,14},{13,15},{14,10},{15,... | collective-permute-start | bytes 786440 | tf_op jit(solution)/shard_map/ppermute | solution.py:255
  9.6 7.8 %collective-permute-start = (bf16[144,128]{1,0:T(8,128)(2,1)}, bf16[144,128]{1,0:T(8,128)(2,1)S(1)}, u32[]{:S(2)}, u32[]{:S(2)}) collective-permute-start(bf16[144,128]{1,0:T(8,128)(2,1)} %get-tuple-element.30.refs_2_), channel_id=1, source_target_pairs={{0,2},{1,3},{2,0},{3,1},{4,6},{5,7},{6,4},{7,5},{8,10},{9,11},{10,... | collective-permute-start | bytes 110600 | tf_op jit(solution)/shard_map/ppermute | solution.py:258
  11.6 5.8 %collective-permute-start.1 = (bf16[144,128]{1,0:T(8,128)(2,1)}, bf16[144,128]{1,0:T(8,128)(2,1)S(1)}, u32[]{:S(2)}, u32[]{:S(2)}) collective-permute-start(bf16[144,128]{1,0:T(8,128)(2,1)} %get-tuple-element.31), channel_id=1, source_target_pairs={{0,1},{1,0},{2,3},{3,2},{4,5},{5,4},{6,7},{7,6},{8,9},{9,8},{10,11... | collective-permute-start | bytes 110600 | tf_op jit(solution)/shard_map/ppermute | solution.py:258
  11.6 5.8 %collective-permute-start.2 = (bf16[144,128]{1,0:T(8,128)(2,1)}, bf16[144,128]{1,0:T(8,128)(2,1)S(1)}, u32[]{:S(2)}, u32[]{:S(2)}) collective-permute-start(bf16[144,128]{1,0:T(8,128)(2,1)} %get-tuple-element.32), channel_id=1, source_target_pairs={{0,3},{1,2},{2,1},{3,0},{4,7},{5,6},{6,5},{7,4},{8,11},{9,10},{10,... | collective-permute-start | bytes 110600 | tf_op jit(solution)/shard_map/ppermute | solution.py:258
  14.7 6.8 %collective-permute-start.11 = (bf16[256,512]{1,0:T(8,128)(2,1)S(1)}, bf16[256,512]{1,0:T(8,128)(2,1)S(1)}, u32[]{:S(2)}, u32[]{:S(2)}) collective-permute-start(bf16[256,512]{1,0:T(8,128)(2,1)S(1)} %get-tuple-element.37.refs_3_), channel_id=1, source_target_pairs={{0,4},{1,5},{4,8},{5,9},{8,12},{9,13},{12,14},{13,15},{14,10},{15,... | collective-permute-start | bytes 786440 | tf_op jit(solution)/shard_map/ppermute | solution.py:255
  14.8 7.8 %collective-permute-start.12 = (bf16[256,512]{1,0:T(8,128)(2,1)S(1)}, bf16[256,512]{1,0:T(8,128)(2,1)S(1)}, u32[]{:S(2)}, u32[]{:S(2)}) collective-permute-start(bf16[256,512]{1,0:T(8,128)(2,1)S(1)} %get-tuple-element.38.refs_4_), channel_id=1, source_target_pairs={{0,2},{1,3},{4,0},{5,1},{8,4},{9,5},{12,8},{13,9},{14,12},{15,13},... | collective-permute-start | bytes 786440 | tf_op jit(solution)/shard_map/ppermute | solution.py:255
  19.7 9.3 %copy-start.2 = (bf16[256,512]{1,0:T(8,128)(2,1)S(1)}, bf16[256,512]{1,0:T(8,128)(2,1)}, u32[]{:S(2)}) copy-start(bf16[256,512]{1,0:T(8,128)(2,1)} %get-tuple-element.28.normed_hbm.normed_ref) | copy-start | bytes 786436
  19.7 9.3 %copy-start.6 = (bf16[512,512]{1,0:T(8,128)(2,1)S(1)}, bf16[512,512]{1,0:T(8,128)(2,1)}, u32[]{:S(2)}) copy-start(bf16[512,512]{1,0:T(8,128)(2,1)} %wq_ref.1) | copy-start | bytes 1572868
  19.7 9.3 %copy-start.7 = (bf16[512,512]{1,0:T(8,128)(2,1)S(1)}, bf16[512,512]{1,0:T(8,128)(2,1)}, u32[]{:S(2)}) copy-start(bf16[512,512]{1,0:T(8,128)(2,1)} %wg_ref.1) | copy-start | bytes 1572868
  19.7 9.3 %copy-start.9 = (f32[64,128]{1,0:T(8,128)S(1)}, f32[64,128]{1,0:T(8,128)}, u32[]{:S(2)}) copy-start(f32[64,128]{1,0:T(8,128)} %omega_ref.1) | copy-start | bytes 98308
  22.5 7.3 %copy-start.8 = (bf16[256,512]{1,0:T(8,128)(2,1)S(1)}, bf16[256,512]{1,0:T(8,128)(2,1)}, u32[]{:S(2)}) copy-start(bf16[256,512]{1,0:T(8,128)(2,1)} %get-tuple-element.36.refs_2_) | copy-start | bytes 786436
  22.5 7.3 %copy-start.11 = (s32[64]{0:T(128)S(1)}, s32[64]{0:T(128)}, u32[]{:S(2)}) copy-start(s32[64]{0:T(128)} %constant.19.clone.table_ref) | copy-start | bytes 772
  22.5 6.2 %collective-permute-start.13 = (bf16[16,2,128,128]{3,2,1,0:T(8,128)(2,1)S(1)}, bf16[16,2,128,128]{3,2,1,0:T(8,128)(2,1)S(1)}, u32[]{:S(2)}, u32[]{:S(2)}) collective-permute-start(bf16[16,2,128,128]{3,2,1,0:T(8,128)(2,1)S(1)} %get-tuple-element.40), channel_id=1, source_target_pairs={{0,1},{1,0},{2,3},{3,2},{4,5},{5,4},{6,7},{7,6},{8,9},{9,8},{10,11... | collective-permute-start | bytes 3145736 | tf_op jit(solution)/shard_map/ppermute | solution.py:258
  22.5 8.7 %collective-permute-start.14 = (bf16[256,512]{1,0:T(8,128)(2,1)S(1)}, bf16[256,512]{1,0:T(8,128)(2,1)S(1)}, u32[]{:S(2)}, u32[]{:S(2)}) collective-permute-start(bf16[256,512]{1,0:T(8,128)(2,1)S(1)} %get-tuple-element.41.refs_5_), channel_id=1, source_target_pairs={{0,4},{1,5},{4,8},{5,9},{8,12},{9,13},{12,14},{13,15},{14,10},{15,... | collective-permute-start | bytes 786440 | tf_op jit(solution)/shard_map/ppermute | solution.py:255
  24.2 8.9 %collective-permute-start.15 = (bf16[256,512]{1,0:T(8,128)(2,1)S(1)}, bf16[256,512]{1,0:T(8,128)(2,1)S(1)}, u32[]{:S(2)}, u32[]{:S(2)}) collective-permute-start(bf16[256,512]{1,0:T(8,128)(2,1)S(1)} %get-tuple-element.42.refs_6_), channel_id=1, source_target_pairs={{0,2},{1,3},{4,0},{5,1},{8,4},{9,5},{12,8},{13,9},{14,12},{15,13},... | collective-permute-start | bytes 786440 | tf_op jit(solution)/shard_map/ppermute | solution.py:255
  24.6 10.6 %collective-permute-start.3 = (bf16[144,128]{1,0:T(8,128)(2,1)S(1)}, bf16[144,128]{1,0:T(8,128)(2,1)S(1)}, u32[]{:S(2)}, u32[]{:S(2)}) collective-permute-start(bf16[144,128]{1,0:T(8,128)(2,1)S(1)} %get-tuple-element.51), channel_id=1, source_target_pairs={{0,4},{1,5},{2,6},{3,7},{4,0},{5,1},{6,2},{7,3},{8,12},{9,13},{10,... | collective-permute-start | bytes 110600 | tf_op jit(solution)/shard_map/ppermute | solution.py:258
  26.2 9.1 %collective-permute-start.4 = (bf16[144,128]{1,0:T(8,128)(2,1)S(1)}, bf16[144,128]{1,0:T(8,128)(2,1)S(1)}, u32[]{:S(2)}, u32[]{:S(2)}) collective-permute-start(bf16[144,128]{1,0:T(8,128)(2,1)S(1)} %get-tuple-element.51), channel_id=1, source_target_pairs={{0,8},{1,9},{2,10},{3,11},{4,12},{5,13},{6,14},{7,15},{8,0},{9,1},... | collective-permute-start | bytes 110600 | tf_op jit(solution)/shard_map/ppermute | solution.py:258
  28.7 8.3 %collective-permute-start.5 = (bf16[144,128]{1,0:T(8,128)(2,1)S(1)}, bf16[144,128]{1,0:T(8,128)(2,1)S(1)}, u32[]{:S(2)}, u32[]{:S(2)}) collective-permute-start(bf16[144,128]{1,0:T(8,128)(2,1)S(1)} %get-tuple-element.51), channel_id=1, source_target_pairs={{0,12},{1,13},{2,14},{3,15},{4,8},{5,9},{6,10},{7,11},{8,4},{9,5},... | collective-permute-start | bytes 110600 | tf_op jit(solution)/shard_map/ppermute | solution.py:258
  33.1 8.9 %collective-permute-start.16 = (bf16[128,512]{1,0:T(8,128)(2,1)S(1)}, bf16[128,512]{1,0:T(8,128)(2,1)S(1)}, u32[]{:S(2)}, u32[]{:S(2)}) collective-permute-start(bf16[128,512]{1,0:T(8,128)(2,1)S(1)} %slice.6), channel_id=1, source_target_pairs={{0,4},{1,5},{4,8},{5,9},{8,12},{9,13},{12,14},{13,15},{14,10},{15,... | collective-permute-start | bytes 393224 | tf_op jit(solution)/shard_map/ppermute | solution.py:255
  35.0 7.1 %collective-permute-start.17 = (bf16[128,512]{1,0:T(8,128)(2,1)S(1)}, bf16[128,512]{1,0:T(8,128)(2,1)S(1)}, u32[]{:S(2)}, u32[]{:S(2)}) collective-permute-start(bf16[128,512]{1,0:T(8,128)(2,1)S(1)} %slice.7), channel_id=1, source_target_pairs={{0,2},{1,3},{4,0},{5,1},{8,4},{9,5},{12,8},{13,9},{14,12},{15,13},... | collective-permute-start | bytes 393224 | tf_op jit(solution)/shard_map/ppermute | solution.py:255
  37.0 4.2 %collective-permute-start.6 = (bf16[144,128]{1,0:T(8,128)(2,1)S(1)}, bf16[144,128]{1,0:T(8,128)(2,1)S(1)}, u32[]{:S(2)}, u32[]{:S(2)}) collective-permute-start(bf16[144,128]{1,0:T(8,128)(2,1)S(1)} %add_convert_fusion.own_ref), channel_id=1, source_target_pairs={{0,2},{1,3},{2,0},{3,1},{4,6},{5,7},{6,4},{7,5},{8,10},{9,11},{10,... | collective-permute-start | bytes 110600 | tf_op jit(solution)/shard_map/ppermute | solution.py:258
  37.1 4.2 %collective-permute-start.7 = (bf16[144,128]{1,0:T(8,128)(2,1)S(1)}, bf16[144,128]{1,0:T(8,128)(2,1)S(1)}, u32[]{:S(2)}, u32[]{:S(2)}) collective-permute-start(bf16[144,128]{1,0:T(8,128)(2,1)S(1)} %add_convert_fusion.own_ref), channel_id=1, source_target_pairs={{0,1},{1,0},{2,3},{3,2},{4,5},{5,4},{6,7},{7,6},{8,9},{9,8},{10,11... | collective-permute-start | bytes 110600 | tf_op jit(solution)/shard_map/ppermute | solution.py:258
  37.2 4.1 %collective-permute-start.8 = (bf16[144,128]{1,0:T(8,128)(2,1)S(1)}, bf16[144,128]{1,0:T(8,128)(2,1)S(1)}, u32[]{:S(2)}, u32[]{:S(2)}) collective-permute-start(bf16[144,128]{1,0:T(8,128)(2,1)S(1)} %add_convert_fusion.own_ref), channel_id=1, source_target_pairs={{0,3},{1,2},{2,1},{3,0},{4,7},{5,6},{6,5},{7,4},{8,11},{9,10},{10,... | collective-permute-start | bytes 110600 | tf_op jit(solution)/shard_map/ppermute | solution.py:258
  39.2 2.0 %copy-start.1 = (bf16[256,512]{1,0:T(8,128)(2,1)S(1)}, bf16[256,512]{1,0:T(8,128)(2,1)}, u32[]{:S(2)}) copy-start(bf16[256,512]{1,0:T(8,128)(2,1)} %x_ref.1) | copy-start | bytes 786436
  39.2 2.0 %copy-start.5 = (bf16[512,512]{1,0:T(8,128)(2,1)S(1)}, bf16[512,512]{1,0:T(8,128)(2,1)}, u32[]{:S(2)}) copy-start(bf16[512,512]{1,0:T(8,128)(2,1)} %wo_ref.1) | copy-start | bytes 1572868
  42.9 1.6 %copy-start.3 = (bf16[512,1024]{1,0:T(8,128)(2,1)S(1)}, bf16[512,1024]{1,0:T(8,128)(2,1)}, u32[]{:S(2)}) copy-start(bf16[512,1024]{1,0:T(8,128)(2,1)} %up_ref.1) | copy-start | bytes 3145732
  42.9 1.6 %copy-start.4 = (bf16[1024,512]{1,0:T(8,128)(2,1)S(1)}, bf16[1024,512]{1,0:T(8,128)(2,1)}, u32[]{:S(2)}) copy-start(bf16[1024,512]{1,0:T(8,128)(2,1)} %down_ref.1) | copy-start | bytes 3145732
  42.9 1.6 %collective-permute-start.18 = (bf16[256,512]{1,0:T(8,128)(2,1)S(1)}, bf16[256,512]{1,0:T(8,128)(2,1)S(1)}, u32[]{:S(2)}, u32[]{:S(2)}) collective-permute-start(bf16[256,512]{1,0:T(8,128)(2,1)S(1)} %shard_map.175), channel_id=1, source_target_pairs={{0,1},{1,0},{2,3},{3,2},{4,5},{5,4},{6,7},{7,6},{8,9},{9,8},{10,11... | collective-permute-start | bytes 786440 | tf_op jit(solution)/shard_map/ppermute | solution.py:258
  (2 other events, 2.4 us)

commit v4 on v3

--- a/solution.py
+++ b/solution.py
@@ -116,7 +116,7 @@
 
 
 def kv_kernel(
-    me_ref, normed_hbm, wk_hbm, wv_hbm, omega_hbm, own_ref, near_ref, core_ref, both_ref, sums_ref,
+    normed_hbm, wk_hbm, wv_hbm, omega_hbm, own_ref, near_ref, core_ref, both_ref, sums_ref,
     normed_ref, wk_ref, wv_ref, omega_ref, normed_sem, wk_sem, wv_sem, omega_sem
 ):
     normed_copy = Fetch(normed_hbm, normed_ref, normed_sem, PIECES)
@@ -156,7 +156,8 @@
         both += lax.dot_general(f_high, v_low, dims, preferred_element_type=F32)
         block = jnp.where(left, both[:feat], both[feat:])
         sums_ref[pair] = jnp.concatenate([block, total[:, :feat], total[:, feat:], pad], axis=0)
-    mine = (me_ref[0] % 2) * 2 + (me_ref[0] // 2) % 2
+    me = lax.axis_index("blk")
+    mine = (me % 2) * 2 + (me // 2) % 2
     own_ref[...] = sums_ref[mine]
     near_ref[...] = sums_ref[mine ^ 1].astype(BF16)
     core_ref[...] = sums_ref[mine ^ 2].astype(BF16)
@@ -203,12 +204,13 @@
 
 
 def attend_kernel(
-    me_ref, x_ref, qf_ref, gate_ref, own_ref, pair_ref, core_ref, both_ref, wo_ref, total_ref, mixed_ref
+    x_ref, qf_ref, gate_ref, own_ref, pair_ref, core_ref, both_ref, wo_ref, total_ref, mixed_ref
 ):
     width = x_ref.shape[1]
     head = width // HEADS
     feat = own_ref.shape[1]
-    mine = (me_ref[0] % 2) * 2 + (me_ref[0] // 2) % 2
+    me = lax.axis_index("blk")
+    mine = (me % 2) * 2 + (me // 2) % 2
     left = lax.broadcasted_iota(jnp.int32, (feat, 2 * head), 1) < head
     ones = pair_ones(2 * feat, 2 * head).astype(BF16)
     joined = []
@@ -230,15 +232,18 @@
     mixed_ref[...] = x_ref[...].astype(F32) + total_ref[...] + dot(gated, wo_ref[...])
 
 
-def product(dense_ref, column, chunk):
+def columns(dense_ref, column, count):
     rows, tile = dense_ref.shape[1:3]
     weights = [
-        jnp.concatenate(
-            [dense_ref[column + col, row] for col in range(chunk.shape[0] // tile)], axis=1
-        )
+        jnp.concatenate([dense_ref[column + col, row] for col in range(count // tile)], axis=1)
         for row in range(rows)
     ]
-    return dot(jnp.concatenate(weights, axis=0), chunk)
+    return jnp.concatenate(weights, axis=0)
+
+
+def late_kernel(total_ref, weights_ref, upper_ref, lower_ref, out_ref):
+    rows = jnp.concatenate([upper_ref[...], lower_ref[...]], axis=0)
+    out_ref[...] = (total_ref[...] + dot(weights_ref[...], rows)).astype(out_ref.dtype)
 
 
 def solution(mesh):
@@ -300,8 +305,8 @@
         own, near, across, both = call(
             kv_kernel,
             (sds((rows, feat), F32), given, given, given),
-            [SMEM] + [HBM] * 4,
-            (me, normed, w_key, w_value, omega),
+            [HBM] * 4,
+            (normed, w_key, w_value, omega),
             [pltpu.VMEM((HEADS // 2, rows, feat), F32)]
             + buffers((normed, PIECES), (w_key, PIECES), (w_value, PIECES), (omega, 1)),
             56,
@@ -333,35 +338,39 @@
         if chips % 2 == 0:
             shifts += [chips // 2]
         home = {chip: p for p, chip in enumerate(order)}
-        table = jnp.asarray(
-            [order[(home[chip] - shift) % chips] for chip in range(chips) for shift in shifts],
-            jnp.int32,
-        )
-
-        def accumulate(matrices, totals, first, chunks, dtype=F32):
-            totals, count = list(totals), len(matrices)
-
-            def body(me_ref, table_ref, *refs):
-                for dense_ref, out, total in zip(refs, refs[-count:], totals or [None] * count):
-                    value = None
-                    if totals:
-                        value = refs[count + [t is total for t in totals].index(True)][...]
-                    place, seen = first, 0
-                    for chunk_ref in refs[count + len(totals) : -count]:
-                        chip = table_ref[(me_ref[0] // 2) * chips + place]
-                        column = chip * row_blocks + seen // tile
-                        part = product(dense_ref, column, chunk_ref[...])
+
+        def lookup(values, index):
+            return sum(jnp.where(index == i, value, 0) for i, value in enumerate(values))
+
+        def accumulate(totals, first, chunks, aside=None):
+            totals = list(totals)
+
+            def body(mine_ref, sibling_ref, *refs):
+                place_here = lookup([home[c] for c in range(chips)], lax.axis_index("blk") // 2)
+                chunk_refs = refs[len(totals) : len(totals) + len(chunks)]
+                outs = refs[len(totals) + len(chunks) :]
+
+                def weights(dense_ref, place):
+                    chip = lookup(order, lax.rem(place_here - shifts[place] + 2 * chips, chips))
+                    return columns(dense_ref, chip * row_blocks, nodes)
+
+                for i, dense_ref in enumerate((mine_ref, sibling_ref)):
+                    value = refs[i][...] if totals else None
+                    for place, chunk_ref in enumerate(chunk_refs):
+                        part = dot(weights(dense_ref, first + place), chunk_ref[...])
                         value = part if value is None else value + part
-                        seen += chunk_ref.shape[0]
-                        if seen == nodes:
-                            place, seen = place + 1, 0
-                    out[...] = value.astype(out.dtype)
-
+                    outs[i][...] = value
+                    if aside is not None:
+                        outs[2 + i][...] = weights(dense_ref, aside)
+
+            outs = [sds((nodes, width), F32)] * 2
+            if aside is not None:
+                outs += [sds((nodes, nodes), BF16)] * 2
             return call(
                 body,
-                [sds((nodes, width), dtype)] * count,
-                [SMEM] * 2 + [VMEM] * (count + len(totals) + len(chunks)),
-                (me, table, *matrices, *totals, *chunks),
+                outs,
+                [VMEM] * (2 + len(totals) + len(chunks)),
+                (dense, sibling, *totals, *chunks),
             )
 
         chunks = [message, ahead, back]
@@ -374,28 +383,29 @@
                 sibling = flip(others, 1)
             if k > 3:
                 ready = 1 + 2 * (k - 2)
-                totals = accumulate((dense, sibling), totals, used, chunks[used:ready])
+                totals = accumulate(totals, used, chunks[used:ready])
                 used = ready
                 ahead, back = after([ahead, back], totals[0])
                 chunks[-2:] = [ahead, back]
             ahead, back = step(ahead, 1), step(back, -1)
             chunks += [ahead, back]
         ready = 1 + 2 * (full - 1)
-        totals = accumulate((dense, sibling), totals, used, chunks[used:ready])
+        totals = accumulate(totals, used, chunks[used:ready])
         ahead, back = after([ahead, back], totals[0], qfeat)
         chunks[-2:] = [ahead, back]
         late = [step(ahead[: nodes // 2], 1), step(back[nodes // 2 :], -1)]
-        totals = accumulate((dense, sibling), totals, ready, chunks[ready:])
+        *totals, mine_late, sibling_late = accumulate(totals, ready, chunks[ready:], len(chunks))
+        gathered = [flip(quarter, bits) for bits in (2, 1, 3)]
         mixed = call(
             attend_kernel,
             sds((nodes, width), F32),
-            [SMEM] + [VMEM] * 9,
-            (me, features, qfeat, gate, quarter, flip(quarter, 2), flip(quarter, 1), flip(quarter, 3), w_out, totals[0]),
-        )
-        late = after(late, *totals, mixed)
-        start = len(chunks)
-        (given,) = accumulate((sibling,), totals[1:], start, late, BF16)
-        (mine,) = accumulate((dense,), [mixed], start, late)
+            [VMEM] * 9,
+            (features, qfeat, gate, quarter, *gathered, w_out, totals[0]),
+        )
+        late = after(late, *totals, *gathered)
+        late_given, late_mine = sds((nodes, width), BF16), sds((nodes, width), F32)
+        given = call(late_kernel, late_given, [VMEM] * 4, (totals[1], sibling_late, *late))
+        mine = call(late_kernel, late_mine, [VMEM] * 4, (mixed, mine_late, *late))
         theirs = flip(given, 1)
 
         def final_kernel(mine_ref, theirs_ref, gain_ref, up_ref, down_ref, out_ref):

time: 46.4 us -> 45.3 us (0.976)
  Pallas kernels: 14.9 us -> 12.6 us
  waiting for transfers between devices: 10.1 us -> 11.1 us
    pallas_call x10, Pallas kernels: 14.9 us -> 12.6 us  [call(): pl.pallas_call(body, out_shape=outs, in_specs=specs, out_specs=jax.tree.m...]
    ppermute x8, waiting for transfers between devices: 6.79 us -> 7.37 us  [step(): return lax.ppermute(value, 'blk', pairs)]
    unnamed x30 -> x28, local copies, waits for them, and re-layouts: 0.84 us -> 1.03 us
  transfers between devices with their start and end apart: 19 -> 19, of which waited for: 8 -> 9; matrix products, arithmetic and copies ran while one was open for 2% -> 2% of each run, Pallas kernels for 21% -> 18%
where the time goes in v4:
time: 45.3 us; the launch traced here: 45 us
  starting transfers between devices  18.4 us (41%)
  Pallas kernels  12.6 us (28%)
  waiting for transfers between devices  11.1 us (25%)
  local copies, waits for them, and re-layouts  1.05 us (2%)
  other arithmetic  0.94 us (2%)
  between operations  0.92 us (2%)
    pallas_call x10, Pallas kernels, call(): pl.pallas_call(body, out_shape=outs, in_specs=specs, out_specs=jax.tree.m...  12.6 us
    ppermute x8, starting transfers between devices, step(): return lax.ppermute(value, 'blk', pairs)  9.33 us
    ppermute x11, starting transfers between devices, flip(): return lax.ppermute(value, 'blk', [(i, i ^ bit) for i in range(size)])  9.04 us
    ppermute x8, waiting for transfers between devices, step(): return lax.ppermute(value, 'blk', pairs)  7.37 us
    ppermute x11, waiting for transfers between devices, flip(): return lax.ppermute(value, 'blk', [(i, i ^ bit) for i in range(size)])  3.74 us
    unnamed x28, local copies, waits for them, and re-layouts  1.03 us
    convert_element_type x1, other arithmetic, on_device(): sent = sums[-1].astype(BF16)  0.91 us
  transfers between devices with their start and end apart: 19, of which 9 were waited for; matrix products, arithmetic and copies ran while one was open for 2% of the time, Pallas kernels for 18%

profile of v4, /device:TPU:0, one launch (start us, length us, event | category | flops | bytes accessed | tf_op | source)
XLA Modules:
  0.0 45.0 jit_solution(15310826169784240997)
XLA Ops:
  0.0 2.6 %shard_map.154 = (bf16[256,512]{1,0:T(8,128)(2,1)}, bf16[256,512]{1,0:T(8,128)(2,1)}) custom-call(bf16[256,512]{1,0:T(8,128)(2,1)} %x_ref.1, f32[1,512]{1,0:T(1,128)} %bitcast.4, bf16[512,512]{1,0:T(8,128)(2,1)} %w_hbm.1), custom_call_target="tpu_custom_call" | custom-call | flops 1 | bytes 1 | tf_op jit(solution)/shard_map/pallas_call | solution.py:36
  2.6 3.0 %collective-permute-start.10 = (bf16[256,512]{1,0:T(8,128)(2,1)}, bf16[256,512]{1,0:T(8,128)(2,1)S(1)}, u32[]{:S(2)}, u32[]{:S(2)}) collective-permute-start(bf16[256,512]{1,0:T(8,128)(2,1)} %get-tuple-element.38.refs_0_), channel_id=1, source_target_pairs={{0,2},{1,3},{4,0},{5,1},{8,4},{9,5},{12,8},{13,9},{14,12},{15,13},... | collective-permute-start | bytes 786440 | tf_op jit(solution)/shard_map/ppermute | solution.py:260
  5.7 3.9 %shard_map.156 = (f32[144,128]{1,0:T(8,128)}, bf16[144,128]{1,0:T(8,128)(2,1)}, bf16[144,128]{1,0:T(8,128)(2,1)}, bf16[144,128]{1,0:T(8,128)(2,1)}) custom-call(bf16[256,512]{1,0:T(8,128)(2,1)} %get-tuple-element.30.normed_ref.normed_hbm, bf16[512,512]{1,0:T(8,128)(2,1)} %wk_hbm.1, bf16[512,512]{1,0:T(8,128)(2,1)} %wv_hbm.1, f32[64,128]{1,0:T(8,128)} %omega_hbm.1), custom_call_target="tpu_custom_call" | custom-call | flops 1 | bytes 1 | tf_op jit(solution)/shard_map/pallas_call | solution.py:36
  9.7 2.0 %collective-permute-start = (bf16[144,128]{1,0:T(8,128)(2,1)}, bf16[144,128]{1,0:T(8,128)(2,1)S(1)}, u32[]{:S(2)}, u32[]{:S(2)}) collective-permute-start(bf16[144,128]{1,0:T(8,128)(2,1)} %get-tuple-element.34.refs_2_), channel_id=1, source_target_pairs={{0,2},{1,3},{2,0},{3,1},{4,6},{5,7},{6,4},{7,5},{8,10},{9,11},{10,... | collective-permute-start | bytes 110600 | tf_op jit(solution)/shard_map/ppermute | solution.py:263
  11.6 0.2 collective-permute-start.2
  11.9 0.3 collective-permute-done.10.refs_1_
  12.2 1.8 %collective-permute-done.9.refs_0_ = bf16[256,512]{1,0:T(8,128)(2,1)S(1)} collective-permute-done((bf16[256,512]{1,0:T(8,128)(2,1)}, bf16[256,512]{1,0:T(8,128)(2,1)S(1)}, u32[]{:S(2)}, u32[]{:S(2)}) %collective-permute-start.9) | collective-permute-done | bytes 262176 | tf_op jit(solution)/shard_map/ppermute | solution.py:260
  14.0 0.8 %copy-done.10 = bf16[144,128]{1,0:T(8,128)(2,1)S(1)} copy-done((bf16[144,128]{1,0:T(8,128)(2,1)S(1)}, bf16[144,128]{1,0:T(8,128)(2,1)}, u32[]{:S(2)}) %copy-start.10) | copy-done | bytes 36888
  14.8 2.0 %collective-permute-start.12 = (bf16[256,512]{1,0:T(8,128)(2,1)S(1)}, bf16[256,512]{1,0:T(8,128)(2,1)S(1)}, u32[]{:S(2)}, u32[]{:S(2)}) collective-permute-start(bf16[256,512]{1,0:T(8,128)(2,1)S(1)} %get-tuple-element.40.refs_2_), channel_id=1, source_target_pairs={{0,2},{1,3},{4,0},{5,1},{8,4},{9,5},{12,8},{13,9},{14,12},{15,13},... | collective-permute-start | bytes 786440 | tf_op jit(solution)/shard_map/ppermute | solution.py:260
  17.5 0.9 %fusion = (bf16[144,128]{1,0:T(8,128)(2,1)S(1)}, f32[144,128]{1,0:T(8,128)S(1)}) fusion(bf16[144,128]{1,0:T(8,128)(2,1)S(1)} %collective-permute-done.2, bf16[144,128]{1,0:T(8,128)(2,1)S(1)} %collective-permute-done.1, f32[144,128]{1,0:T(8,128)} %get-tuple-element.33, bf16[144,128]{1,0:T(8,128)(2,1)S(1)} %collective-permute-done), kind=kLoop, calls=%fused_computation.2 | loop fusion | flops 129024 | bytes 294912 | tf_op jit(solution)/shard_map/convert_element_type | solution.py:319
  18.4 1.2 %shard_map.157 = (bf16[16,2,128,128]{3,2,1,0:T(8,128)(2,1)S(1)}, bf16[16,2,128,128]{3,2,1,0:T(8,128)(2,1)S(1)}) custom-call(s32[1]{0:T(128)} %bitcast.1.core_ref, s32[48]{0:T(128)S(1)} %copy-done.12, s32[48]{0:T(128)S(1)} %copy-done.13, s32[1]{0:T(128)S(6)} %copy.35.count_ref, bf16[48,128,128]{2,1,0:T(8,128)(2,1)S(1)} %copy-done, ...), custom_call_target="tpu_custom_call" | custom-call | flops 1 | bytes 1 | tf_op jit(solution)/shard_map/pallas_call | solution.py:36
  19.7 1.8 %collective-permute-done.11.refs_0_ = bf16[256,512]{1,0:T(8,128)(2,1)S(1)} collective-permute-done((bf16[256,512]{1,0:T(8,128)(2,1)S(1)}, bf16[256,512]{1,0:T(8,128)(2,1)S(1)}, u32[]{:S(2)}, u32[]{:S(2)}) %collective-permute-start.11) | collective-permute-done | bytes 262176 | tf_op jit(solution)/shard_map/ppermute | solution.py:260
  21.5 1.0 %collective-permute-done.12.refs_1_ = bf16[256,512]{1,0:T(8,128)(2,1)S(1)} collective-permute-done((bf16[256,512]{1,0:T(8,128)(2,1)S(1)}, bf16[256,512]{1,0:T(8,128)(2,1)S(1)}, u32[]{:S(2)}, u32[]{:S(2)}) %collective-permute-start.12) | collective-permute-done | bytes 262176 | tf_op jit(solution)/shard_map/ppermute | solution.py:260
  22.5 1.6 %collective-permute-start.14 = (bf16[256,512]{1,0:T(8,128)(2,1)S(1)}, bf16[256,512]{1,0:T(8,128)(2,1)S(1)}, u32[]{:S(2)}, u32[]{:S(2)}) collective-permute-start(bf16[256,512]{1,0:T(8,128)(2,1)S(1)} %get-tuple-element.43.refs_3_), channel_id=1, source_target_pairs={{0,4},{1,5},{4,8},{5,9},{8,12},{9,13},{12,14},{13,15},{14,10},{15,... | collective-permute-start | bytes 786440 | tf_op jit(solution)/shard_map/ppermute | solution.py:260
  24.1 0.4 collective-permute-start.15
  24.6 1.6 %collective-permute-start.3 = (bf16[144,128]{1,0:T(8,128)(2,1)S(1)}, bf16[144,128]{1,0:T(8,128)(2,1)S(1)}, u32[]{:S(2)}, u32[]{:S(2)}) collective-permute-start(bf16[144,128]{1,0:T(8,128)(2,1)S(1)} %get-tuple-element.55), channel_id=1, source_target_pairs={{0,4},{1,5},{2,6},{3,7},{4,0},{5,1},{6,2},{7,3},{8,12},{9,13},{10,... | collective-permute-start | bytes 110600 | tf_op jit(solution)/shard_map/ppermute | solution.py:263
  26.1 2.5 %collective-permute-start.4 = (bf16[144,128]{1,0:T(8,128)(2,1)S(1)}, bf16[144,128]{1,0:T(8,128)(2,1)S(1)}, u32[]{:S(2)}, u32[]{:S(2)}) collective-permute-start(bf16[144,128]{1,0:T(8,128)(2,1)S(1)} %get-tuple-element.55), channel_id=1, source_target_pairs={{0,8},{1,9},{2,10},{3,11},{4,12},{5,13},{6,14},{7,15},{8,0},{9,1},... | collective-permute-start | bytes 110600 | tf_op jit(solution)/shard_map/ppermute | solution.py:263
  28.7 0.3 collective-permute-start.5
  29.0 0.8 %shard_map.155 = (bf16[256,1024]{1,0:T(8,128)(2,1)S(1)}, f32[256,512]{1,0:T(8,128)S(1)}) custom-call(bf16[256,512]{1,0:T(8,128)(2,1)S(1)} %copy-done.4, bf16[512,512]{1,0:T(8,128)(2,1)S(1)} %copy-done.5, bf16[512,512]{1,0:T(8,128)(2,1)S(1)} %copy-done.6, f32[64,128]{1,0:T(8,128)S(1)} %copy-done.9), custom_call_target="tpu_custom_call" | custom-call | flops 1 | bytes 1 | tf_op jit(solution)/shard_map/pallas_call | solution.py:36
  29.8 0.8 %shard_map.160 = (f32[256,512]{1,0:T(8,128)S(1)}, f32[256,512]{1,0:T(8,128)S(1)}) custom-call(bf16[16,2,128,128]{3,2,1,0:T(8,128)(2,1)S(1)} %get-tuple-element.37.refs_3_.mine_ref, bf16[16,2,128,128]{3,2,1,0:T(8,128)(2,1)S(1)} %collective-permute-done.13.sibling_ref, bf16[256,512]{1,0:T(8,128)(2,1)S(1)} %copy-done.8, ...), custom_call_target="tpu_custom_call" | custom-call | flops 1 | bytes 1 | tf_op jit(solution)/shard_map/pallas_call | solution.py:36
  30.6 0.6 %collective-permute-done.14.refs_0_ = bf16[256,512]{1,0:T(8,128)(2,1)S(1)} collective-permute-done((bf16[256,512]{1,0:T(8,128)(2,1)S(1)}, bf16[256,512]{1,0:T(8,128)(2,1)S(1)}, u32[]{:S(2)}, u32[]{:S(2)}) %collective-permute-start.14) | collective-permute-done | bytes 262176 | tf_op jit(solution)/shard_map/ppermute | solution.py:260
  31.3 1.8 %collective-permute-done.15.refs_1_ = bf16[256,512]{1,0:T(8,128)(2,1)S(1)} collective-permute-done((bf16[256,512]{1,0:T(8,128)(2,1)S(1)}, bf16[256,512]{1,0:T(8,128)(2,1)S(1)}, u32[]{:S(2)}, u32[]{:S(2)}) %collective-permute-start.15) | collective-permute-done | bytes 262176 | tf_op jit(solution)/shard_map/ppermute | solution.py:260
  33.0 1.9 %collective-permute-start.16 = (bf16[128,512]{1,0:T(8,128)(2,1)S(1)}, bf16[128,512]{1,0:T(8,128)(2,1)S(1)}, u32[]{:S(2)}, u32[]{:S(2)}) collective-permute-start(bf16[128,512]{1,0:T(8,128)(2,1)S(1)} %slice.6), channel_id=1, source_target_pairs={{0,4},{1,5},{4,8},{5,9},{8,12},{9,13},{12,14},{13,15},{14,10},{15,... | collective-permute-start | bytes 393224 | tf_op jit(solution)/shard_map/ppermute | solution.py:260
  34.9 0.3 collective-permute-start.17
  35.2 1.8 %collective-permute-done.5 = bf16[144,128]{1,0:T(8,128)(2,1)S(1)} collective-permute-done((bf16[144,128]{1,0:T(8,128)(2,1)S(1)}, bf16[144,128]{1,0:T(8,128)(2,1)S(1)}, u32[]{:S(2)}, u32[]{:S(2)}) %collective-permute-start.5) | collective-permute-done | bytes 36896 | tf_op jit(solution)/shard_map/ppermute | solution.py:263
  37.2 2.0 %collective-permute-start.8 = (bf16[144,128]{1,0:T(8,128)(2,1)S(1)}, bf16[144,128]{1,0:T(8,128)(2,1)S(1)}, u32[]{:S(2)}, u32[]{:S(2)}) collective-permute-start(bf16[144,128]{1,0:T(8,128)(2,1)S(1)} %add_convert_fusion.own_ref), channel_id=1, source_target_pairs={{0,3},{1,2},{2,1},{3,0},{4,7},{5,6},{6,5},{7,4},{8,11},{9,10},{10,... | collective-permute-start | bytes 110600 | tf_op jit(solution)/shard_map/ppermute | solution.py:263
  39.2 0.4 shard_map.162
  39.7 1.6 %collective-permute-done.6.pair_ref.refs_4_ = bf16[144,128]{1,0:T(8,128)(2,1)S(1)} collective-permute-done((bf16[144,128]{1,0:T(8,128)(2,1)S(1)}, bf16[144,128]{1,0:T(8,128)(2,1)S(1)}, u32[]{:S(2)}, u32[]{:S(2)}) %collective-permute-start.6) | collective-permute-done | bytes 36896 | tf_op jit(solution)/shard_map/ppermute | solution.py:263
  41.5 0.3 collective-permute-start.18
  41.8 0.7 %shard_map.163.total_ref = f32[256,512]{1,0:T(8,128)S(1)} custom-call(bf16[256,512]{1,0:T(8,128)(2,1)S(1)} %copy-done.1, bf16[256,1024]{1,0:T(8,128)(2,1)S(1)} %get-tuple-element.31.refs_3_.qf_ref, f32[256,512]{1,0:T(8,128)S(1)} %get-tuple-element.32.gate_ref, bf16[144,128]{1,0:T(8,128)(2,1)S(1)} %add_convert_fusion.own_ref, ...), custom_call_target="tpu_custom_call" | custom-call | flops 1 | bytes 1 | tf_op jit(solution)/shard_map/pallas_call | solution.py:36
  42.8 0.4 collective-permute-done.18.theirs_ref
  43.3 1.6 %shard_map.167 = bf16[256,512]{1,0:T(8,128)(2,1)} custom-call(f32[256,512]{1,0:T(8,128)S(1)} %shard_map.165.mine_ref, bf16[256,512]{1,0:T(8,128)(2,1)S(1)} %collective-permute-done.18.theirs_ref, f32[1,512]{1,0:T(1,128)S(1)} %bitcast.3, bf16[512,1024]{1,0:T(8,128)(2,1)S(1)} %copy-done.2, bf16[1024,512]{1,0:T(8,128)(2,1)S(1)} %copy-done.3), custom_call_target="tpu_custom_call" | custom-call | flops 1 | bytes 1 | tf_op jit(solution)/shard_map/pallas_call | solution.py:36
  (52 shorter events, 1.1 us)
Async XLA Ops:
  0.0 18.4 %copy-start = (bf16[48,128,128]{2,1,0:T(8,128)(2,1)S(1)}, bf16[48,128,128]{2,1,0:T(8,128)(2,1)}, u32[]{:S(2)}) copy-start(bf16[48,128,128]{2,1,0:T(8,128)(2,1)} %tiles_ref.1) | copy-start | bytes 4718596
  0.0 18.4 %copy-start.12 = (s32[48]{0:T(128)S(1)}, s32[48]{0:T(128)}, u32[]{:S(2)}) copy-start(s32[48]{0:T(128)} %rows_ref.1) | copy-start | bytes 580
  0.0 18.4 %copy-start.13 = (s32[48]{0:T(128)S(1)}, s32[48]{0:T(128)}, u32[]{:S(2)}) copy-start(s32[48]{0:T(128)} %cols_ref.1) | copy-start | bytes 580
  2.6 9.6 %collective-permute-start.10 = (bf16[256,512]{1,0:T(8,128)(2,1)}, bf16[256,512]{1,0:T(8,128)(2,1)S(1)}, u32[]{:S(2)}, u32[]{:S(2)}) collective-permute-start(bf16[256,512]{1,0:T(8,128)(2,1)} %get-tuple-element.38.refs_0_), channel_id=1, source_target_pairs={{0,2},{1,3},{4,0},{5,1},{8,4},{9,5},{12,8},{13,9},{14,12},{15,13},... | collective-permute-start | bytes 786440 | tf_op jit(solution)/shard_map/ppermute | solution.py:260
  5.6 8.4 %collective-permute-start.9 = (bf16[256,512]{1,0:T(8,128)(2,1)}, bf16[256,512]{1,0:T(8,128)(2,1)S(1)}, u32[]{:S(2)}, u32[]{:S(2)}) collective-permute-start(bf16[256,512]{1,0:T(8,128)(2,1)} %get-tuple-element.38.refs_0_), channel_id=1, source_target_pairs={{0,4},{1,5},{4,8},{5,9},{8,12},{9,13},{12,14},{13,15},{14,10},{15,... | collective-permute-start | bytes 786440 | tf_op jit(solution)/shard_map/ppermute | solution.py:260
  9.7 7.8 %collective-permute-start = (bf16[144,128]{1,0:T(8,128)(2,1)}, bf16[144,128]{1,0:T(8,128)(2,1)S(1)}, u32[]{:S(2)}, u32[]{:S(2)}) collective-permute-start(bf16[144,128]{1,0:T(8,128)(2,1)} %get-tuple-element.34.refs_2_), channel_id=1, source_target_pairs={{0,2},{1,3},{2,0},{3,1},{4,6},{5,7},{6,4},{7,5},{8,10},{9,11},{10,... | collective-permute-start | bytes 110600 | tf_op jit(solution)/shard_map/ppermute | solution.py:263
  11.6 5.8 %collective-permute-start.1 = (bf16[144,128]{1,0:T(8,128)(2,1)}, bf16[144,128]{1,0:T(8,128)(2,1)S(1)}, u32[]{:S(2)}, u32[]{:S(2)}) collective-permute-start(bf16[144,128]{1,0:T(8,128)(2,1)} %get-tuple-element.35), channel_id=1, source_target_pairs={{0,1},{1,0},{2,3},{3,2},{4,5},{5,4},{6,7},{7,6},{8,9},{9,8},{10,11... | collective-permute-start | bytes 110600 | tf_op jit(solution)/shard_map/ppermute | solution.py:263
  11.6 5.8 %collective-permute-start.2 = (bf16[144,128]{1,0:T(8,128)(2,1)}, bf16[144,128]{1,0:T(8,128)(2,1)S(1)}, u32[]{:S(2)}, u32[]{:S(2)}) collective-permute-start(bf16[144,128]{1,0:T(8,128)(2,1)} %get-tuple-element.36), channel_id=1, source_target_pairs={{0,3},{1,2},{2,1},{3,0},{4,7},{5,6},{6,5},{7,4},{8,11},{9,10},{10,... | collective-permute-start | bytes 110600 | tf_op jit(solution)/shard_map/ppermute | solution.py:263
  14.8 6.8 %collective-permute-start.11 = (bf16[256,512]{1,0:T(8,128)(2,1)S(1)}, bf16[256,512]{1,0:T(8,128)(2,1)S(1)}, u32[]{:S(2)}, u32[]{:S(2)}) collective-permute-start(bf16[256,512]{1,0:T(8,128)(2,1)S(1)} %get-tuple-element.39.refs_1_), channel_id=1, source_target_pairs={{0,4},{1,5},{4,8},{5,9},{8,12},{9,13},{12,14},{13,15},{14,10},{15,... | collective-permute-start | bytes 786440 | tf_op jit(solution)/shard_map/ppermute | solution.py:260
  14.8 7.8 %collective-permute-start.12 = (bf16[256,512]{1,0:T(8,128)(2,1)S(1)}, bf16[256,512]{1,0:T(8,128)(2,1)S(1)}, u32[]{:S(2)}, u32[]{:S(2)}) collective-permute-start(bf16[256,512]{1,0:T(8,128)(2,1)S(1)} %get-tuple-element.40.refs_2_), channel_id=1, source_target_pairs={{0,2},{1,3},{4,0},{5,1},{8,4},{9,5},{12,8},{13,9},{14,12},{15,13},... | collective-permute-start | bytes 786440 | tf_op jit(solution)/shard_map/ppermute | solution.py:260
  19.6 9.3 %copy-start.4 = (bf16[256,512]{1,0:T(8,128)(2,1)S(1)}, bf16[256,512]{1,0:T(8,128)(2,1)}, u32[]{:S(2)}) copy-start(bf16[256,512]{1,0:T(8,128)(2,1)} %get-tuple-element.30.normed_ref.normed_hbm) | copy-start | bytes 786436
  19.6 9.3 %copy-start.5 = (bf16[512,512]{1,0:T(8,128)(2,1)S(1)}, bf16[512,512]{1,0:T(8,128)(2,1)}, u32[]{:S(2)}) copy-start(bf16[512,512]{1,0:T(8,128)(2,1)} %wq_ref.1) | copy-start | bytes 1572868
  19.7 9.3 %copy-start.6 = (bf16[512,512]{1,0:T(8,128)(2,1)S(1)}, bf16[512,512]{1,0:T(8,128)(2,1)}, u32[]{:S(2)}) copy-start(bf16[512,512]{1,0:T(8,128)(2,1)} %wg_ref.1) | copy-start | bytes 1572868
  19.7 9.3 %copy-start.9 = (f32[64,128]{1,0:T(8,128)S(1)}, f32[64,128]{1,0:T(8,128)}, u32[]{:S(2)}) copy-start(f32[64,128]{1,0:T(8,128)} %omega_hbm.1) | copy-start | bytes 98308
  22.5 7.3 %copy-start.8 = (bf16[256,512]{1,0:T(8,128)(2,1)S(1)}, bf16[256,512]{1,0:T(8,128)(2,1)}, u32[]{:S(2)}) copy-start(bf16[256,512]{1,0:T(8,128)(2,1)} %get-tuple-element.38.refs_0_) | copy-start | bytes 786436
  22.5 6.1 %collective-permute-start.13 = (bf16[16,2,128,128]{3,2,1,0:T(8,128)(2,1)S(1)}, bf16[16,2,128,128]{3,2,1,0:T(8,128)(2,1)S(1)}, u32[]{:S(2)}, u32[]{:S(2)}) collective-permute-start(bf16[16,2,128,128]{3,2,1,0:T(8,128)(2,1)S(1)} %get-tuple-element.42), channel_id=1, source_target_pairs={{0,1},{1,0},{2,3},{3,2},{4,5},{5,4},{6,7},{7,6},{8,9},{9,8},{10,11... | collective-permute-start | bytes 3145736 | tf_op jit(solution)/shard_map/ppermute | solution.py:263
  22.5 8.7 %collective-permute-start.14 = (bf16[256,512]{1,0:T(8,128)(2,1)S(1)}, bf16[256,512]{1,0:T(8,128)(2,1)S(1)}, u32[]{:S(2)}, u32[]{:S(2)}) collective-permute-start(bf16[256,512]{1,0:T(8,128)(2,1)S(1)} %get-tuple-element.43.refs_3_), channel_id=1, source_target_pairs={{0,4},{1,5},{4,8},{5,9},{8,12},{9,13},{12,14},{13,15},{14,10},{15,... | collective-permute-start | bytes 786440 | tf_op jit(solution)/shard_map/ppermute | solution.py:260
  24.1 8.9 %collective-permute-start.15 = (bf16[256,512]{1,0:T(8,128)(2,1)S(1)}, bf16[256,512]{1,0:T(8,128)(2,1)S(1)}, u32[]{:S(2)}, u32[]{:S(2)}) collective-permute-start(bf16[256,512]{1,0:T(8,128)(2,1)S(1)} %get-tuple-element.44.refs_4_), channel_id=1, source_target_pairs={{0,2},{1,3},{4,0},{5,1},{8,4},{9,5},{12,8},{13,9},{14,12},{15,13},... | collective-permute-start | bytes 786440 | tf_op jit(solution)/shard_map/ppermute | solution.py:260
  24.6 10.6 %collective-permute-start.3 = (bf16[144,128]{1,0:T(8,128)(2,1)S(1)}, bf16[144,128]{1,0:T(8,128)(2,1)S(1)}, u32[]{:S(2)}, u32[]{:S(2)}) collective-permute-start(bf16[144,128]{1,0:T(8,128)(2,1)S(1)} %get-tuple-element.55), channel_id=1, source_target_pairs={{0,4},{1,5},{2,6},{3,7},{4,0},{5,1},{6,2},{7,3},{8,12},{9,13},{10,... | collective-permute-start | bytes 110600 | tf_op jit(solution)/shard_map/ppermute | solution.py:263
  26.1 9.1 %collective-permute-start.4 = (bf16[144,128]{1,0:T(8,128)(2,1)S(1)}, bf16[144,128]{1,0:T(8,128)(2,1)S(1)}, u32[]{:S(2)}, u32[]{:S(2)}) collective-permute-start(bf16[144,128]{1,0:T(8,128)(2,1)S(1)} %get-tuple-element.55), channel_id=1, source_target_pairs={{0,8},{1,9},{2,10},{3,11},{4,12},{5,13},{6,14},{7,15},{8,0},{9,1},... | collective-permute-start | bytes 110600 | tf_op jit(solution)/shard_map/ppermute | solution.py:263
  28.7 8.3 %collective-permute-start.5 = (bf16[144,128]{1,0:T(8,128)(2,1)S(1)}, bf16[144,128]{1,0:T(8,128)(2,1)S(1)}, u32[]{:S(2)}, u32[]{:S(2)}) collective-permute-start(bf16[144,128]{1,0:T(8,128)(2,1)S(1)} %get-tuple-element.55), channel_id=1, source_target_pairs={{0,12},{1,13},{2,14},{3,15},{4,8},{5,9},{6,10},{7,11},{8,4},{9,5},... | collective-permute-start | bytes 110600 | tf_op jit(solution)/shard_map/ppermute | solution.py:263
  33.0 8.2 %collective-permute-start.16 = (bf16[128,512]{1,0:T(8,128)(2,1)S(1)}, bf16[128,512]{1,0:T(8,128)(2,1)S(1)}, u32[]{:S(2)}, u32[]{:S(2)}) collective-permute-start(bf16[128,512]{1,0:T(8,128)(2,1)S(1)} %slice.6), channel_id=1, source_target_pairs={{0,4},{1,5},{4,8},{5,9},{8,12},{9,13},{12,14},{13,15},{14,10},{15,... | collective-permute-start | bytes 393224 | tf_op jit(solution)/shard_map/ppermute | solution.py:260
  34.9 6.4 %collective-permute-start.17 = (bf16[128,512]{1,0:T(8,128)(2,1)S(1)}, bf16[128,512]{1,0:T(8,128)(2,1)S(1)}, u32[]{:S(2)}, u32[]{:S(2)}) collective-permute-start(bf16[128,512]{1,0:T(8,128)(2,1)S(1)} %slice.7), channel_id=1, source_target_pairs={{0,2},{1,3},{4,0},{5,1},{8,4},{9,5},{12,8},{13,9},{14,12},{15,13},... | collective-permute-start | bytes 393224 | tf_op jit(solution)/shard_map/ppermute | solution.py:260
  37.0 4.2 %collective-permute-start.6 = (bf16[144,128]{1,0:T(8,128)(2,1)S(1)}, bf16[144,128]{1,0:T(8,128)(2,1)S(1)}, u32[]{:S(2)}, u32[]{:S(2)}) collective-permute-start(bf16[144,128]{1,0:T(8,128)(2,1)S(1)} %add_convert_fusion.own_ref), channel_id=1, source_target_pairs={{0,2},{1,3},{2,0},{3,1},{4,6},{5,7},{6,4},{7,5},{8,10},{9,11},{10,... | collective-permute-start | bytes 110600 | tf_op jit(solution)/shard_map/ppermute | solution.py:263
  37.1 4.2 %collective-permute-start.7 = (bf16[144,128]{1,0:T(8,128)(2,1)S(1)}, bf16[144,128]{1,0:T(8,128)(2,1)S(1)}, u32[]{:S(2)}, u32[]{:S(2)}) collective-permute-start(bf16[144,128]{1,0:T(8,128)(2,1)S(1)} %add_convert_fusion.own_ref), channel_id=1, source_target_pairs={{0,1},{1,0},{2,3},{3,2},{4,5},{5,4},{6,7},{7,6},{8,9},{9,8},{10,11... | collective-permute-start | bytes 110600 | tf_op jit(solution)/shard_map/ppermute | solution.py:263
  37.2 4.1 %collective-permute-start.8 = (bf16[144,128]{1,0:T(8,128)(2,1)S(1)}, bf16[144,128]{1,0:T(8,128)(2,1)S(1)}, u32[]{:S(2)}, u32[]{:S(2)}) collective-permute-start(bf16[144,128]{1,0:T(8,128)(2,1)S(1)} %add_convert_fusion.own_ref), channel_id=1, source_target_pairs={{0,3},{1,2},{2,1},{3,0},{4,7},{5,6},{6,5},{7,4},{8,11},{9,10},{10,... | collective-permute-start | bytes 110600 | tf_op jit(solution)/shard_map/ppermute | solution.py:263
  39.7 2.1 %copy-start.1 = (bf16[256,512]{1,0:T(8,128)(2,1)S(1)}, bf16[256,512]{1,0:T(8,128)(2,1)}, u32[]{:S(2)}) copy-start(bf16[256,512]{1,0:T(8,128)(2,1)} %x_ref.1) | copy-start | bytes 786436
  39.7 2.1 %copy-start.7 = (bf16[512,512]{1,0:T(8,128)(2,1)S(1)}, bf16[512,512]{1,0:T(8,128)(2,1)}, u32[]{:S(2)}) copy-start(bf16[512,512]{1,0:T(8,128)(2,1)} %wo_ref.1) | copy-start | bytes 1572868
  41.5 1.6 %collective-permute-start.18 = (bf16[256,512]{1,0:T(8,128)(2,1)S(1)}, bf16[256,512]{1,0:T(8,128)(2,1)S(1)}, u32[]{:S(2)}, u32[]{:S(2)}) collective-permute-start(bf16[256,512]{1,0:T(8,128)(2,1)S(1)} %shard_map.166), channel_id=1, source_target_pairs={{0,1},{1,0},{2,3},{3,2},{4,5},{5,4},{6,7},{7,6},{8,9},{9,8},{10,11... | collective-permute-start | bytes 786440 | tf_op jit(solution)/shard_map/ppermute | solution.py:263
  41.8 1.3 %copy-start.2 = (bf16[512,1024]{1,0:T(8,128)(2,1)S(1)}, bf16[512,1024]{1,0:T(8,128)(2,1)}, u32[]{:S(2)}) copy-start(bf16[512,1024]{1,0:T(8,128)(2,1)} %up_ref.1) | copy-start | bytes 3145732
  41.8 1.5 %copy-start.3 = (bf16[1024,512]{1,0:T(8,128)(2,1)S(1)}, bf16[1024,512]{1,0:T(8,128)(2,1)}, u32[]{:S(2)}) copy-start(bf16[1024,512]{1,0:T(8,128)(2,1)} %down_ref.1) | copy-start | bytes 3145732
  41.8 1.5 %copy-start.11 = (f32[512]{0:T(512)S(1)}, f32[512]{0:T(512)}, u32[]{:S(2)}) copy-start(f32[512]{0:T(512)} %param.29) | copy-start | bytes 6148
  (1 other events, 0.8 us)

commit v5 on v4

--- a/solution.py
+++ b/solution.py
@@ -37,7 +37,7 @@
         body,
         out_shape=outs,
         in_specs=specs,
-        out_specs=jax.tree.map(lambda _: VMEM, outs),
+        out_specs=jax.tree.map(lambda o: SMEM if o.shape == (1,) else VMEM, outs),
         scratch_shapes=scratch,
         compiler_params=pltpu.CompilerParams(vmem_limit_bytes=int(limit * 2**20)),
         cost_estimate=pl.CostEstimate(flops=1, bytes_accessed=1, transcendentals=0),
@@ -49,7 +49,7 @@
     return pl.pallas_call(
         lambda *refs: None,
         out_shape=[sds(v.shape, v.dtype) for v in values],
-        in_specs=[any_space] * (len(values) + len(others)),
+        in_specs=[SMEM if v.shape == (1,) else any_space for v in (*values, *others)],
         out_specs=[any_space] * len(values),
         input_output_aliases={i: i for i in range(len(values))},
         compiler_params=pltpu.CompilerParams(vmem_limit_bytes=2**20),
@@ -116,7 +116,7 @@
 
 
 def kv_kernel(
-    normed_hbm, wk_hbm, wv_hbm, omega_hbm, own_ref, near_ref, core_ref, both_ref, sums_ref,
+    normed_hbm, wk_hbm, wv_hbm, omega_hbm, own_ref, near_ref, core_ref, both_ref, done_ref, sums_ref,
     normed_ref, wk_ref, wv_ref, omega_ref, normed_sem, wk_sem, wv_sem, omega_sem
 ):
     normed_copy = Fetch(normed_hbm, normed_ref, normed_sem, PIECES)
@@ -162,6 +162,7 @@
     near_ref[...] = sums_ref[mine ^ 1].astype(BF16)
     core_ref[...] = sums_ref[mine ^ 2].astype(BF16)
     both_ref[...] = sums_ref[mine ^ 3].astype(BF16)
+    done_ref[0] = mine
 
 
 def query_kernel(normed_ref, wq_ref, wg_ref, omega_ref, qf_ref, gate_ref):
@@ -302,20 +303,20 @@
 
         rows = feat + 16
         given = sds((rows, feat), BF16)
-        own, near, across, both = call(
+        own, near, across, both, done = call(
             kv_kernel,
-            (sds((rows, feat), F32), given, given, given),
+            (sds((rows, feat), F32), given, given, given, sds((1,), jnp.int32)),
             [HBM] * 4,
             (normed, w_key, w_value, omega),
             [pltpu.VMEM((HEADS // 2, rows, feat), F32)]
             + buffers((normed, PIECES), (w_key, PIECES), (w_value, PIECES), (omega, 1)),
             56,
         )
-        ahead, back = after([ahead, back], near)
+        ahead, back = after([ahead, back], done)
         sums = [sum((flip(v, b).astype(F32) for v, b in ((near, 2), (across, 1), (both, 3))), own)]
         bit = 4
         while bit < size:
-            hops = [bit, 2 * bit, 3 * bit] if 2 * bit < size else [bit]
+            hops = [3 * bit, 2 * bit, bit] if 2 * bit < size else [bit]
             sent = sums[-1].astype(BF16)
             sums.append(sum((flip(sent, hop).astype(F32) for hop in hops), sums[-1]))
             bit *= 4
@@ -391,7 +392,7 @@
             chunks += [ahead, back]
         ready = 1 + 2 * (full - 1)
         totals = accumulate(totals, used, chunks[used:ready])
-        ahead, back = after([ahead, back], totals[0], qfeat)
+        ahead, back = after([ahead, back], qfeat, totals[0])
         chunks[-2:] = [ahead, back]
         late = [step(ahead[: nodes // 2], 1), step(back[nodes // 2 :], -1)]
         *totals, mine_late, sibling_late = accumulate(totals, ready, chunks[ready:], len(chunks))

time: 45.3 us -> 44.9 us (level)
  local copies, waits for them, and re-layouts: 1.05 us -> 0.28 us
  Pallas kernels: 12.6 us -> 13.1 us
    unnamed x28 -> x26, local copies, waits for them, and re-layouts: 1.03 us -> 0.26 us
    pallas_call x4, Pallas kernels: 0.01 us -> 0.62 us  [after(): pl.pallas_call(lambda *refs: None, out_shape=[sds(v.shape, v.dtype) for v...]
    ppermute x11, waiting for transfers between devices: 3.74 us -> 3.25 us  [flip(): return lax.ppermute(value, 'blk', [(i, i ^ bit) for i in range(size)])]
  transfers between devices with their start and end apart: 19 -> 19, of which waited for: 9 -> 10; matrix products, arithmetic and copies ran while one was open for 2% -> 2% of each run, Pallas kernels for 18% -> 19%
where the time goes in v5:
time: 44.9 us; the launch traced here: 44.6 us
  starting transfers between devices  18.7 us (42%)
  Pallas kernels  13.1 us (29%)
  waiting for transfers between devices  10.7 us (24%)
  other arithmetic  0.94 us (2%)
  between operations  0.94 us (2%)
    pallas_call x10, Pallas kernels, call(): pl.pallas_call(body, out_shape=outs, in_specs=specs, out_specs=jax.tree.m...  12.5 us
    ppermute x8, starting transfers between devices, step(): return lax.ppermute(value, 'blk', pairs)  9.68 us
    ppermute x11, starting transfers between devices, flip(): return lax.ppermute(value, 'blk', [(i, i ^ bit) for i in range(size)])  9.04 us
    ppermute x8, waiting for transfers between devices, step(): return lax.ppermute(value, 'blk', pairs)  7.43 us
    ppermute x11, waiting for transfers between devices, flip(): return lax.ppermute(value, 'blk', [(i, i ^ bit) for i in range(size)])  3.25 us
    convert_element_type x1, other arithmetic, on_device(): sent = sums[-1].astype(BF16)  0.91 us
  transfers between devices with their start and end apart: 19, of which 10 were waited for; matrix products, arithmetic and copies ran while one was open for 2% of the time, Pallas kernels for 19%

profile of v5, /device:TPU:0, one launch (start us, length us, event | category | flops | bytes accessed | tf_op | source)
XLA Modules:
  0.0 44.6 jit_solution(17937047213543367881)
XLA Ops:
  0.0 2.6 %shard_map.154 = (bf16[256,512]{1,0:T(8,128)(2,1)}, bf16[256,512]{1,0:T(8,128)(2,1)}) custom-call(bf16[256,512]{1,0:T(8,128)(2,1)} %x_ref.1, f32[1,512]{1,0:T(1,128)} %bitcast.4, bf16[512,512]{1,0:T(8,128)(2,1)} %w_hbm.1), custom_call_target="tpu_custom_call" | custom-call | flops 1 | bytes 1 | tf_op jit(solution)/shard_map/pallas_call | solution.py:36
  2.6 3.0 %collective-permute-start.10 = (bf16[256,512]{1,0:T(8,128)(2,1)}, bf16[256,512]{1,0:T(8,128)(2,1)S(1)}, u32[]{:S(2)}, u32[]{:S(2)}) collective-permute-start(bf16[256,512]{1,0:T(8,128)(2,1)} %get-tuple-element.39.refs_0_), channel_id=1, source_target_pairs={{0,2},{1,3},{4,0},{5,1},{8,4},{9,5},{12,8},{13,9},{14,12},{15,13},... | collective-permute-start | bytes 786440 | tf_op jit(solution)/shard_map/ppermute | solution.py:261
  5.7 3.9 %shard_map.156 = (f32[144,128]{1,0:T(8,128)}, bf16[144,128]{1,0:T(8,128)(2,1)}, bf16[144,128]{1,0:T(8,128)(2,1)}, bf16[144,128]{1,0:T(8,128)(2,1)}, s32[1]{0:T(128)}) custom-call(bf16[256,512]{1,0:T(8,128)(2,1)} %get-tuple-element.31.normed_ref.normed_hbm, bf16[512,512]{1,0:T(8,128)(2,1)} %wk_hbm.1, bf16[512,512]{1,0:T(8,128)(2,1)} %wv_hbm.1, ...), custom_call_target="tpu_custom_call" | custom-call | flops 1 | bytes 1 | tf_op jit(solution)/shard_map/pallas_call | solution.py:36
  9.7 2.0 %collective-permute-start = (bf16[144,128]{1,0:T(8,128)(2,1)}, bf16[144,128]{1,0:T(8,128)(2,1)S(1)}, u32[]{:S(2)}, u32[]{:S(2)}) collective-permute-start(bf16[144,128]{1,0:T(8,128)(2,1)} %get-tuple-element.35), channel_id=1, source_target_pairs={{0,2},{1,3},{2,0},{3,1},{4,6},{5,7},{6,4},{7,5},{8,10},{9,11},{10,... | collective-permute-start | bytes 110600 | tf_op jit(solution)/shard_map/ppermute | solution.py:264
  11.6 0.2 collective-permute-start.2
  11.9 0.3 collective-permute-done.10.refs_1_
  12.2 1.8 %collective-permute-done.9.refs_0_ = bf16[256,512]{1,0:T(8,128)(2,1)S(1)} collective-permute-done((bf16[256,512]{1,0:T(8,128)(2,1)}, bf16[256,512]{1,0:T(8,128)(2,1)S(1)}, u32[]{:S(2)}, u32[]{:S(2)}) %collective-permute-start.9) | collective-permute-done | bytes 262176 | tf_op jit(solution)/shard_map/ppermute | solution.py:261
  14.0 0.6 %shard_map.158 = (bf16[256,512]{1,0:T(8,128)(2,1)S(1)}, bf16[256,512]{1,0:T(8,128)(2,1)S(1)}) custom-call(bf16[256,512]{1,0:T(8,128)(2,1)S(1)} %collective-permute-done.9.refs_0_, bf16[256,512]{1,0:T(8,128)(2,1)S(1)} %collective-permute-done.10.refs_1_, s32[1]{0:T(128)} %get-tuple-element.40.refs_2_), custom_call_target="tpu_custom_call", output_to_operand_aliasing={{0}: (0, {}), {1}: (1, {})} | custom-call | flops 1 | bytes 1 | tf_op jit(solution)/shard_map/pallas_call | solution.py:49
  14.7 2.0 %collective-permute-start.12 = (bf16[256,512]{1,0:T(8,128)(2,1)S(1)}, bf16[256,512]{1,0:T(8,128)(2,1)S(1)}, u32[]{:S(2)}, u32[]{:S(2)}) collective-permute-start(bf16[256,512]{1,0:T(8,128)(2,1)S(1)} %get-tuple-element.42.refs_2_), channel_id=1, source_target_pairs={{0,2},{1,3},{4,0},{5,1},{8,4},{9,5},{12,8},{13,9},{14,12},{15,13},... | collective-permute-start | bytes 786440 | tf_op jit(solution)/shard_map/ppermute | solution.py:261
  17.4 0.9 %fusion = (bf16[144,128]{1,0:T(8,128)(2,1)S(1)}, f32[144,128]{1,0:T(8,128)S(1)}) fusion(bf16[144,128]{1,0:T(8,128)(2,1)S(1)} %collective-permute-done.2, bf16[144,128]{1,0:T(8,128)(2,1)S(1)} %collective-permute-done.1, f32[144,128]{1,0:T(8,128)} %get-tuple-element.34, bf16[144,128]{1,0:T(8,128)(2,1)S(1)} %collective-permute-done), kind=kLoop, calls=%fused_computation.2 | loop fusion | flops 129024 | bytes 294912 | tf_op jit(solution)/shard_map/convert_element_type | solution.py:320
  18.3 1.1 %shard_map.157 = (bf16[16,2,128,128]{3,2,1,0:T(8,128)(2,1)S(1)}, bf16[16,2,128,128]{3,2,1,0:T(8,128)(2,1)S(1)}) custom-call(s32[1]{0:T(128)} %bitcast.1.core_ref, s32[48]{0:T(128)S(1)} %copy-done.11, s32[48]{0:T(128)S(1)} %copy-done.12, s32[1]{0:T(128)S(6)} %copy.35.count_ref, bf16[48,128,128]{2,1,0:T(8,128)(2,1)S(1)} %copy-done, ...), custom_call_target="tpu_custom_call" | custom-call | flops 1 | bytes 1 | tf_op jit(solution)/shard_map/pallas_call | solution.py:36
  19.5 2.1 %collective-permute-done.11.refs_0_ = bf16[256,512]{1,0:T(8,128)(2,1)S(1)} collective-permute-done((bf16[256,512]{1,0:T(8,128)(2,1)S(1)}, bf16[256,512]{1,0:T(8,128)(2,1)S(1)}, u32[]{:S(2)}, u32[]{:S(2)}) %collective-permute-start.11) | collective-permute-done | bytes 262176 | tf_op jit(solution)/shard_map/ppermute | solution.py:261
  21.5 0.9 %collective-permute-done.12.refs_1_ = bf16[256,512]{1,0:T(8,128)(2,1)S(1)} collective-permute-done((bf16[256,512]{1,0:T(8,128)(2,1)S(1)}, bf16[256,512]{1,0:T(8,128)(2,1)S(1)}, u32[]{:S(2)}, u32[]{:S(2)}) %collective-permute-start.12) | collective-permute-done | bytes 262176 | tf_op jit(solution)/shard_map/ppermute | solution.py:261
  22.5 1.6 %collective-permute-start.14 = (bf16[256,512]{1,0:T(8,128)(2,1)S(1)}, bf16[256,512]{1,0:T(8,128)(2,1)S(1)}, u32[]{:S(2)}, u32[]{:S(2)}) collective-permute-start(bf16[256,512]{1,0:T(8,128)(2,1)S(1)} %get-tuple-element.45.refs_3_), channel_id=1, source_target_pairs={{0,4},{1,5},{4,8},{5,9},{8,12},{9,13},{12,14},{13,15},{14,10},{15,... | collective-permute-start | bytes 786440 | tf_op jit(solution)/shard_map/ppermute | solution.py:261
  24.0 0.4 %collective-permute-start.15 = (bf16[256,512]{1,0:T(8,128)(2,1)S(1)}, bf16[256,512]{1,0:T(8,128)(2,1)S(1)}, u32[]{:S(2)}, u32[]{:S(2)}) collective-permute-start(bf16[256,512]{1,0:T(8,128)(2,1)S(1)} %get-tuple-element.46.refs_4_), channel_id=1, source_target_pairs={{0,2},{1,3},{4,0},{5,1},{8,4},{9,5},{12,8},{13,9},{14,12},{15,13},... | collective-permute-start | bytes 786440 | tf_op jit(solution)/shard_map/ppermute | solution.py:261
  24.5 3.5 %collective-permute-start.3 = (bf16[144,128]{1,0:T(8,128)(2,1)S(1)}, bf16[144,128]{1,0:T(8,128)(2,1)S(1)}, u32[]{:S(2)}, u32[]{:S(2)}) collective-permute-start(bf16[144,128]{1,0:T(8,128)(2,1)S(1)} %get-tuple-element.57), channel_id=1, source_target_pairs={{0,12},{1,13},{2,14},{3,15},{4,8},{5,9},{6,10},{7,11},{8,4},{9,5},... | collective-permute-start | bytes 110600 | tf_op jit(solution)/shard_map/ppermute | solution.py:264
  28.0 0.8 %collective-permute-start.5 = (bf16[144,128]{1,0:T(8,128)(2,1)S(1)}, bf16[144,128]{1,0:T(8,128)(2,1)S(1)}, u32[]{:S(2)}, u32[]{:S(2)}) collective-permute-start(bf16[144,128]{1,0:T(8,128)(2,1)S(1)} %get-tuple-element.57), channel_id=1, source_target_pairs={{0,4},{1,5},{2,6},{3,7},{4,0},{5,1},{6,2},{7,3},{8,12},{9,13},{10,... | collective-permute-start | bytes 110600 | tf_op jit(solution)/shard_map/ppermute | solution.py:264
  28.9 0.8 %shard_map.155 = (bf16[256,1024]{1,0:T(8,128)(2,1)S(1)}, f32[256,512]{1,0:T(8,128)S(1)}) custom-call(bf16[256,512]{1,0:T(8,128)(2,1)S(1)} %copy-done.4, bf16[512,512]{1,0:T(8,128)(2,1)S(1)} %copy-done.5, bf16[512,512]{1,0:T(8,128)(2,1)S(1)} %copy-done.6, f32[64,128]{1,0:T(8,128)S(1)} %copy-done.9), custom_call_target="tpu_custom_call" | custom-call | flops 1 | bytes 1 | tf_op jit(solution)/shard_map/pallas_call | solution.py:36
  29.7 0.8 %shard_map.160 = (f32[256,512]{1,0:T(8,128)S(1)}, f32[256,512]{1,0:T(8,128)S(1)}) custom-call(bf16[16,2,128,128]{3,2,1,0:T(8,128)(2,1)S(1)} %get-tuple-element.38.refs_3_.mine_ref, bf16[16,2,128,128]{3,2,1,0:T(8,128)(2,1)S(1)} %collective-permute-done.13.sibling_ref, bf16[256,512]{1,0:T(8,128)(2,1)S(1)} %copy-done.8, ...), custom_call_target="tpu_custom_call" | custom-call | flops 1 | bytes 1 | tf_op jit(solution)/shard_map/pallas_call | solution.py:36
  30.5 0.6 %collective-permute-done.14.refs_0_ = bf16[256,512]{1,0:T(8,128)(2,1)S(1)} collective-permute-done((bf16[256,512]{1,0:T(8,128)(2,1)S(1)}, bf16[256,512]{1,0:T(8,128)(2,1)S(1)}, u32[]{:S(2)}, u32[]{:S(2)}) %collective-permute-start.14) | collective-permute-done | bytes 262176 | tf_op jit(solution)/shard_map/ppermute | solution.py:261
  31.2 1.7 %collective-permute-done.15.refs_1_ = bf16[256,512]{1,0:T(8,128)(2,1)S(1)} collective-permute-done((bf16[256,512]{1,0:T(8,128)(2,1)S(1)}, bf16[256,512]{1,0:T(8,128)(2,1)S(1)}, u32[]{:S(2)}, u32[]{:S(2)}) %collective-permute-start.15) | collective-permute-done | bytes 262176 | tf_op jit(solution)/shard_map/ppermute | solution.py:261
  32.9 2.4 %collective-permute-start.16 = (bf16[128,512]{1,0:T(8,128)(2,1)S(1)}, bf16[128,512]{1,0:T(8,128)(2,1)S(1)}, u32[]{:S(2)}, u32[]{:S(2)}) collective-permute-start(bf16[128,512]{1,0:T(8,128)(2,1)S(1)} %slice.6), channel_id=1, source_target_pairs={{0,4},{1,5},{4,8},{5,9},{8,12},{9,13},{12,14},{13,15},{14,10},{15,... | collective-permute-start | bytes 393224 | tf_op jit(solution)/shard_map/ppermute | solution.py:261
  35.3 0.6 %collective-permute-done.3 = bf16[144,128]{1,0:T(8,128)(2,1)S(1)} collective-permute-done((bf16[144,128]{1,0:T(8,128)(2,1)S(1)}, bf16[144,128]{1,0:T(8,128)(2,1)S(1)}, u32[]{:S(2)}, u32[]{:S(2)}) %collective-permute-start.3) | collective-permute-done | bytes 36896 | tf_op jit(solution)/shard_map/ppermute | solution.py:264
  35.9 0.7 %collective-permute-done.4 = bf16[144,128]{1,0:T(8,128)(2,1)S(1)} collective-permute-done((bf16[144,128]{1,0:T(8,128)(2,1)S(1)}, bf16[144,128]{1,0:T(8,128)(2,1)S(1)}, u32[]{:S(2)}, u32[]{:S(2)}) %collective-permute-start.4) | collective-permute-done | bytes 36896 | tf_op jit(solution)/shard_map/ppermute | solution.py:264
  36.9 2.0 %collective-permute-start.8 = (bf16[144,128]{1,0:T(8,128)(2,1)S(1)}, bf16[144,128]{1,0:T(8,128)(2,1)S(1)}, u32[]{:S(2)}, u32[]{:S(2)}) collective-permute-start(bf16[144,128]{1,0:T(8,128)(2,1)S(1)} %add_convert_fusion.own_ref), channel_id=1, source_target_pairs={{0,3},{1,2},{2,1},{3,0},{4,7},{5,6},{6,5},{7,4},{8,11},{9,10},{10,... | collective-permute-start | bytes 110600 | tf_op jit(solution)/shard_map/ppermute | solution.py:264
  38.9 0.4 shard_map.162
  39.4 1.6 %collective-permute-done.6.pair_ref.refs_4_ = bf16[144,128]{1,0:T(8,128)(2,1)S(1)} collective-permute-done((bf16[144,128]{1,0:T(8,128)(2,1)S(1)}, bf16[144,128]{1,0:T(8,128)(2,1)S(1)}, u32[]{:S(2)}, u32[]{:S(2)}) %collective-permute-start.6) | collective-permute-done | bytes 36896 | tf_op jit(solution)/shard_map/ppermute | solution.py:264
  41.2 0.3 collective-permute-start.18
  41.5 0.7 %shard_map.163.total_ref = f32[256,512]{1,0:T(8,128)S(1)} custom-call(bf16[256,512]{1,0:T(8,128)(2,1)S(1)} %copy-done.1, bf16[256,1024]{1,0:T(8,128)(2,1)S(1)} %get-tuple-element.32.refs_2_.qf_ref, f32[256,512]{1,0:T(8,128)S(1)} %get-tuple-element.33.gate_ref, bf16[144,128]{1,0:T(8,128)(2,1)S(1)} %add_convert_fusion.own_ref, ...), custom_call_target="tpu_custom_call" | custom-call | flops 1 | bytes 1 | tf_op jit(solution)/shard_map/pallas_call | solution.py:36
  42.2 0.2 shard_map.165.mine_ref
  42.5 0.3 collective-permute-done.18.theirs_ref
  43.0 1.6 %shard_map.167 = bf16[256,512]{1,0:T(8,128)(2,1)} custom-call(f32[256,512]{1,0:T(8,128)S(1)} %shard_map.165.mine_ref, bf16[256,512]{1,0:T(8,128)(2,1)S(1)} %collective-permute-done.18.theirs_ref, f32[1,512]{1,0:T(1,128)S(1)} %bitcast.3, bf16[512,1024]{1,0:T(8,128)(2,1)S(1)} %copy-done.2, bf16[1024,512]{1,0:T(8,128)(2,1)S(1)} %copy-done.3), custom_call_target="tpu_custom_call" | custom-call | flops 1 | bytes 1 | tf_op jit(solution)/shard_map/pallas_call | solution.py:36
  (50 shorter events, 1.0 us)
Async XLA Ops:
  0.0 18.3 %copy-start = (bf16[48,128,128]{2,1,0:T(8,128)(2,1)S(1)}, bf16[48,128,128]{2,1,0:T(8,128)(2,1)}, u32[]{:S(2)}) copy-start(bf16[48,128,128]{2,1,0:T(8,128)(2,1)} %tiles_ref.1) | copy-start | bytes 4718596
  0.0 18.3 %copy-start.11 = (s32[48]{0:T(128)S(1)}, s32[48]{0:T(128)}, u32[]{:S(2)}) copy-start(s32[48]{0:T(128)} %rows_ref.1) | copy-start | bytes 580
  0.0 18.3 %copy-start.12 = (s32[48]{0:T(128)S(1)}, s32[48]{0:T(128)}, u32[]{:S(2)}) copy-start(s32[48]{0:T(128)} %cols_ref.1) | copy-start | bytes 580
  2.6 9.6 %collective-permute-start.10 = (bf16[256,512]{1,0:T(8,128)(2,1)}, bf16[256,512]{1,0:T(8,128)(2,1)S(1)}, u32[]{:S(2)}, u32[]{:S(2)}) collective-permute-start(bf16[256,512]{1,0:T(8,128)(2,1)} %get-tuple-element.39.refs_0_), channel_id=1, source_target_pairs={{0,2},{1,3},{4,0},{5,1},{8,4},{9,5},{12,8},{13,9},{14,12},{15,13},... | collective-permute-start | bytes 786440 | tf_op jit(solution)/shard_map/ppermute | solution.py:261
  5.6 8.4 %collective-permute-start.9 = (bf16[256,512]{1,0:T(8,128)(2,1)}, bf16[256,512]{1,0:T(8,128)(2,1)S(1)}, u32[]{:S(2)}, u32[]{:S(2)}) collective-permute-start(bf16[256,512]{1,0:T(8,128)(2,1)} %get-tuple-element.39.refs_0_), channel_id=1, source_target_pairs={{0,4},{1,5},{4,8},{5,9},{8,12},{9,13},{12,14},{13,15},{14,10},{15,... | collective-permute-start | bytes 786440 | tf_op jit(solution)/shard_map/ppermute | solution.py:261
  9.7 7.7 %collective-permute-start = (bf16[144,128]{1,0:T(8,128)(2,1)}, bf16[144,128]{1,0:T(8,128)(2,1)S(1)}, u32[]{:S(2)}, u32[]{:S(2)}) collective-permute-start(bf16[144,128]{1,0:T(8,128)(2,1)} %get-tuple-element.35), channel_id=1, source_target_pairs={{0,2},{1,3},{2,0},{3,1},{4,6},{5,7},{6,4},{7,5},{8,10},{9,11},{10,... | collective-permute-start | bytes 110600 | tf_op jit(solution)/shard_map/ppermute | solution.py:264
  11.6 5.7 %collective-permute-start.1 = (bf16[144,128]{1,0:T(8,128)(2,1)}, bf16[144,128]{1,0:T(8,128)(2,1)S(1)}, u32[]{:S(2)}, u32[]{:S(2)}) collective-permute-start(bf16[144,128]{1,0:T(8,128)(2,1)} %get-tuple-element.36), channel_id=1, source_target_pairs={{0,1},{1,0},{2,3},{3,2},{4,5},{5,4},{6,7},{7,6},{8,9},{9,8},{10,11... | collective-permute-start | bytes 110600 | tf_op jit(solution)/shard_map/ppermute | solution.py:264
  11.6 5.7 %collective-permute-start.2 = (bf16[144,128]{1,0:T(8,128)(2,1)}, bf16[144,128]{1,0:T(8,128)(2,1)S(1)}, u32[]{:S(2)}, u32[]{:S(2)}) collective-permute-start(bf16[144,128]{1,0:T(8,128)(2,1)} %get-tuple-element.37), channel_id=1, source_target_pairs={{0,3},{1,2},{2,1},{3,0},{4,7},{5,6},{6,5},{7,4},{8,11},{9,10},{10,... | collective-permute-start | bytes 110600 | tf_op jit(solution)/shard_map/ppermute | solution.py:264
  14.6 6.9 %collective-permute-start.11 = (bf16[256,512]{1,0:T(8,128)(2,1)S(1)}, bf16[256,512]{1,0:T(8,128)(2,1)S(1)}, u32[]{:S(2)}, u32[]{:S(2)}) collective-permute-start(bf16[256,512]{1,0:T(8,128)(2,1)S(1)} %get-tuple-element.41.refs_1_), channel_id=1, source_target_pairs={{0,4},{1,5},{4,8},{5,9},{8,12},{9,13},{12,14},{13,15},{14,10},{15,... | collective-permute-start | bytes 786440 | tf_op jit(solution)/shard_map/ppermute | solution.py:261
  14.7 7.8 %collective-permute-start.12 = (bf16[256,512]{1,0:T(8,128)(2,1)S(1)}, bf16[256,512]{1,0:T(8,128)(2,1)S(1)}, u32[]{:S(2)}, u32[]{:S(2)}) collective-permute-start(bf16[256,512]{1,0:T(8,128)(2,1)S(1)} %get-tuple-element.42.refs_2_), channel_id=1, source_target_pairs={{0,2},{1,3},{4,0},{5,1},{8,4},{9,5},{12,8},{13,9},{14,12},{15,13},... | collective-permute-start | bytes 786440 | tf_op jit(solution)/shard_map/ppermute | solution.py:261
  19.4 9.5 %copy-start.4 = (bf16[256,512]{1,0:T(8,128)(2,1)S(1)}, bf16[256,512]{1,0:T(8,128)(2,1)}, u32[]{:S(2)}) copy-start(bf16[256,512]{1,0:T(8,128)(2,1)} %get-tuple-element.31.normed_ref.normed_hbm) | copy-start | bytes 786436
  19.4 9.5 %copy-start.5 = (bf16[512,512]{1,0:T(8,128)(2,1)S(1)}, bf16[512,512]{1,0:T(8,128)(2,1)}, u32[]{:S(2)}) copy-start(bf16[512,512]{1,0:T(8,128)(2,1)} %wq_ref.1) | copy-start | bytes 1572868
  19.4 9.5 %copy-start.6 = (bf16[512,512]{1,0:T(8,128)(2,1)S(1)}, bf16[512,512]{1,0:T(8,128)(2,1)}, u32[]{:S(2)}) copy-start(bf16[512,512]{1,0:T(8,128)(2,1)} %wg_ref.1) | copy-start | bytes 1572868
  19.4 9.4 %copy-start.9 = (f32[64,128]{1,0:T(8,128)S(1)}, f32[64,128]{1,0:T(8,128)}, u32[]{:S(2)}) copy-start(f32[64,128]{1,0:T(8,128)} %omega_hbm.1) | copy-start | bytes 98308
  22.4 7.3 %copy-start.8 = (bf16[256,512]{1,0:T(8,128)(2,1)S(1)}, bf16[256,512]{1,0:T(8,128)(2,1)}, u32[]{:S(2)}) copy-start(bf16[256,512]{1,0:T(8,128)(2,1)} %get-tuple-element.39.refs_0_) | copy-start | bytes 786436
  22.4 5.6 %collective-permute-start.13 = (bf16[16,2,128,128]{3,2,1,0:T(8,128)(2,1)S(1)}, bf16[16,2,128,128]{3,2,1,0:T(8,128)(2,1)S(1)}, u32[]{:S(2)}, u32[]{:S(2)}) collective-permute-start(bf16[16,2,128,128]{3,2,1,0:T(8,128)(2,1)S(1)} %get-tuple-element.44), channel_id=1, source_target_pairs={{0,1},{1,0},{2,3},{3,2},{4,5},{5,4},{6,7},{7,6},{8,9},{9,8},{10,11... | collective-permute-start | bytes 3145736 | tf_op jit(solution)/shard_map/ppermute | solution.py:264
  22.5 8.7 %collective-permute-start.14 = (bf16[256,512]{1,0:T(8,128)(2,1)S(1)}, bf16[256,512]{1,0:T(8,128)(2,1)S(1)}, u32[]{:S(2)}, u32[]{:S(2)}) collective-permute-start(bf16[256,512]{1,0:T(8,128)(2,1)S(1)} %get-tuple-element.45.refs_3_), channel_id=1, source_target_pairs={{0,4},{1,5},{4,8},{5,9},{8,12},{9,13},{12,14},{13,15},{14,10},{15,... | collective-permute-start | bytes 786440 | tf_op jit(solution)/shard_map/ppermute | solution.py:261
  24.0 8.8 %collective-permute-start.15 = (bf16[256,512]{1,0:T(8,128)(2,1)S(1)}, bf16[256,512]{1,0:T(8,128)(2,1)S(1)}, u32[]{:S(2)}, u32[]{:S(2)}) collective-permute-start(bf16[256,512]{1,0:T(8,128)(2,1)S(1)} %get-tuple-element.46.refs_4_), channel_id=1, source_target_pairs={{0,2},{1,3},{4,0},{5,1},{8,4},{9,5},{12,8},{13,9},{14,12},{15,13},... | collective-permute-start | bytes 786440 | tf_op jit(solution)/shard_map/ppermute | solution.py:261
  24.5 11.5 %collective-permute-start.3 = (bf16[144,128]{1,0:T(8,128)(2,1)S(1)}, bf16[144,128]{1,0:T(8,128)(2,1)S(1)}, u32[]{:S(2)}, u32[]{:S(2)}) collective-permute-start(bf16[144,128]{1,0:T(8,128)(2,1)S(1)} %get-tuple-element.57), channel_id=1, source_target_pairs={{0,12},{1,13},{2,14},{3,15},{4,8},{5,9},{6,10},{7,11},{8,4},{9,5},... | collective-permute-start | bytes 110600 | tf_op jit(solution)/shard_map/ppermute | solution.py:264
  28.0 8.6 %collective-permute-start.4 = (bf16[144,128]{1,0:T(8,128)(2,1)S(1)}, bf16[144,128]{1,0:T(8,128)(2,1)S(1)}, u32[]{:S(2)}, u32[]{:S(2)}) collective-permute-start(bf16[144,128]{1,0:T(8,128)(2,1)S(1)} %get-tuple-element.57), channel_id=1, source_target_pairs={{0,8},{1,9},{2,10},{3,11},{4,12},{5,13},{6,14},{7,15},{8,0},{9,1},... | collective-permute-start | bytes 110600 | tf_op jit(solution)/shard_map/ppermute | solution.py:264
  28.0 8.6 %collective-permute-start.5 = (bf16[144,128]{1,0:T(8,128)(2,1)S(1)}, bf16[144,128]{1,0:T(8,128)(2,1)S(1)}, u32[]{:S(2)}, u32[]{:S(2)}) collective-permute-start(bf16[144,128]{1,0:T(8,128)(2,1)S(1)} %get-tuple-element.57), channel_id=1, source_target_pairs={{0,4},{1,5},{2,6},{3,7},{4,0},{5,1},{6,2},{7,3},{8,12},{9,13},{10,... | collective-permute-start | bytes 110600 | tf_op jit(solution)/shard_map/ppermute | solution.py:264
  32.9 8.1 %collective-permute-start.16 = (bf16[128,512]{1,0:T(8,128)(2,1)S(1)}, bf16[128,512]{1,0:T(8,128)(2,1)S(1)}, u32[]{:S(2)}, u32[]{:S(2)}) collective-permute-start(bf16[128,512]{1,0:T(8,128)(2,1)S(1)} %slice.6), channel_id=1, source_target_pairs={{0,4},{1,5},{4,8},{5,9},{8,12},{9,13},{12,14},{13,15},{14,10},{15,... | collective-permute-start | bytes 393224 | tf_op jit(solution)/shard_map/ppermute | solution.py:261
  35.3 5.7 %collective-permute-start.17 = (bf16[128,512]{1,0:T(8,128)(2,1)S(1)}, bf16[128,512]{1,0:T(8,128)(2,1)S(1)}, u32[]{:S(2)}, u32[]{:S(2)}) collective-permute-start(bf16[128,512]{1,0:T(8,128)(2,1)S(1)} %slice.7), channel_id=1, source_target_pairs={{0,2},{1,3},{4,0},{5,1},{8,4},{9,5},{12,8},{13,9},{14,12},{15,13},... | collective-permute-start | bytes 393224 | tf_op jit(solution)/shard_map/ppermute | solution.py:261
  36.7 4.2 %collective-permute-start.6 = (bf16[144,128]{1,0:T(8,128)(2,1)S(1)}, bf16[144,128]{1,0:T(8,128)(2,1)S(1)}, u32[]{:S(2)}, u32[]{:S(2)}) collective-permute-start(bf16[144,128]{1,0:T(8,128)(2,1)S(1)} %add_convert_fusion.own_ref), channel_id=1, source_target_pairs={{0,2},{1,3},{2,0},{3,1},{4,6},{5,7},{6,4},{7,5},{8,10},{9,11},{10,... | collective-permute-start | bytes 110600 | tf_op jit(solution)/shard_map/ppermute | solution.py:264
  36.8 4.2 %collective-permute-start.7 = (bf16[144,128]{1,0:T(8,128)(2,1)S(1)}, bf16[144,128]{1,0:T(8,128)(2,1)S(1)}, u32[]{:S(2)}, u32[]{:S(2)}) collective-permute-start(bf16[144,128]{1,0:T(8,128)(2,1)S(1)} %add_convert_fusion.own_ref), channel_id=1, source_target_pairs={{0,1},{1,0},{2,3},{3,2},{4,5},{5,4},{6,7},{7,6},{8,9},{9,8},{10,11... | collective-permute-start | bytes 110600 | tf_op jit(solution)/shard_map/ppermute | solution.py:264
  36.9 4.1 %collective-permute-start.8 = (bf16[144,128]{1,0:T(8,128)(2,1)S(1)}, bf16[144,128]{1,0:T(8,128)(2,1)S(1)}, u32[]{:S(2)}, u32[]{:S(2)}) collective-permute-start(bf16[144,128]{1,0:T(8,128)(2,1)S(1)} %add_convert_fusion.own_ref), channel_id=1, source_target_pairs={{0,3},{1,2},{2,1},{3,0},{4,7},{5,6},{6,5},{7,4},{8,11},{9,10},{10,... | collective-permute-start | bytes 110600 | tf_op jit(solution)/shard_map/ppermute | solution.py:264
  39.3 2.1 %copy-start.1 = (bf16[256,512]{1,0:T(8,128)(2,1)S(1)}, bf16[256,512]{1,0:T(8,128)(2,1)}, u32[]{:S(2)}) copy-start(bf16[256,512]{1,0:T(8,128)(2,1)} %x_ref.1) | copy-start | bytes 786436
  39.4 2.1 %copy-start.7 = (bf16[512,512]{1,0:T(8,128)(2,1)S(1)}, bf16[512,512]{1,0:T(8,128)(2,1)}, u32[]{:S(2)}) copy-start(bf16[512,512]{1,0:T(8,128)(2,1)} %wo_ref.1) | copy-start | bytes 1572868
  41.2 1.6 %collective-permute-start.18 = (bf16[256,512]{1,0:T(8,128)(2,1)S(1)}, bf16[256,512]{1,0:T(8,128)(2,1)S(1)}, u32[]{:S(2)}, u32[]{:S(2)}) collective-permute-start(bf16[256,512]{1,0:T(8,128)(2,1)S(1)} %shard_map.166), channel_id=1, source_target_pairs={{0,1},{1,0},{2,3},{3,2},{4,5},{5,4},{6,7},{7,6},{8,9},{9,8},{10,11... | collective-permute-start | bytes 786440 | tf_op jit(solution)/shard_map/ppermute | solution.py:264
  41.5 1.3 %copy-start.2 = (bf16[512,1024]{1,0:T(8,128)(2,1)S(1)}, bf16[512,1024]{1,0:T(8,128)(2,1)}, u32[]{:S(2)}) copy-start(bf16[512,1024]{1,0:T(8,128)(2,1)} %up_ref.1) | copy-start | bytes 3145732
  41.5 1.5 %copy-start.3 = (bf16[1024,512]{1,0:T(8,128)(2,1)S(1)}, bf16[1024,512]{1,0:T(8,128)(2,1)}, u32[]{:S(2)}) copy-start(bf16[1024,512]{1,0:T(8,128)(2,1)} %down_ref.1) | copy-start | bytes 3145732
  41.5 1.5 %copy-start.10 = (f32[512]{0:T(512)S(1)}, f32[512]{0:T(512)}, u32[]{:S(2)}) copy-start(f32[512]{0:T(512)} %param.29) | copy-start | bytes 6148

commit v6 on v5

--- a/solution.py
+++ b/solution.py
@@ -345,11 +345,12 @@
 
         def accumulate(totals, first, chunks, aside=None):
             totals = list(totals)
+            early = [] if aside is None else [w_up, w_down]
 
             def body(mine_ref, sibling_ref, *refs):
                 place_here = lookup([home[c] for c in range(chips)], lax.axis_index("blk") // 2)
                 chunk_refs = refs[len(totals) : len(totals) + len(chunks)]
-                outs = refs[len(totals) + len(chunks) :]
+                outs = refs[len(totals) + len(chunks) + len(early) :]
 
                 def weights(dense_ref, place):
                     chip = lookup(order, lax.rem(place_here - shifts[place] + 2 * chips, chips))
@@ -370,8 +371,9 @@
             return call(
                 body,
                 outs,
-                [VMEM] * (2 + len(totals) + len(chunks)),
-                (dense, sibling, *totals, *chunks),
+                [VMEM] * (2 + len(totals) + len(chunks))
+                + [pl.BlockSpec(memory_space=pl.ANY)] * len(early),
+                (dense, sibling, *totals, *chunks, *early),
             )
 
         chunks = [message, ahead, back]

time: 44.9 us -> 44.6 us (level)
  Pallas kernels: 13.1 us -> 13.6 us
  waiting for transfers between devices: 10.7 us -> 10.2 us
    ppermute x8, waiting for transfers between devices: 7.43 us -> 6.87 us  [step(): return lax.ppermute(value, 'blk', pairs)]
    pallas_call x10, Pallas kernels: 12.5 us -> 13 us  [call(): pl.pallas_call(body, out_shape=outs, in_specs=specs, out_specs=jax.tree.m...]
  transfers between devices with their start and end apart: 19 -> 19, of which waited for: 10 -> 10; matrix products, arithmetic and copies ran while one was open for 2% -> 2% of each run, Pallas kernels for 19% -> 21%
where the time goes in v6:
time: 44.6 us; the launch traced here: 44.4 us
  starting transfers between devices  18.7 us (42%)
  Pallas kernels  13.6 us (30%)
  waiting for transfers between devices  10.2 us (23%)
  other arithmetic  0.94 us (2%)
  between operations  0.94 us (2%)
    pallas_call x10, Pallas kernels, call(): pl.pallas_call(body, out_shape=outs, in_specs=specs, out_specs=jax.tree.m...  13 us
    ppermute x8, starting transfers between devices, step(): return lax.ppermute(value, 'blk', pairs)  9.68 us
    ppermute x11, starting transfers between devices, flip(): return lax.ppermute(value, 'blk', [(i, i ^ bit) for i in range(size)])  9.04 us
    ppermute x8, waiting for transfers between devices, step(): return lax.ppermute(value, 'blk', pairs)  6.87 us
    ppermute x11, waiting for transfers between devices, flip(): return lax.ppermute(value, 'blk', [(i, i ^ bit) for i in range(size)])  3.28 us
    convert_element_type x1, other arithmetic, on_device(): sent = sums[-1].astype(BF16)  0.91 us
  transfers between devices with their start and end apart: 19, of which 10 were waited for; matrix products, arithmetic and copies ran while one was open for 2% of the time, Pallas kernels for 21%

profile of v6, /device:TPU:0, one launch (start us, length us, event | category | flops | bytes accessed | tf_op | source)
XLA Modules:
  0.0 44.4 jit_solution(16436147308743325859)
XLA Ops:
  0.0 2.6 %shard_map.154 = (bf16[256,512]{1,0:T(8,128)(2,1)}, bf16[256,512]{1,0:T(8,128)(2,1)}) custom-call(bf16[256,512]{1,0:T(8,128)(2,1)} %x_ref.1, f32[1,512]{1,0:T(1,128)} %bitcast.4, bf16[512,512]{1,0:T(8,128)(2,1)} %w_hbm.1), custom_call_target="tpu_custom_call" | custom-call | flops 1 | bytes 1 | tf_op jit(solution)/shard_map/pallas_call | solution.py:36
  2.6 3.0 %collective-permute-start.10 = (bf16[256,512]{1,0:T(8,128)(2,1)}, bf16[256,512]{1,0:T(8,128)(2,1)S(1)}, u32[]{:S(2)}, u32[]{:S(2)}) collective-permute-start(bf16[256,512]{1,0:T(8,128)(2,1)} %get-tuple-element.39.refs_0_), channel_id=1, source_target_pairs={{0,2},{1,3},{4,0},{5,1},{8,4},{9,5},{12,8},{13,9},{14,12},{15,13},... | collective-permute-start | bytes 786440 | tf_op jit(solution)/shard_map/ppermute | solution.py:261
  5.7 3.9 %shard_map.156 = (f32[144,128]{1,0:T(8,128)}, bf16[144,128]{1,0:T(8,128)(2,1)}, bf16[144,128]{1,0:T(8,128)(2,1)}, bf16[144,128]{1,0:T(8,128)(2,1)}, s32[1]{0:T(128)}) custom-call(bf16[256,512]{1,0:T(8,128)(2,1)} %get-tuple-element.31.normed_ref.normed_hbm, bf16[512,512]{1,0:T(8,128)(2,1)} %wk_hbm.1, bf16[512,512]{1,0:T(8,128)(2,1)} %wv_hbm.1, ...), custom_call_target="tpu_custom_call" | custom-call | flops 1 | bytes 1 | tf_op jit(solution)/shard_map/pallas_call | solution.py:36
  9.7 2.0 %collective-permute-start = (bf16[144,128]{1,0:T(8,128)(2,1)}, bf16[144,128]{1,0:T(8,128)(2,1)S(1)}, u32[]{:S(2)}, u32[]{:S(2)}) collective-permute-start(bf16[144,128]{1,0:T(8,128)(2,1)} %get-tuple-element.35), channel_id=1, source_target_pairs={{0,2},{1,3},{2,0},{3,1},{4,6},{5,7},{6,4},{7,5},{8,10},{9,11},{10,... | collective-permute-start | bytes 110600 | tf_op jit(solution)/shard_map/ppermute | solution.py:264
  11.6 0.2 collective-permute-start.2
  11.9 0.3 collective-permute-done.10.refs_1_
  12.2 1.8 %collective-permute-done.9.refs_0_ = bf16[256,512]{1,0:T(8,128)(2,1)S(1)} collective-permute-done((bf16[256,512]{1,0:T(8,128)(2,1)}, bf16[256,512]{1,0:T(8,128)(2,1)S(1)}, u32[]{:S(2)}, u32[]{:S(2)}) %collective-permute-start.9) | collective-permute-done | bytes 262176 | tf_op jit(solution)/shard_map/ppermute | solution.py:261
  14.0 0.6 %shard_map.158 = (bf16[256,512]{1,0:T(8,128)(2,1)S(1)}, bf16[256,512]{1,0:T(8,128)(2,1)S(1)}) custom-call(bf16[256,512]{1,0:T(8,128)(2,1)S(1)} %collective-permute-done.9.refs_0_, bf16[256,512]{1,0:T(8,128)(2,1)S(1)} %collective-permute-done.10.refs_1_, s32[1]{0:T(128)} %get-tuple-element.40.refs_2_), custom_call_target="tpu_custom_call", output_to_operand_aliasing={{0}: (0, {}), {1}: (1, {})} | custom-call | flops 1 | bytes 1 | tf_op jit(solution)/shard_map/pallas_call | solution.py:49
  14.7 2.0 %collective-permute-start.12 = (bf16[256,512]{1,0:T(8,128)(2,1)S(1)}, bf16[256,512]{1,0:T(8,128)(2,1)S(1)}, u32[]{:S(2)}, u32[]{:S(2)}) collective-permute-start(bf16[256,512]{1,0:T(8,128)(2,1)S(1)} %get-tuple-element.42.refs_2_), channel_id=1, source_target_pairs={{0,2},{1,3},{4,0},{5,1},{8,4},{9,5},{12,8},{13,9},{14,12},{15,13},... | collective-permute-start | bytes 786440 | tf_op jit(solution)/shard_map/ppermute | solution.py:261
  17.4 0.9 %fusion = (bf16[144,128]{1,0:T(8,128)(2,1)S(1)}, f32[144,128]{1,0:T(8,128)S(1)}) fusion(bf16[144,128]{1,0:T(8,128)(2,1)S(1)} %collective-permute-done.2, bf16[144,128]{1,0:T(8,128)(2,1)S(1)} %collective-permute-done.1, f32[144,128]{1,0:T(8,128)} %get-tuple-element.34, bf16[144,128]{1,0:T(8,128)(2,1)S(1)} %collective-permute-done), kind=kLoop, calls=%fused_computation.2 | loop fusion | flops 129024 | bytes 294912 | tf_op jit(solution)/shard_map/convert_element_type | solution.py:320
  18.3 1.6 %shard_map.157 = (bf16[16,2,128,128]{3,2,1,0:T(8,128)(2,1)S(1)}, bf16[16,2,128,128]{3,2,1,0:T(8,128)(2,1)S(1)}) custom-call(s32[1]{0:T(128)} %bitcast.1.core_ref, s32[48]{0:T(128)S(1)} %copy-done.11, s32[48]{0:T(128)S(1)} %copy-done.12, s32[1]{0:T(128)S(6)} %copy.35.count_ref, bf16[48,128,128]{2,1,0:T(8,128)(2,1)S(1)} %copy-done.2, ...), custom_call_target="tpu_custom_call" | custom-call | flops 1 | bytes 1 | tf_op jit(solution)/shard_map/pallas_call | solution.py:36
  20.0 1.5 %collective-permute-done.11.refs_0_ = bf16[256,512]{1,0:T(8,128)(2,1)S(1)} collective-permute-done((bf16[256,512]{1,0:T(8,128)(2,1)S(1)}, bf16[256,512]{1,0:T(8,128)(2,1)S(1)}, u32[]{:S(2)}, u32[]{:S(2)}) %collective-permute-start.11) | collective-permute-done | bytes 262176 | tf_op jit(solution)/shard_map/ppermute | solution.py:261
  21.5 0.9 %collective-permute-done.12.refs_1_ = bf16[256,512]{1,0:T(8,128)(2,1)S(1)} collective-permute-done((bf16[256,512]{1,0:T(8,128)(2,1)S(1)}, bf16[256,512]{1,0:T(8,128)(2,1)S(1)}, u32[]{:S(2)}, u32[]{:S(2)}) %collective-permute-start.12) | collective-permute-done | bytes 262176 | tf_op jit(solution)/shard_map/ppermute | solution.py:261
  22.5 1.6 %collective-permute-start.14 = (bf16[256,512]{1,0:T(8,128)(2,1)S(1)}, bf16[256,512]{1,0:T(8,128)(2,1)S(1)}, u32[]{:S(2)}, u32[]{:S(2)}) collective-permute-start(bf16[256,512]{1,0:T(8,128)(2,1)S(1)} %get-tuple-element.45.refs_3_), channel_id=1, source_target_pairs={{0,4},{1,5},{4,8},{5,9},{8,12},{9,13},{12,14},{13,15},{14,10},{15,... | collective-permute-start | bytes 786440 | tf_op jit(solution)/shard_map/ppermute | solution.py:261
  24.0 0.4 %collective-permute-start.15 = (bf16[256,512]{1,0:T(8,128)(2,1)S(1)}, bf16[256,512]{1,0:T(8,128)(2,1)S(1)}, u32[]{:S(2)}, u32[]{:S(2)}) collective-permute-start(bf16[256,512]{1,0:T(8,128)(2,1)S(1)} %get-tuple-element.46.refs_4_), channel_id=1, source_target_pairs={{0,2},{1,3},{4,0},{5,1},{8,4},{9,5},{12,8},{13,9},{14,12},{15,13},... | collective-permute-start | bytes 786440 | tf_op jit(solution)/shard_map/ppermute | solution.py:261
  24.5 3.5 %collective-permute-start.3 = (bf16[144,128]{1,0:T(8,128)(2,1)S(1)}, bf16[144,128]{1,0:T(8,128)(2,1)S(1)}, u32[]{:S(2)}, u32[]{:S(2)}) collective-permute-start(bf16[144,128]{1,0:T(8,128)(2,1)S(1)} %get-tuple-element.57), channel_id=1, source_target_pairs={{0,12},{1,13},{2,14},{3,15},{4,8},{5,9},{6,10},{7,11},{8,4},{9,5},... | collective-permute-start | bytes 110600 | tf_op jit(solution)/shard_map/ppermute | solution.py:264
  28.0 0.8 %collective-permute-start.5 = (bf16[144,128]{1,0:T(8,128)(2,1)S(1)}, bf16[144,128]{1,0:T(8,128)(2,1)S(1)}, u32[]{:S(2)}, u32[]{:S(2)}) collective-permute-start(bf16[144,128]{1,0:T(8,128)(2,1)S(1)} %get-tuple-element.57), channel_id=1, source_target_pairs={{0,4},{1,5},{2,6},{3,7},{4,0},{5,1},{6,2},{7,3},{8,12},{9,13},{10,... | collective-permute-start | bytes 110600 | tf_op jit(solution)/shard_map/ppermute | solution.py:264
  28.9 0.8 %shard_map.155 = (bf16[256,1024]{1,0:T(8,128)(2,1)S(1)}, f32[256,512]{1,0:T(8,128)S(1)}) custom-call(bf16[256,512]{1,0:T(8,128)(2,1)S(1)} %copy-done.4, bf16[512,512]{1,0:T(8,128)(2,1)S(1)} %copy-done.5, bf16[512,512]{1,0:T(8,128)(2,1)S(1)} %copy-done.6, f32[64,128]{1,0:T(8,128)S(1)} %copy-done.9), custom_call_target="tpu_custom_call" | custom-call | flops 1 | bytes 1 | tf_op jit(solution)/shard_map/pallas_call | solution.py:36
  29.7 0.8 %shard_map.160 = (f32[256,512]{1,0:T(8,128)S(1)}, f32[256,512]{1,0:T(8,128)S(1)}) custom-call(bf16[16,2,128,128]{3,2,1,0:T(8,128)(2,1)S(1)} %get-tuple-element.38.refs_3_.mine_ref, bf16[16,2,128,128]{3,2,1,0:T(8,128)(2,1)S(1)} %collective-permute-done.13.sibling_ref, bf16[256,512]{1,0:T(8,128)(2,1)S(1)} %copy-done.8, ...), custom_call_target="tpu_custom_call" | custom-call | flops 1 | bytes 1 | tf_op jit(solution)/shard_map/pallas_call | solution.py:36
  30.6 0.6 %collective-permute-done.14.refs_0_ = bf16[256,512]{1,0:T(8,128)(2,1)S(1)} collective-permute-done((bf16[256,512]{1,0:T(8,128)(2,1)S(1)}, bf16[256,512]{1,0:T(8,128)(2,1)S(1)}, u32[]{:S(2)}, u32[]{:S(2)}) %collective-permute-start.14) | collective-permute-done | bytes 262176 | tf_op jit(solution)/shard_map/ppermute | solution.py:261
  31.2 1.7 %collective-permute-done.15.refs_1_ = bf16[256,512]{1,0:T(8,128)(2,1)S(1)} collective-permute-done((bf16[256,512]{1,0:T(8,128)(2,1)S(1)}, bf16[256,512]{1,0:T(8,128)(2,1)S(1)}, u32[]{:S(2)}, u32[]{:S(2)}) %collective-permute-start.15) | collective-permute-done | bytes 262176 | tf_op jit(solution)/shard_map/ppermute | solution.py:261
  32.9 2.4 %collective-permute-start.16 = (bf16[128,512]{1,0:T(8,128)(2,1)S(1)}, bf16[128,512]{1,0:T(8,128)(2,1)S(1)}, u32[]{:S(2)}, u32[]{:S(2)}) collective-permute-start(bf16[128,512]{1,0:T(8,128)(2,1)S(1)} %slice.6), channel_id=1, source_target_pairs={{0,4},{1,5},{4,8},{5,9},{8,12},{9,13},{12,14},{13,15},{14,10},{15,... | collective-permute-start | bytes 393224 | tf_op jit(solution)/shard_map/ppermute | solution.py:261
  35.3 0.6 %collective-permute-done.3 = bf16[144,128]{1,0:T(8,128)(2,1)S(1)} collective-permute-done((bf16[144,128]{1,0:T(8,128)(2,1)S(1)}, bf16[144,128]{1,0:T(8,128)(2,1)S(1)}, u32[]{:S(2)}, u32[]{:S(2)}) %collective-permute-start.3) | collective-permute-done | bytes 36896 | tf_op jit(solution)/shard_map/ppermute | solution.py:264
  35.9 0.7 %collective-permute-done.4 = bf16[144,128]{1,0:T(8,128)(2,1)S(1)} collective-permute-done((bf16[144,128]{1,0:T(8,128)(2,1)S(1)}, bf16[144,128]{1,0:T(8,128)(2,1)S(1)}, u32[]{:S(2)}, u32[]{:S(2)}) %collective-permute-start.4) | collective-permute-done | bytes 36896 | tf_op jit(solution)/shard_map/ppermute | solution.py:264
  36.9 2.0 %collective-permute-start.8 = (bf16[144,128]{1,0:T(8,128)(2,1)S(1)}, bf16[144,128]{1,0:T(8,128)(2,1)S(1)}, u32[]{:S(2)}, u32[]{:S(2)}) collective-permute-start(bf16[144,128]{1,0:T(8,128)(2,1)S(1)} %add_convert_fusion.own_ref), channel_id=1, source_target_pairs={{0,3},{1,2},{2,1},{3,0},{4,7},{5,6},{6,5},{7,4},{8,11},{9,10},{10,... | collective-permute-start | bytes 110600 | tf_op jit(solution)/shard_map/ppermute | solution.py:264
  38.9 0.4 shard_map.162
  39.4 1.6 %collective-permute-done.6.pair_ref.refs_4_ = bf16[144,128]{1,0:T(8,128)(2,1)S(1)} collective-permute-done((bf16[144,128]{1,0:T(8,128)(2,1)S(1)}, bf16[144,128]{1,0:T(8,128)(2,1)S(1)}, u32[]{:S(2)}, u32[]{:S(2)}) %collective-permute-start.6) | collective-permute-done | bytes 36896 | tf_op jit(solution)/shard_map/ppermute | solution.py:264
  41.0 0.2 shard_map.166
  41.2 0.3 collective-permute-start.18
  41.5 0.7 %shard_map.163.total_ref = f32[256,512]{1,0:T(8,128)S(1)} custom-call(bf16[256,512]{1,0:T(8,128)(2,1)S(1)} %copy-done.3, bf16[256,1024]{1,0:T(8,128)(2,1)S(1)} %get-tuple-element.32.refs_2_.qf_ref, f32[256,512]{1,0:T(8,128)S(1)} %get-tuple-element.33.gate_ref, bf16[144,128]{1,0:T(8,128)(2,1)S(1)} %add_convert_fusion.own_ref, ...), custom_call_target="tpu_custom_call" | custom-call | flops 1 | bytes 1 | tf_op jit(solution)/shard_map/pallas_call | solution.py:36
  42.4 0.4 collective-permute-done.18.theirs_ref
  42.8 1.6 %shard_map.167 = bf16[256,512]{1,0:T(8,128)(2,1)} custom-call(f32[256,512]{1,0:T(8,128)S(1)} %shard_map.165.mine_ref, bf16[256,512]{1,0:T(8,128)(2,1)S(1)} %collective-permute-done.18.theirs_ref, f32[1,512]{1,0:T(1,128)S(1)} %bitcast.3, bf16[512,1024]{1,0:T(8,128)(2,1)S(1)} %copy-done, bf16[1024,512]{1,0:T(8,128)(2,1)S(1)} %copy-done.1), custom_call_target="tpu_custom_call" | custom-call | flops 1 | bytes 1 | tf_op jit(solution)/shard_map/pallas_call | solution.py:36
  (50 shorter events, 0.8 us)
Async XLA Ops:
  0.0 18.3 %copy-start.2 = (bf16[48,128,128]{2,1,0:T(8,128)(2,1)S(1)}, bf16[48,128,128]{2,1,0:T(8,128)(2,1)}, u32[]{:S(2)}) copy-start(bf16[48,128,128]{2,1,0:T(8,128)(2,1)} %tiles_ref.1) | copy-start | bytes 4718596
  0.0 18.3 %copy-start.11 = (s32[48]{0:T(128)S(1)}, s32[48]{0:T(128)}, u32[]{:S(2)}) copy-start(s32[48]{0:T(128)} %rows_ref.1) | copy-start | bytes 580
  0.0 18.3 %copy-start.12 = (s32[48]{0:T(128)S(1)}, s32[48]{0:T(128)}, u32[]{:S(2)}) copy-start(s32[48]{0:T(128)} %cols_ref.1) | copy-start | bytes 580
  2.6 9.6 %collective-permute-start.10 = (bf16[256,512]{1,0:T(8,128)(2,1)}, bf16[256,512]{1,0:T(8,128)(2,1)S(1)}, u32[]{:S(2)}, u32[]{:S(2)}) collective-permute-start(bf16[256,512]{1,0:T(8,128)(2,1)} %get-tuple-element.39.refs_0_), channel_id=1, source_target_pairs={{0,2},{1,3},{4,0},{5,1},{8,4},{9,5},{12,8},{13,9},{14,12},{15,13},... | collective-permute-start | bytes 786440 | tf_op jit(solution)/shard_map/ppermute | solution.py:261
  5.6 8.4 %collective-permute-start.9 = (bf16[256,512]{1,0:T(8,128)(2,1)}, bf16[256,512]{1,0:T(8,128)(2,1)S(1)}, u32[]{:S(2)}, u32[]{:S(2)}) collective-permute-start(bf16[256,512]{1,0:T(8,128)(2,1)} %get-tuple-element.39.refs_0_), channel_id=1, source_target_pairs={{0,4},{1,5},{4,8},{5,9},{8,12},{9,13},{12,14},{13,15},{14,10},{15,... | collective-permute-start | bytes 786440 | tf_op jit(solution)/shard_map/ppermute | solution.py:261
  9.7 7.7 %collective-permute-start = (bf16[144,128]{1,0:T(8,128)(2,1)}, bf16[144,128]{1,0:T(8,128)(2,1)S(1)}, u32[]{:S(2)}, u32[]{:S(2)}) collective-permute-start(bf16[144,128]{1,0:T(8,128)(2,1)} %get-tuple-element.35), channel_id=1, source_target_pairs={{0,2},{1,3},{2,0},{3,1},{4,6},{5,7},{6,4},{7,5},{8,10},{9,11},{10,... | collective-permute-start | bytes 110600 | tf_op jit(solution)/shard_map/ppermute | solution.py:264
  11.6 5.7 %collective-permute-start.1 = (bf16[144,128]{1,0:T(8,128)(2,1)}, bf16[144,128]{1,0:T(8,128)(2,1)S(1)}, u32[]{:S(2)}, u32[]{:S(2)}) collective-permute-start(bf16[144,128]{1,0:T(8,128)(2,1)} %get-tuple-element.36), channel_id=1, source_target_pairs={{0,1},{1,0},{2,3},{3,2},{4,5},{5,4},{6,7},{7,6},{8,9},{9,8},{10,11... | collective-permute-start | bytes 110600 | tf_op jit(solution)/shard_map/ppermute | solution.py:264
  11.6 5.7 %collective-permute-start.2 = (bf16[144,128]{1,0:T(8,128)(2,1)}, bf16[144,128]{1,0:T(8,128)(2,1)S(1)}, u32[]{:S(2)}, u32[]{:S(2)}) collective-permute-start(bf16[144,128]{1,0:T(8,128)(2,1)} %get-tuple-element.37), channel_id=1, source_target_pairs={{0,3},{1,2},{2,1},{3,0},{4,7},{5,6},{6,5},{7,4},{8,11},{9,10},{10,... | collective-permute-start | bytes 110600 | tf_op jit(solution)/shard_map/ppermute | solution.py:264
  14.6 6.9 %collective-permute-start.11 = (bf16[256,512]{1,0:T(8,128)(2,1)S(1)}, bf16[256,512]{1,0:T(8,128)(2,1)S(1)}, u32[]{:S(2)}, u32[]{:S(2)}) collective-permute-start(bf16[256,512]{1,0:T(8,128)(2,1)S(1)} %get-tuple-element.41.refs_1_), channel_id=1, source_target_pairs={{0,4},{1,5},{4,8},{5,9},{8,12},{9,13},{12,14},{13,15},{14,10},{15,... | collective-permute-start | bytes 786440 | tf_op jit(solution)/shard_map/ppermute | solution.py:261
  14.7 7.8 %collective-permute-start.12 = (bf16[256,512]{1,0:T(8,128)(2,1)S(1)}, bf16[256,512]{1,0:T(8,128)(2,1)S(1)}, u32[]{:S(2)}, u32[]{:S(2)}) collective-permute-start(bf16[256,512]{1,0:T(8,128)(2,1)S(1)} %get-tuple-element.42.refs_2_), channel_id=1, source_target_pairs={{0,2},{1,3},{4,0},{5,1},{8,4},{9,5},{12,8},{13,9},{14,12},{15,13},... | collective-permute-start | bytes 786440 | tf_op jit(solution)/shard_map/ppermute | solution.py:261
  19.9 8.9 %copy-start.4 = (bf16[256,512]{1,0:T(8,128)(2,1)S(1)}, bf16[256,512]{1,0:T(8,128)(2,1)}, u32[]{:S(2)}) copy-start(bf16[256,512]{1,0:T(8,128)(2,1)} %get-tuple-element.31.normed_ref.normed_hbm) | copy-start | bytes 786436
  19.9 8.9 %copy-start.5 = (bf16[512,512]{1,0:T(8,128)(2,1)S(1)}, bf16[512,512]{1,0:T(8,128)(2,1)}, u32[]{:S(2)}) copy-start(bf16[512,512]{1,0:T(8,128)(2,1)} %wq_ref.1) | copy-start | bytes 1572868
  20.0 8.9 %copy-start.6 = (bf16[512,512]{1,0:T(8,128)(2,1)S(1)}, bf16[512,512]{1,0:T(8,128)(2,1)}, u32[]{:S(2)}) copy-start(bf16[512,512]{1,0:T(8,128)(2,1)} %wg_ref.1) | copy-start | bytes 1572868
  20.0 8.9 %copy-start.9 = (f32[64,128]{1,0:T(8,128)S(1)}, f32[64,128]{1,0:T(8,128)}, u32[]{:S(2)}) copy-start(f32[64,128]{1,0:T(8,128)} %omega_hbm.1) | copy-start | bytes 98308
  22.4 7.3 %copy-start.8 = (bf16[256,512]{1,0:T(8,128)(2,1)S(1)}, bf16[256,512]{1,0:T(8,128)(2,1)}, u32[]{:S(2)}) copy-start(bf16[256,512]{1,0:T(8,128)(2,1)} %get-tuple-element.39.refs_0_) | copy-start | bytes 786436
  22.4 5.6 %collective-permute-start.13 = (bf16[16,2,128,128]{3,2,1,0:T(8,128)(2,1)S(1)}, bf16[16,2,128,128]{3,2,1,0:T(8,128)(2,1)S(1)}, u32[]{:S(2)}, u32[]{:S(2)}) collective-permute-start(bf16[16,2,128,128]{3,2,1,0:T(8,128)(2,1)S(1)} %get-tuple-element.44), channel_id=1, source_target_pairs={{0,1},{1,0},{2,3},{3,2},{4,5},{5,4},{6,7},{7,6},{8,9},{9,8},{10,11... | collective-permute-start | bytes 3145736 | tf_op jit(solution)/shard_map/ppermute | solution.py:264
  22.5 8.7 %collective-permute-start.14 = (bf16[256,512]{1,0:T(8,128)(2,1)S(1)}, bf16[256,512]{1,0:T(8,128)(2,1)S(1)}, u32[]{:S(2)}, u32[]{:S(2)}) collective-permute-start(bf16[256,512]{1,0:T(8,128)(2,1)S(1)} %get-tuple-element.45.refs_3_), channel_id=1, source_target_pairs={{0,4},{1,5},{4,8},{5,9},{8,12},{9,13},{12,14},{13,15},{14,10},{15,... | collective-permute-start | bytes 786440 | tf_op jit(solution)/shard_map/ppermute | solution.py:261
  24.0 8.8 %collective-permute-start.15 = (bf16[256,512]{1,0:T(8,128)(2,1)S(1)}, bf16[256,512]{1,0:T(8,128)(2,1)S(1)}, u32[]{:S(2)}, u32[]{:S(2)}) collective-permute-start(bf16[256,512]{1,0:T(8,128)(2,1)S(1)} %get-tuple-element.46.refs_4_), channel_id=1, source_target_pairs={{0,2},{1,3},{4,0},{5,1},{8,4},{9,5},{12,8},{13,9},{14,12},{15,13},... | collective-permute-start | bytes 786440 | tf_op jit(solution)/shard_map/ppermute | solution.py:261
  24.5 11.5 %collective-permute-start.3 = (bf16[144,128]{1,0:T(8,128)(2,1)S(1)}, bf16[144,128]{1,0:T(8,128)(2,1)S(1)}, u32[]{:S(2)}, u32[]{:S(2)}) collective-permute-start(bf16[144,128]{1,0:T(8,128)(2,1)S(1)} %get-tuple-element.57), channel_id=1, source_target_pairs={{0,12},{1,13},{2,14},{3,15},{4,8},{5,9},{6,10},{7,11},{8,4},{9,5},... | collective-permute-start | bytes 110600 | tf_op jit(solution)/shard_map/ppermute | solution.py:264
  28.0 8.6 %collective-permute-start.4 = (bf16[144,128]{1,0:T(8,128)(2,1)S(1)}, bf16[144,128]{1,0:T(8,128)(2,1)S(1)}, u32[]{:S(2)}, u32[]{:S(2)}) collective-permute-start(bf16[144,128]{1,0:T(8,128)(2,1)S(1)} %get-tuple-element.57), channel_id=1, source_target_pairs={{0,8},{1,9},{2,10},{3,11},{4,12},{5,13},{6,14},{7,15},{8,0},{9,1},... | collective-permute-start | bytes 110600 | tf_op jit(solution)/shard_map/ppermute | solution.py:264
  28.0 8.6 %collective-permute-start.5 = (bf16[144,128]{1,0:T(8,128)(2,1)S(1)}, bf16[144,128]{1,0:T(8,128)(2,1)S(1)}, u32[]{:S(2)}, u32[]{:S(2)}) collective-permute-start(bf16[144,128]{1,0:T(8,128)(2,1)S(1)} %get-tuple-element.57), channel_id=1, source_target_pairs={{0,4},{1,5},{2,6},{3,7},{4,0},{5,1},{6,2},{7,3},{8,12},{9,13},{10,... | collective-permute-start | bytes 110600 | tf_op jit(solution)/shard_map/ppermute | solution.py:264
  30.5 8.4 %copy-start = (bf16[512,1024]{1,0:T(8,128)(2,1)S(1)}, bf16[512,1024]{1,0:T(8,128)(2,1)}, u32[]{:S(2)}) copy-start(bf16[512,1024]{1,0:T(8,128)(2,1)} %up_ref.1) | copy-start | bytes 3145732
  30.6 8.3 %copy-start.1 = (bf16[1024,512]{1,0:T(8,128)(2,1)S(1)}, bf16[1024,512]{1,0:T(8,128)(2,1)}, u32[]{:S(2)}) copy-start(bf16[1024,512]{1,0:T(8,128)(2,1)} %down_ref.1) | copy-start | bytes 3145732
  32.9 8.1 %collective-permute-start.16 = (bf16[128,512]{1,0:T(8,128)(2,1)S(1)}, bf16[128,512]{1,0:T(8,128)(2,1)S(1)}, u32[]{:S(2)}, u32[]{:S(2)}) collective-permute-start(bf16[128,512]{1,0:T(8,128)(2,1)S(1)} %slice.6), channel_id=1, source_target_pairs={{0,4},{1,5},{4,8},{5,9},{8,12},{9,13},{12,14},{13,15},{14,10},{15,... | collective-permute-start | bytes 393224 | tf_op jit(solution)/shard_map/ppermute | solution.py:261
  35.3 5.7 %collective-permute-start.17 = (bf16[128,512]{1,0:T(8,128)(2,1)S(1)}, bf16[128,512]{1,0:T(8,128)(2,1)S(1)}, u32[]{:S(2)}, u32[]{:S(2)}) collective-permute-start(bf16[128,512]{1,0:T(8,128)(2,1)S(1)} %slice.7), channel_id=1, source_target_pairs={{0,2},{1,3},{4,0},{5,1},{8,4},{9,5},{12,8},{13,9},{14,12},{15,13},... | collective-permute-start | bytes 393224 | tf_op jit(solution)/shard_map/ppermute | solution.py:261
  36.7 4.2 %collective-permute-start.6 = (bf16[144,128]{1,0:T(8,128)(2,1)S(1)}, bf16[144,128]{1,0:T(8,128)(2,1)S(1)}, u32[]{:S(2)}, u32[]{:S(2)}) collective-permute-start(bf16[144,128]{1,0:T(8,128)(2,1)S(1)} %add_convert_fusion.own_ref), channel_id=1, source_target_pairs={{0,2},{1,3},{2,0},{3,1},{4,6},{5,7},{6,4},{7,5},{8,10},{9,11},{10,... | collective-permute-start | bytes 110600 | tf_op jit(solution)/shard_map/ppermute | solution.py:264
  36.8 4.2 %collective-permute-start.7 = (bf16[144,128]{1,0:T(8,128)(2,1)S(1)}, bf16[144,128]{1,0:T(8,128)(2,1)S(1)}, u32[]{:S(2)}, u32[]{:S(2)}) collective-permute-start(bf16[144,128]{1,0:T(8,128)(2,1)S(1)} %add_convert_fusion.own_ref), channel_id=1, source_target_pairs={{0,1},{1,0},{2,3},{3,2},{4,5},{5,4},{6,7},{7,6},{8,9},{9,8},{10,11... | collective-permute-start | bytes 110600 | tf_op jit(solution)/shard_map/ppermute | solution.py:264
  36.9 4.1 %collective-permute-start.8 = (bf16[144,128]{1,0:T(8,128)(2,1)S(1)}, bf16[144,128]{1,0:T(8,128)(2,1)S(1)}, u32[]{:S(2)}, u32[]{:S(2)}) collective-permute-start(bf16[144,128]{1,0:T(8,128)(2,1)S(1)} %add_convert_fusion.own_ref), channel_id=1, source_target_pairs={{0,3},{1,2},{2,1},{3,0},{4,7},{5,6},{6,5},{7,4},{8,11},{9,10},{10,... | collective-permute-start | bytes 110600 | tf_op jit(solution)/shard_map/ppermute | solution.py:264
  39.4 2.1 %copy-start.3 = (bf16[256,512]{1,0:T(8,128)(2,1)S(1)}, bf16[256,512]{1,0:T(8,128)(2,1)}, u32[]{:S(2)}) copy-start(bf16[256,512]{1,0:T(8,128)(2,1)} %x_ref.1) | copy-start | bytes 786436
  39.4 2.1 %copy-start.7 = (bf16[512,512]{1,0:T(8,128)(2,1)S(1)}, bf16[512,512]{1,0:T(8,128)(2,1)}, u32[]{:S(2)}) copy-start(bf16[512,512]{1,0:T(8,128)(2,1)} %wo_ref.1) | copy-start | bytes 1572868
  41.2 1.6 %collective-permute-start.18 = (bf16[256,512]{1,0:T(8,128)(2,1)S(1)}, bf16[256,512]{1,0:T(8,128)(2,1)S(1)}, u32[]{:S(2)}, u32[]{:S(2)}) collective-permute-start(bf16[256,512]{1,0:T(8,128)(2,1)S(1)} %shard_map.166), channel_id=1, source_target_pairs={{0,1},{1,0},{2,3},{3,2},{4,5},{5,4},{6,7},{7,6},{8,9},{9,8},{10,11... | collective-permute-start | bytes 786440 | tf_op jit(solution)/shard_map/ppermute | solution.py:264
  41.5 1.3 %copy-start.10 = (f32[512]{0:T(512)S(1)}, f32[512]{0:T(512)}, u32[]{:S(2)}) copy-start(f32[512]{0:T(512)} %param.29) | copy-start | bytes 6148

commit v7 on v6

--- a/solution.py
+++ b/solution.py
@@ -405,7 +405,7 @@
             [VMEM] * 9,
             (features, qfeat, gate, quarter, *gathered, w_out, totals[0]),
         )
-        late = after(late, *totals, *gathered)
+        late = after(late, *gathered)
         late_given, late_mine = sds((nodes, width), BF16), sds((nodes, width), F32)
         given = call(late_kernel, late_given, [VMEM] * 4, (totals[1], sibling_late, *late))
         mine = call(late_kernel, late_mine, [VMEM] * 4, (mixed, mine_late, *late))

time: 44.6 us -> 44.7 us (level)
  waiting for transfers between devices: 10.2 us -> 10.9 us
    ppermute x8, waiting for transfers between devices: 6.87 us -> 7.39 us  [step(): return lax.ppermute(value, 'blk', pairs)]
  transfers between devices with their start and end apart: 19 -> 19, of which waited for: 10 -> 9; matrix products, arithmetic and copies ran while one was open for 2% -> 2% of each run, Pallas kernels for 21% -> 20%
where the time goes in v7:
time: 44.7 us; the launch traced here: 44.5 us
  starting transfers between devices  18.4 us (41%)
  Pallas kernels  13.3 us (30%)
  waiting for transfers between devices  10.9 us (24%)
  other arithmetic  0.94 us (2%)
  between operations  0.93 us (2%)
    pallas_call x10, Pallas kernels, call(): pl.pallas_call(body, out_shape=outs, in_specs=specs, out_specs=jax.tree.m...  12.7 us
    ppermute x8, starting transfers between devices, step(): return lax.ppermute(value, 'blk', pairs)  9.32 us
    ppermute x11, starting transfers between devices, flip(): return lax.ppermute(value, 'blk', [(i, i ^ bit) for i in range(size)])  9.04 us
    ppermute x8, waiting for transfers between devices, step(): return lax.ppermute(value, 'blk', pairs)  7.39 us
    ppermute x11, waiting for transfers between devices, flip(): return lax.ppermute(value, 'blk', [(i, i ^ bit) for i in range(size)])  3.48 us
    convert_element_type x1, other arithmetic, on_device(): sent = sums[-1].astype(BF16)  0.91 us
  transfers between devices with their start and end apart: 19, of which 9 were waited for; matrix products, arithmetic and copies ran while one was open for 2% of the time, Pallas kernels for 20%

profile of v7, /device:TPU:0, one launch (start us, length us, event | category | flops | bytes accessed | tf_op | source)
XLA Modules:
  0.0 44.5 jit_solution(15023153904214738454)
XLA Ops:
  0.0 2.6 %shard_map.154 = (bf16[256,512]{1,0:T(8,128)(2,1)}, bf16[256,512]{1,0:T(8,128)(2,1)}) custom-call(bf16[256,512]{1,0:T(8,128)(2,1)} %x_ref.1, f32[1,512]{1,0:T(1,128)} %bitcast.4, bf16[512,512]{1,0:T(8,128)(2,1)} %w_hbm.1), custom_call_target="tpu_custom_call" | custom-call | flops 1 | bytes 1 | tf_op jit(solution)/shard_map/pallas_call | solution.py:36
  2.6 3.1 %collective-permute-start.9 = (bf16[256,512]{1,0:T(8,128)(2,1)}, bf16[256,512]{1,0:T(8,128)(2,1)S(1)}, u32[]{:S(2)}, u32[]{:S(2)}) collective-permute-start(bf16[256,512]{1,0:T(8,128)(2,1)} %get-tuple-element.39.refs_0_), channel_id=1, source_target_pairs={{0,4},{1,5},{4,8},{5,9},{8,12},{9,13},{12,14},{13,15},{14,10},{15,... | collective-permute-start | bytes 786440 | tf_op jit(solution)/shard_map/ppermute | solution.py:261
  5.7 3.9 %shard_map.156 = (f32[144,128]{1,0:T(8,128)}, bf16[144,128]{1,0:T(8,128)(2,1)}, bf16[144,128]{1,0:T(8,128)(2,1)}, bf16[144,128]{1,0:T(8,128)(2,1)}, s32[1]{0:T(128)}) custom-call(bf16[256,512]{1,0:T(8,128)(2,1)} %get-tuple-element.31.normed_ref.normed_hbm, bf16[512,512]{1,0:T(8,128)(2,1)} %wk_hbm.1, bf16[512,512]{1,0:T(8,128)(2,1)} %wv_hbm.1, ...), custom_call_target="tpu_custom_call" | custom-call | flops 1 | bytes 1 | tf_op jit(solution)/shard_map/pallas_call | solution.py:36
  9.6 0.9 %collective-permute-start.2 = (bf16[144,128]{1,0:T(8,128)(2,1)}, bf16[144,128]{1,0:T(8,128)(2,1)S(1)}, u32[]{:S(2)}, u32[]{:S(2)}) collective-permute-start(bf16[144,128]{1,0:T(8,128)(2,1)} %get-tuple-element.37), channel_id=1, source_target_pairs={{0,3},{1,2},{2,1},{3,0},{4,7},{5,6},{6,5},{7,4},{8,11},{9,10},{10,... | collective-permute-start | bytes 110600 | tf_op jit(solution)/shard_map/ppermute | solution.py:264
  10.5 1.2 %collective-permute-start.1 = (bf16[144,128]{1,0:T(8,128)(2,1)}, bf16[144,128]{1,0:T(8,128)(2,1)S(1)}, u32[]{:S(2)}, u32[]{:S(2)}) collective-permute-start(bf16[144,128]{1,0:T(8,128)(2,1)} %get-tuple-element.36), channel_id=1, source_target_pairs={{0,1},{1,0},{2,3},{3,2},{4,5},{5,4},{6,7},{7,6},{8,9},{9,8},{10,11... | collective-permute-start | bytes 110600 | tf_op jit(solution)/shard_map/ppermute | solution.py:264
  11.8 0.3 collective-permute-done.9.refs_0_
  12.1 1.5 %collective-permute-done.10.refs_1_ = bf16[256,512]{1,0:T(8,128)(2,1)S(1)} collective-permute-done((bf16[256,512]{1,0:T(8,128)(2,1)}, bf16[256,512]{1,0:T(8,128)(2,1)S(1)}, u32[]{:S(2)}, u32[]{:S(2)}) %collective-permute-start.10) | collective-permute-done | bytes 262176 | tf_op jit(solution)/shard_map/ppermute | solution.py:261
  13.6 0.6 %shard_map.158 = (bf16[256,512]{1,0:T(8,128)(2,1)S(1)}, bf16[256,512]{1,0:T(8,128)(2,1)S(1)}) custom-call(bf16[256,512]{1,0:T(8,128)(2,1)S(1)} %collective-permute-done.9.refs_0_, bf16[256,512]{1,0:T(8,128)(2,1)S(1)} %collective-permute-done.10.refs_1_, s32[1]{0:T(128)} %get-tuple-element.40.refs_2_), custom_call_target="tpu_custom_call", output_to_operand_aliasing={{0}: (0, {}), {1}: (1, {})} | custom-call | flops 1 | bytes 1 | tf_op jit(solution)/shard_map/pallas_call | solution.py:49
  14.3 1.6 %collective-permute-start.11 = (bf16[256,512]{1,0:T(8,128)(2,1)S(1)}, bf16[256,512]{1,0:T(8,128)(2,1)S(1)}, u32[]{:S(2)}, u32[]{:S(2)}) collective-permute-start(bf16[256,512]{1,0:T(8,128)(2,1)S(1)} %get-tuple-element.41.refs_1_), channel_id=1, source_target_pairs={{0,4},{1,5},{4,8},{5,9},{8,12},{9,13},{12,14},{13,15},{14,10},{15,... | collective-permute-start | bytes 786440 | tf_op jit(solution)/shard_map/ppermute | solution.py:261
  15.9 0.4 %collective-permute-start.12 = (bf16[256,512]{1,0:T(8,128)(2,1)S(1)}, bf16[256,512]{1,0:T(8,128)(2,1)S(1)}, u32[]{:S(2)}, u32[]{:S(2)}) collective-permute-start(bf16[256,512]{1,0:T(8,128)(2,1)S(1)} %get-tuple-element.42.refs_2_), channel_id=1, source_target_pairs={{0,2},{1,3},{4,0},{5,1},{8,4},{9,5},{12,8},{13,9},{14,12},{15,13},... | collective-permute-start | bytes 786440 | tf_op jit(solution)/shard_map/ppermute | solution.py:261
  17.0 0.9 %fusion = (bf16[144,128]{1,0:T(8,128)(2,1)S(1)}, f32[144,128]{1,0:T(8,128)S(1)}) fusion(bf16[144,128]{1,0:T(8,128)(2,1)S(1)} %collective-permute-done.2, bf16[144,128]{1,0:T(8,128)(2,1)S(1)} %collective-permute-done.1, f32[144,128]{1,0:T(8,128)} %get-tuple-element.34, bf16[144,128]{1,0:T(8,128)(2,1)S(1)} %collective-permute-done), kind=kLoop, calls=%fused_computation.2 | loop fusion | flops 129024 | bytes 294912 | tf_op jit(solution)/shard_map/convert_element_type | solution.py:320
  18.0 1.3 %shard_map.157 = (bf16[16,2,128,128]{3,2,1,0:T(8,128)(2,1)S(1)}, bf16[16,2,128,128]{3,2,1,0:T(8,128)(2,1)S(1)}) custom-call(s32[1]{0:T(128)} %bitcast.1.core_ref, s32[48]{0:T(128)S(1)} %copy-done.11, s32[48]{0:T(128)S(1)} %copy-done.12, s32[1]{0:T(128)S(6)} %copy.35.count_ref, bf16[48,128,128]{2,1,0:T(8,128)(2,1)S(1)} %copy-done.2, ...), custom_call_target="tpu_custom_call" | custom-call | flops 1 | bytes 1 | tf_op jit(solution)/shard_map/pallas_call | solution.py:36
  19.3 2.2 %collective-permute-done.11.refs_0_ = bf16[256,512]{1,0:T(8,128)(2,1)S(1)} collective-permute-done((bf16[256,512]{1,0:T(8,128)(2,1)S(1)}, bf16[256,512]{1,0:T(8,128)(2,1)S(1)}, u32[]{:S(2)}, u32[]{:S(2)}) %collective-permute-start.11) | collective-permute-done | bytes 262176 | tf_op jit(solution)/shard_map/ppermute | solution.py:261
  21.5 0.9 %collective-permute-done.12.refs_1_ = bf16[256,512]{1,0:T(8,128)(2,1)S(1)} collective-permute-done((bf16[256,512]{1,0:T(8,128)(2,1)S(1)}, bf16[256,512]{1,0:T(8,128)(2,1)S(1)}, u32[]{:S(2)}, u32[]{:S(2)}) %collective-permute-start.12) | collective-permute-done | bytes 262176 | tf_op jit(solution)/shard_map/ppermute | solution.py:261
  22.5 1.6 %collective-permute-start.14 = (bf16[256,512]{1,0:T(8,128)(2,1)S(1)}, bf16[256,512]{1,0:T(8,128)(2,1)S(1)}, u32[]{:S(2)}, u32[]{:S(2)}) collective-permute-start(bf16[256,512]{1,0:T(8,128)(2,1)S(1)} %get-tuple-element.45.refs_3_), channel_id=1, source_target_pairs={{0,4},{1,5},{4,8},{5,9},{8,12},{9,13},{12,14},{13,15},{14,10},{15,... | collective-permute-start | bytes 786440 | tf_op jit(solution)/shard_map/ppermute | solution.py:261
  24.1 0.4 %collective-permute-start.15 = (bf16[256,512]{1,0:T(8,128)(2,1)S(1)}, bf16[256,512]{1,0:T(8,128)(2,1)S(1)}, u32[]{:S(2)}, u32[]{:S(2)}) collective-permute-start(bf16[256,512]{1,0:T(8,128)(2,1)S(1)} %get-tuple-element.46.refs_4_), channel_id=1, source_target_pairs={{0,2},{1,3},{4,0},{5,1},{8,4},{9,5},{12,8},{13,9},{14,12},{15,13},... | collective-permute-start | bytes 786440 | tf_op jit(solution)/shard_map/ppermute | solution.py:261
  24.5 1.6 %collective-permute-start.5 = (bf16[144,128]{1,0:T(8,128)(2,1)S(1)}, bf16[144,128]{1,0:T(8,128)(2,1)S(1)}, u32[]{:S(2)}, u32[]{:S(2)}) collective-permute-start(bf16[144,128]{1,0:T(8,128)(2,1)S(1)} %get-tuple-element.57), channel_id=1, source_target_pairs={{0,4},{1,5},{2,6},{3,7},{4,0},{5,1},{6,2},{7,3},{8,12},{9,13},{10,... | collective-permute-start | bytes 110600 | tf_op jit(solution)/shard_map/ppermute | solution.py:264
  26.1 2.2 %collective-permute-start.4 = (bf16[144,128]{1,0:T(8,128)(2,1)S(1)}, bf16[144,128]{1,0:T(8,128)(2,1)S(1)}, u32[]{:S(2)}, u32[]{:S(2)}) collective-permute-start(bf16[144,128]{1,0:T(8,128)(2,1)S(1)} %get-tuple-element.57), channel_id=1, source_target_pairs={{0,8},{1,9},{2,10},{3,11},{4,12},{5,13},{6,14},{7,15},{8,0},{9,1},... | collective-permute-start | bytes 110600 | tf_op jit(solution)/shard_map/ppermute | solution.py:264
  28.3 0.6 %collective-permute-start.3 = (bf16[144,128]{1,0:T(8,128)(2,1)S(1)}, bf16[144,128]{1,0:T(8,128)(2,1)S(1)}, u32[]{:S(2)}, u32[]{:S(2)}) collective-permute-start(bf16[144,128]{1,0:T(8,128)(2,1)S(1)} %get-tuple-element.57), channel_id=1, source_target_pairs={{0,12},{1,13},{2,14},{3,15},{4,8},{5,9},{6,10},{7,11},{8,4},{9,5},... | collective-permute-start | bytes 110600 | tf_op jit(solution)/shard_map/ppermute | solution.py:264
  28.9 0.8 %shard_map.155 = (bf16[256,1024]{1,0:T(8,128)(2,1)S(1)}, f32[256,512]{1,0:T(8,128)S(1)}) custom-call(bf16[256,512]{1,0:T(8,128)(2,1)S(1)} %copy-done.4, bf16[512,512]{1,0:T(8,128)(2,1)S(1)} %copy-done.5, bf16[512,512]{1,0:T(8,128)(2,1)S(1)} %copy-done.6, f32[64,128]{1,0:T(8,128)S(1)} %copy-done.9), custom_call_target="tpu_custom_call" | custom-call | flops 1 | bytes 1 | tf_op jit(solution)/shard_map/pallas_call | solution.py:36
  29.7 0.8 %shard_map.160 = (f32[256,512]{1,0:T(8,128)S(1)}, f32[256,512]{1,0:T(8,128)S(1)}) custom-call(bf16[16,2,128,128]{3,2,1,0:T(8,128)(2,1)S(1)} %get-tuple-element.38.refs_3_.mine_ref, bf16[16,2,128,128]{3,2,1,0:T(8,128)(2,1)S(1)} %collective-permute-done.13.sibling_ref, bf16[256,512]{1,0:T(8,128)(2,1)S(1)} %copy-done.8, ...), custom_call_target="tpu_custom_call" | custom-call | flops 1 | bytes 1 | tf_op jit(solution)/shard_map/pallas_call | solution.py:36
  30.6 0.6 %collective-permute-done.14.refs_0_ = bf16[256,512]{1,0:T(8,128)(2,1)S(1)} collective-permute-done((bf16[256,512]{1,0:T(8,128)(2,1)S(1)}, bf16[256,512]{1,0:T(8,128)(2,1)S(1)}, u32[]{:S(2)}, u32[]{:S(2)}) %collective-permute-start.14) | collective-permute-done | bytes 262176 | tf_op jit(solution)/shard_map/ppermute | solution.py:261
  31.2 1.8 %collective-permute-done.15.refs_1_ = bf16[256,512]{1,0:T(8,128)(2,1)S(1)} collective-permute-done((bf16[256,512]{1,0:T(8,128)(2,1)S(1)}, bf16[256,512]{1,0:T(8,128)(2,1)S(1)}, u32[]{:S(2)}, u32[]{:S(2)}) %collective-permute-start.15) | collective-permute-done | bytes 262176 | tf_op jit(solution)/shard_map/ppermute | solution.py:261
  33.0 1.7 %collective-permute-start.16 = (bf16[128,512]{1,0:T(8,128)(2,1)S(1)}, bf16[128,512]{1,0:T(8,128)(2,1)S(1)}, u32[]{:S(2)}, u32[]{:S(2)}) collective-permute-start(bf16[128,512]{1,0:T(8,128)(2,1)S(1)} %slice.6), channel_id=1, source_target_pairs={{0,4},{1,5},{4,8},{5,9},{8,12},{9,13},{12,14},{13,15},{14,10},{15,... | collective-permute-start | bytes 393224 | tf_op jit(solution)/shard_map/ppermute | solution.py:261
  34.8 0.4 collective-permute-start.17
  35.2 1.5 %collective-permute-done.3 = bf16[144,128]{1,0:T(8,128)(2,1)S(1)} collective-permute-done((bf16[144,128]{1,0:T(8,128)(2,1)S(1)}, bf16[144,128]{1,0:T(8,128)(2,1)S(1)}, u32[]{:S(2)}, u32[]{:S(2)}) %collective-permute-start.3) | collective-permute-done | bytes 36896 | tf_op jit(solution)/shard_map/ppermute | solution.py:264
  36.9 2.0 %collective-permute-start.8 = (bf16[144,128]{1,0:T(8,128)(2,1)S(1)}, bf16[144,128]{1,0:T(8,128)(2,1)S(1)}, u32[]{:S(2)}, u32[]{:S(2)}) collective-permute-start(bf16[144,128]{1,0:T(8,128)(2,1)S(1)} %add_convert_fusion.own_ref), channel_id=1, source_target_pairs={{0,3},{1,2},{2,1},{3,0},{4,7},{5,6},{6,5},{7,4},{8,11},{9,10},{10,... | collective-permute-start | bytes 110600 | tf_op jit(solution)/shard_map/ppermute | solution.py:264
  39.0 0.4 shard_map.162
  39.4 1.6 %collective-permute-done.6.pair_ref.refs_2_ = bf16[144,128]{1,0:T(8,128)(2,1)S(1)} collective-permute-done((bf16[144,128]{1,0:T(8,128)(2,1)S(1)}, bf16[144,128]{1,0:T(8,128)(2,1)S(1)}, u32[]{:S(2)}, u32[]{:S(2)}) %collective-permute-start.6) | collective-permute-done | bytes 36896 | tf_op jit(solution)/shard_map/ppermute | solution.py:264
  41.5 0.7 %shard_map.163.total_ref = f32[256,512]{1,0:T(8,128)S(1)} custom-call(bf16[256,512]{1,0:T(8,128)(2,1)S(1)} %copy-done.3, bf16[256,1024]{1,0:T(8,128)(2,1)S(1)} %get-tuple-element.32.refs_2_.qf_ref, f32[256,512]{1,0:T(8,128)S(1)} %get-tuple-element.33.gate_ref, bf16[144,128]{1,0:T(8,128)(2,1)S(1)} %add_convert_fusion.own_ref, ...), custom_call_target="tpu_custom_call" | custom-call | flops 1 | bytes 1 | tf_op jit(solution)/shard_map/pallas_call | solution.py:36
  42.5 0.4 collective-permute-done.18.theirs_ref
  42.9 1.6 %shard_map.167 = bf16[256,512]{1,0:T(8,128)(2,1)} custom-call(f32[256,512]{1,0:T(8,128)S(1)} %shard_map.165.mine_ref, bf16[256,512]{1,0:T(8,128)(2,1)S(1)} %collective-permute-done.18.theirs_ref, f32[1,512]{1,0:T(1,128)S(1)} %bitcast.3, bf16[512,1024]{1,0:T(8,128)(2,1)S(1)} %copy-done, bf16[1024,512]{1,0:T(8,128)(2,1)S(1)} %copy-done.1), custom_call_target="tpu_custom_call" | custom-call | flops 1 | bytes 1 | tf_op jit(solution)/shard_map/pallas_call | solution.py:36
  (50 shorter events, 1.1 us)
Async XLA Ops:
  0.0 17.9 %copy-start.11 = (s32[48]{0:T(128)S(1)}, s32[48]{0:T(128)}, u32[]{:S(2)}) copy-start(s32[48]{0:T(128)} %rows_ref.1) | copy-start | bytes 580
  0.0 18.0 %copy-start.12 = (s32[48]{0:T(128)S(1)}, s32[48]{0:T(128)}, u32[]{:S(2)}) copy-start(s32[48]{0:T(128)} %cols_ref.1) | copy-start | bytes 580
  0.0 18.0 %copy-start.2 = (bf16[48,128,128]{2,1,0:T(8,128)(2,1)S(1)}, bf16[48,128,128]{2,1,0:T(8,128)(2,1)}, u32[]{:S(2)}) copy-start(bf16[48,128,128]{2,1,0:T(8,128)(2,1)} %tiles_ref.1) | copy-start | bytes 4718596
  2.6 9.5 %collective-permute-start.9 = (bf16[256,512]{1,0:T(8,128)(2,1)}, bf16[256,512]{1,0:T(8,128)(2,1)S(1)}, u32[]{:S(2)}, u32[]{:S(2)}) collective-permute-start(bf16[256,512]{1,0:T(8,128)(2,1)} %get-tuple-element.39.refs_0_), channel_id=1, source_target_pairs={{0,4},{1,5},{4,8},{5,9},{8,12},{9,13},{12,14},{13,15},{14,10},{15,... | collective-permute-start | bytes 786440 | tf_op jit(solution)/shard_map/ppermute | solution.py:261
  5.7 8.0 %collective-permute-start.10 = (bf16[256,512]{1,0:T(8,128)(2,1)}, bf16[256,512]{1,0:T(8,128)(2,1)S(1)}, u32[]{:S(2)}, u32[]{:S(2)}) collective-permute-start(bf16[256,512]{1,0:T(8,128)(2,1)} %get-tuple-element.39.refs_0_), channel_id=1, source_target_pairs={{0,2},{1,3},{4,0},{5,1},{8,4},{9,5},{12,8},{13,9},{14,12},{15,13},... | collective-permute-start | bytes 786440 | tf_op jit(solution)/shard_map/ppermute | solution.py:261
  9.6 7.4 %collective-permute-start.2 = (bf16[144,128]{1,0:T(8,128)(2,1)}, bf16[144,128]{1,0:T(8,128)(2,1)S(1)}, u32[]{:S(2)}, u32[]{:S(2)}) collective-permute-start(bf16[144,128]{1,0:T(8,128)(2,1)} %get-tuple-element.37), channel_id=1, source_target_pairs={{0,3},{1,2},{2,1},{3,0},{4,7},{5,6},{6,5},{7,4},{8,11},{9,10},{10,... | collective-permute-start | bytes 110600 | tf_op jit(solution)/shard_map/ppermute | solution.py:264
  10.5 6.5 %collective-permute-start.1 = (bf16[144,128]{1,0:T(8,128)(2,1)}, bf16[144,128]{1,0:T(8,128)(2,1)S(1)}, u32[]{:S(2)}, u32[]{:S(2)}) collective-permute-start(bf16[144,128]{1,0:T(8,128)(2,1)} %get-tuple-element.36), channel_id=1, source_target_pairs={{0,1},{1,0},{2,3},{3,2},{4,5},{5,4},{6,7},{7,6},{8,9},{9,8},{10,11... | collective-permute-start | bytes 110600 | tf_op jit(solution)/shard_map/ppermute | solution.py:264
  11.7 5.3 %collective-permute-start = (bf16[144,128]{1,0:T(8,128)(2,1)}, bf16[144,128]{1,0:T(8,128)(2,1)S(1)}, u32[]{:S(2)}, u32[]{:S(2)}) collective-permute-start(bf16[144,128]{1,0:T(8,128)(2,1)} %get-tuple-element.35), channel_id=1, source_target_pairs={{0,2},{1,3},{2,0},{3,1},{4,6},{5,7},{6,4},{7,5},{8,10},{9,11},{10,... | collective-permute-start | bytes 110600 | tf_op jit(solution)/shard_map/ppermute | solution.py:264
  14.3 7.3 %collective-permute-start.11 = (bf16[256,512]{1,0:T(8,128)(2,1)S(1)}, bf16[256,512]{1,0:T(8,128)(2,1)S(1)}, u32[]{:S(2)}, u32[]{:S(2)}) collective-permute-start(bf16[256,512]{1,0:T(8,128)(2,1)S(1)} %get-tuple-element.41.refs_1_), channel_id=1, source_target_pairs={{0,4},{1,5},{4,8},{5,9},{8,12},{9,13},{12,14},{13,15},{14,10},{15,... | collective-permute-start | bytes 786440 | tf_op jit(solution)/shard_map/ppermute | solution.py:261
  15.9 6.6 %collective-permute-start.12 = (bf16[256,512]{1,0:T(8,128)(2,1)S(1)}, bf16[256,512]{1,0:T(8,128)(2,1)S(1)}, u32[]{:S(2)}, u32[]{:S(2)}) collective-permute-start(bf16[256,512]{1,0:T(8,128)(2,1)S(1)} %get-tuple-element.42.refs_2_), channel_id=1, source_target_pairs={{0,2},{1,3},{4,0},{5,1},{8,4},{9,5},{12,8},{13,9},{14,12},{15,13},... | collective-permute-start | bytes 786440 | tf_op jit(solution)/shard_map/ppermute | solution.py:261
  19.3 9.6 %copy-start.4 = (bf16[256,512]{1,0:T(8,128)(2,1)S(1)}, bf16[256,512]{1,0:T(8,128)(2,1)}, u32[]{:S(2)}) copy-start(bf16[256,512]{1,0:T(8,128)(2,1)} %get-tuple-element.31.normed_ref.normed_hbm) | copy-start | bytes 786436
  19.3 9.6 %copy-start.5 = (bf16[512,512]{1,0:T(8,128)(2,1)S(1)}, bf16[512,512]{1,0:T(8,128)(2,1)}, u32[]{:S(2)}) copy-start(bf16[512,512]{1,0:T(8,128)(2,1)} %wq_ref.1) | copy-start | bytes 1572868
  19.3 9.6 %copy-start.6 = (bf16[512,512]{1,0:T(8,128)(2,1)S(1)}, bf16[512,512]{1,0:T(8,128)(2,1)}, u32[]{:S(2)}) copy-start(bf16[512,512]{1,0:T(8,128)(2,1)} %wg_ref.1) | copy-start | bytes 1572868
  19.3 9.6 %copy-start.9 = (f32[64,128]{1,0:T(8,128)S(1)}, f32[64,128]{1,0:T(8,128)}, u32[]{:S(2)}) copy-start(f32[64,128]{1,0:T(8,128)} %omega_hbm.1) | copy-start | bytes 98308
  22.5 7.2 %copy-start.8 = (bf16[256,512]{1,0:T(8,128)(2,1)S(1)}, bf16[256,512]{1,0:T(8,128)(2,1)}, u32[]{:S(2)}) copy-start(bf16[256,512]{1,0:T(8,128)(2,1)} %get-tuple-element.39.refs_0_) | copy-start | bytes 786436
  22.5 5.8 %collective-permute-start.13 = (bf16[16,2,128,128]{3,2,1,0:T(8,128)(2,1)S(1)}, bf16[16,2,128,128]{3,2,1,0:T(8,128)(2,1)S(1)}, u32[]{:S(2)}, u32[]{:S(2)}) collective-permute-start(bf16[16,2,128,128]{3,2,1,0:T(8,128)(2,1)S(1)} %get-tuple-element.44), channel_id=1, source_target_pairs={{0,1},{1,0},{2,3},{3,2},{4,5},{5,4},{6,7},{7,6},{8,9},{9,8},{10,11... | collective-permute-start | bytes 3145736 | tf_op jit(solution)/shard_map/ppermute | solution.py:264
  22.5 8.7 %collective-permute-start.14 = (bf16[256,512]{1,0:T(8,128)(2,1)S(1)}, bf16[256,512]{1,0:T(8,128)(2,1)S(1)}, u32[]{:S(2)}, u32[]{:S(2)}) collective-permute-start(bf16[256,512]{1,0:T(8,128)(2,1)S(1)} %get-tuple-element.45.refs_3_), channel_id=1, source_target_pairs={{0,4},{1,5},{4,8},{5,9},{8,12},{9,13},{12,14},{13,15},{14,10},{15,... | collective-permute-start | bytes 786440 | tf_op jit(solution)/shard_map/ppermute | solution.py:261
  24.1 9.0 %collective-permute-start.15 = (bf16[256,512]{1,0:T(8,128)(2,1)S(1)}, bf16[256,512]{1,0:T(8,128)(2,1)S(1)}, u32[]{:S(2)}, u32[]{:S(2)}) collective-permute-start(bf16[256,512]{1,0:T(8,128)(2,1)S(1)} %get-tuple-element.46.refs_4_), channel_id=1, source_target_pairs={{0,2},{1,3},{4,0},{5,1},{8,4},{9,5},{12,8},{13,9},{14,12},{15,13},... | collective-permute-start | bytes 786440 | tf_op jit(solution)/shard_map/ppermute | solution.py:261
  24.5 10.7 %collective-permute-start.5 = (bf16[144,128]{1,0:T(8,128)(2,1)S(1)}, bf16[144,128]{1,0:T(8,128)(2,1)S(1)}, u32[]{:S(2)}, u32[]{:S(2)}) collective-permute-start(bf16[144,128]{1,0:T(8,128)(2,1)S(1)} %get-tuple-element.57), channel_id=1, source_target_pairs={{0,4},{1,5},{2,6},{3,7},{4,0},{5,1},{6,2},{7,3},{8,12},{9,13},{10,... | collective-permute-start | bytes 110600 | tf_op jit(solution)/shard_map/ppermute | solution.py:264
  26.1 9.1 %collective-permute-start.4 = (bf16[144,128]{1,0:T(8,128)(2,1)S(1)}, bf16[144,128]{1,0:T(8,128)(2,1)S(1)}, u32[]{:S(2)}, u32[]{:S(2)}) collective-permute-start(bf16[144,128]{1,0:T(8,128)(2,1)S(1)} %get-tuple-element.57), channel_id=1, source_target_pairs={{0,8},{1,9},{2,10},{3,11},{4,12},{5,13},{6,14},{7,15},{8,0},{9,1},... | collective-permute-start | bytes 110600 | tf_op jit(solution)/shard_map/ppermute | solution.py:264
  28.3 8.4 %collective-permute-start.3 = (bf16[144,128]{1,0:T(8,128)(2,1)S(1)}, bf16[144,128]{1,0:T(8,128)(2,1)S(1)}, u32[]{:S(2)}, u32[]{:S(2)}) collective-permute-start(bf16[144,128]{1,0:T(8,128)(2,1)S(1)} %get-tuple-element.57), channel_id=1, source_target_pairs={{0,12},{1,13},{2,14},{3,15},{4,8},{5,9},{6,10},{7,11},{8,4},{9,5},... | collective-permute-start | bytes 110600 | tf_op jit(solution)/shard_map/ppermute | solution.py:264
  30.6 8.4 %copy-start = (bf16[512,1024]{1,0:T(8,128)(2,1)S(1)}, bf16[512,1024]{1,0:T(8,128)(2,1)}, u32[]{:S(2)}) copy-start(bf16[512,1024]{1,0:T(8,128)(2,1)} %up_ref.1) | copy-start | bytes 3145732
  30.6 8.4 %copy-start.1 = (bf16[1024,512]{1,0:T(8,128)(2,1)S(1)}, bf16[1024,512]{1,0:T(8,128)(2,1)}, u32[]{:S(2)}) copy-start(bf16[1024,512]{1,0:T(8,128)(2,1)} %down_ref.1) | copy-start | bytes 3145732
  33.0 8.0 %collective-permute-start.16 = (bf16[128,512]{1,0:T(8,128)(2,1)S(1)}, bf16[128,512]{1,0:T(8,128)(2,1)S(1)}, u32[]{:S(2)}, u32[]{:S(2)}) collective-permute-start(bf16[128,512]{1,0:T(8,128)(2,1)S(1)} %slice.6), channel_id=1, source_target_pairs={{0,4},{1,5},{4,8},{5,9},{8,12},{9,13},{12,14},{13,15},{14,10},{15,... | collective-permute-start | bytes 393224 | tf_op jit(solution)/shard_map/ppermute | solution.py:261
  34.8 6.2 %collective-permute-start.17 = (bf16[128,512]{1,0:T(8,128)(2,1)S(1)}, bf16[128,512]{1,0:T(8,128)(2,1)S(1)}, u32[]{:S(2)}, u32[]{:S(2)}) collective-permute-start(bf16[128,512]{1,0:T(8,128)(2,1)S(1)} %slice.7), channel_id=1, source_target_pairs={{0,2},{1,3},{4,0},{5,1},{8,4},{9,5},{12,8},{13,9},{14,12},{15,13},... | collective-permute-start | bytes 393224 | tf_op jit(solution)/shard_map/ppermute | solution.py:261
  36.7 4.2 %collective-permute-start.6 = (bf16[144,128]{1,0:T(8,128)(2,1)S(1)}, bf16[144,128]{1,0:T(8,128)(2,1)S(1)}, u32[]{:S(2)}, u32[]{:S(2)}) collective-permute-start(bf16[144,128]{1,0:T(8,128)(2,1)S(1)} %add_convert_fusion.own_ref), channel_id=1, source_target_pairs={{0,2},{1,3},{2,0},{3,1},{4,6},{5,7},{6,4},{7,5},{8,10},{9,11},{10,... | collective-permute-start | bytes 110600 | tf_op jit(solution)/shard_map/ppermute | solution.py:264
  36.8 4.2 %collective-permute-start.7 = (bf16[144,128]{1,0:T(8,128)(2,1)S(1)}, bf16[144,128]{1,0:T(8,128)(2,1)S(1)}, u32[]{:S(2)}, u32[]{:S(2)}) collective-permute-start(bf16[144,128]{1,0:T(8,128)(2,1)S(1)} %add_convert_fusion.own_ref), channel_id=1, source_target_pairs={{0,1},{1,0},{2,3},{3,2},{4,5},{5,4},{6,7},{7,6},{8,9},{9,8},{10,11... | collective-permute-start | bytes 110600 | tf_op jit(solution)/shard_map/ppermute | solution.py:264
  36.9 4.1 %collective-permute-start.8 = (bf16[144,128]{1,0:T(8,128)(2,1)S(1)}, bf16[144,128]{1,0:T(8,128)(2,1)S(1)}, u32[]{:S(2)}, u32[]{:S(2)}) collective-permute-start(bf16[144,128]{1,0:T(8,128)(2,1)S(1)} %add_convert_fusion.own_ref), channel_id=1, source_target_pairs={{0,3},{1,2},{2,1},{3,0},{4,7},{5,6},{6,5},{7,4},{8,11},{9,10},{10,... | collective-permute-start | bytes 110600 | tf_op jit(solution)/shard_map/ppermute | solution.py:264
  39.4 2.1 %copy-start.3 = (bf16[256,512]{1,0:T(8,128)(2,1)S(1)}, bf16[256,512]{1,0:T(8,128)(2,1)}, u32[]{:S(2)}) copy-start(bf16[256,512]{1,0:T(8,128)(2,1)} %x_ref.1) | copy-start | bytes 786436
  39.4 2.1 %copy-start.7 = (bf16[512,512]{1,0:T(8,128)(2,1)S(1)}, bf16[512,512]{1,0:T(8,128)(2,1)}, u32[]{:S(2)}) copy-start(bf16[512,512]{1,0:T(8,128)(2,1)} %wo_ref.1) | copy-start | bytes 1572868
  41.3 1.6 %collective-permute-start.18 = (bf16[256,512]{1,0:T(8,128)(2,1)S(1)}, bf16[256,512]{1,0:T(8,128)(2,1)S(1)}, u32[]{:S(2)}, u32[]{:S(2)}) collective-permute-start(bf16[256,512]{1,0:T(8,128)(2,1)S(1)} %shard_map.166), channel_id=1, source_target_pairs={{0,1},{1,0},{2,3},{3,2},{4,5},{5,4},{6,7},{7,6},{8,9},{9,8},{10,11... | collective-permute-start | bytes 786440 | tf_op jit(solution)/shard_map/ppermute | solution.py:264
  41.5 1.3 %copy-start.10 = (f32[512]{0:T(512)S(1)}, f32[512]{0:T(512)}, u32[]{:S(2)}) copy-start(f32[512]{0:T(512)} %param.29) | copy-start | bytes 6148
